TPU v7x, 512 devices: a whole 4x4x16 slice. The times are simulated.
512 devices in a mesh: slab: 16 (over x, z_lo), tile: 32 (over z_hi, y, core).
Axes of the slice: x: 4, y: 4, z: 16 (z_hi: 4, z_lo: 4; z = z_hi * 4 + z_lo), core: 2. Of those that a mesh axis runs over, the one named last changes fastest.
Arguments:
- positions: float32 [32, 32, 3, 128], P('slab', 'tile'), may hold values from 0 to 32, as said below
- species: int32 [32, 32, 128], P('slab', 'tile'), may hold values from 0 to 5
- occupied: int32 [32, 32, 128], P('slab', 'tile'), may hold values 0 or 1
- embedding: bfloat16 [6, 128], replicated, may hold values from -6 to 6
- first_radial_weight: float32 [2, 8, 128], replicated, may hold values from -2 to 2
- radial_two: float32 [2, 8, 128], replicated, may hold values from -2 to 2
- mix_scalar: bfloat16 [128, 128], replicated, may hold values from -0.5 to 0.5
- vector_channel_weight: bfloat16 [128, 128], replicated, may hold values from -0.5 to 0.5
- out_weight: bfloat16 [128, 128], replicated, may hold values from -0.5 to 0.5
- read_weight: float32 [128], replicated, may hold values from -0.5 to 0.5
Outputs:
- energies: float32 [32, 32, 128], P('slab', 'tile')
- forces: float32 [32, 32, 3, 128], P('slab', 'tile')
Inputs may be any that keep to these rules, and one draw needn't show every extreme that they name: `positions`: coordinates in angstrom from the corner of the atom's own cell, which spans 5 along slab, 10 along tile and 32 along the third direction.
All inputs are finite; a program needn't handle non-finite values. No bound on the sum of `occupied` on one device may be relied on, other than what follows from the above.
Results may differ from a plain program's by a relative error of at most 0.023.
Values may be sent and summed in bfloat16 or wider, within the bound.
No kernel may reach another device: no remote copies, remote signals or barrier semaphores. Data moves between devices by JAX's collectives and lax.ppermute only.
A program may use at most 64 MiB of HBM per device.

v0:
```python
import jax
import jax.numpy as jnp
import numpy as np
from jax import lax
from jax.sharding import PartitionSpec as P

CUTOFF = 5.0
CUTOFF_SQUARE = 25.0
CELL_SLAB = 5.0
CELL_TILE = 10.0
NEIGHBOUR_DIVISOR = 4.0
STEPS_AROUND = [(slab_step, tile_step) for slab_step in (-1, 0, 1) for tile_step in (-1, 0, 1)]
OWN_CELLS = np.array([4, 7], dtype=np.int32)
SOURCE_TABLE = np.array(
    [[(own_row + 1 + pair[0]) * 3 + 1 + pair[1] for pair in STEPS_AROUND] for own_row in (0, 1)],
    dtype=np.int32,
)
SHIFT_TABLE = np.array(
    [
        [[pair[0] * CELL_SLAB, pair[1] * CELL_TILE, 0.0] for pair in STEPS_AROUND]
        for own_row in (0, 1)
    ],
    dtype=np.float32,
)
SELF_TABLE = np.array(
    [[int(pair[0] == 0 and pair[1] == 0) for pair in STEPS_AROUND] for own_row in (0, 1)],
    dtype=np.int32,
)
ROWS_FROM = {-1: (0, 1), 0: (1, 3), 1: (3, 4)}
ROWS_TO = {-1: (1, 2), 0: (0, 2), 1: (0, 1)}


def shifted(block, axis, distance):
    devices = range(lax.axis_size(axis))
    route = [((i - distance) % len(devices), i) for i in devices]
    return lax.ppermute(block, axis, route)


def extended(cells, sides, width):
    for axis, dim in sides:
        count = lax.axis_size(axis)
        head = lax.slice_in_dim(cells, 0, width, axis=dim)
        tail = lax.slice_in_dim(cells, cells.shape[dim] - width, cells.shape[dim], axis=dim)
        cells = jnp.concatenate(
            [
                lax.ppermute(tail, axis, [(i, (i + 1) % count) for i in range(count)]),
                cells,
                lax.ppermute(head, axis, [((i + 1) % count, i) for i in range(count)]),
            ],
            axis=dim,
        )
    return cells


def edge_kernels(receivers, senders, receiver_codes, sender_codes, same_block, basis_count):
    offsets = senders[:, None, :] - receivers[:, :, None]
    scaled = jnp.sum(offsets * offsets, axis=0) / CUTOFF_SQUARE
    length = receivers.shape[1]
    row_ids = lax.broadcasted_iota(jnp.int32, (length, length), 0)
    col_ids = lax.broadcasted_iota(jnp.int32, (length, length), 1)
    distinct = jnp.logical_or(jnp.logical_not(same_block), row_ids != col_ids)
    present = distinct & (receiver_codes[:, None] > -0.5) & (sender_codes[None, :] > -0.5)
    envelope = jnp.where(present, jnp.square(jnp.maximum(1.0 - scaled, 0.0)), 0.0)
    centres = (jnp.arange(basis_count, dtype=jnp.float32) + 0.5) / basis_count
    radial = (
        jnp.exp(-0.5 * jnp.square((scaled[None] - centres[:, None, None]) * basis_count))
        * envelope[None]
    )
    directed = radial[:, None] * (offsets / CUTOFF)[None]
    return jnp.concatenate([radial[:, None], directed], axis=1).astype(jnp.bfloat16)


def pair_lists(block_index):
    sources = jnp.asarray(SOURCE_TABLE)[block_index]
    shifts = jnp.asarray(SHIFT_TABLE)[block_index]
    selves = jnp.asarray(SELF_TABLE)[block_index]
    return (sources, shifts, selves)


def first_layer(
    ext_positions, ext_codes, embedding, first_radial_weight, mix_scalar, vector_channel_weight
):
    basis_count = first_radial_weight.shape[1]
    species_count = embedding.shape[0]
    length = ext_positions.shape[2]
    labels = jnp.arange(species_count, dtype=jnp.float32)
    species_hot = (jnp.abs(ext_codes[:, None, :] - labels[None, :, None]) < 0.5).astype(
        jnp.bfloat16
    )
    element_lookup = embedding.astype(jnp.float32)
    own_table = jnp.asarray(OWN_CELLS)

    def block_update(block_index):
        own_index = own_table[block_index]
        receivers = lax.dynamic_index_in_dim(ext_positions, own_index, 0, False)
        receiver_codes = lax.dynamic_index_in_dim(ext_codes, own_index, 0, False)

        def visit_pair(running_totals, listed):
            source, shift, itself = listed
            senders = lax.dynamic_index_in_dim(ext_positions, source, 0, False) + shift[:, None]
            sender_codes = lax.dynamic_index_in_dim(ext_codes, source, 0, False)
            sender_onehot = lax.dynamic_index_in_dim(species_hot, source, 0, False)
            radial_filters = edge_kernels(
                receivers, senders, receiver_codes, sender_codes, itself > 0, basis_count
            )
            tallied_entries = jnp.einsum(
                "uxfy,zy->uxfz", radial_filters, sender_onehot, preferred_element_type=jnp.float32
            )
            return (running_totals + tallied_entries, None)

        start_totals = jnp.zeros((basis_count, 4, length, species_count), jnp.float32)
        running_totals, ignored = lax.scan(
            jax.checkpoint(visit_pair), start_totals, pair_lists(block_index)
        )
        fetched_rows = jnp.einsum("gpen,nw->gpwe", running_totals, element_lookup)
        scalar_sum = (
            jnp.einsum("bc,bci->ci", first_radial_weight[0], fetched_rows[:, 0]) / NEIGHBOUR_DIVISOR
        )
        pooled_vector = (
            jnp.einsum("kt,kwtx->wtx", first_radial_weight[1], fetched_rows[:, 1:])
            / NEIGHBOUR_DIVISOR
        )
        own_hot = lax.dynamic_index_in_dim(species_hot, own_index, 0, False)
        initial = jnp.dot(embedding.T, own_hot, preferred_element_type=jnp.float32)
        invariant = (scalar_sum + jnp.sum(pooled_vector * pooled_vector, axis=0)).astype(
            jnp.bfloat16
        )
        hidden = lax.dot_general(
            mix_scalar, invariant, (((0,), (0,)), ((), ())), preferred_element_type=jnp.float32
        )
        incoming_vector = pooled_vector.astype(jnp.bfloat16)
        new_vector = jnp.einsum(
            "qw,nqp->nwp",
            vector_channel_weight,
            incoming_vector,
            preferred_element_type=jnp.float32,
        )
        return (initial + jax.nn.silu(hidden), new_vector)

    return lax.map(block_update, jnp.arange(2, dtype=jnp.int32))


def second_layer(ext_positions, ext_codes, ext_features, radial_two, out_weight, read_weight):
    basis_count = radial_two.shape[1]
    width = out_weight.shape[0]
    length = ext_positions.shape[2]
    own_table = jnp.asarray(OWN_CELLS)

    def block_energy(block_index):
        own_index = own_table[block_index]
        receivers = lax.dynamic_index_in_dim(ext_positions, own_index, 0, False)
        receiver_codes = lax.dynamic_index_in_dim(ext_codes, own_index, 0, False)

        def visit_pair(running_totals, listed):
            source, shift, itself = listed
            senders = lax.dynamic_index_in_dim(ext_positions, source, 0, False) + shift[:, None]
            sender_codes = lax.dynamic_index_in_dim(ext_codes, source, 0, False)
            sender_features = lax.dynamic_index_in_dim(ext_features, source, 0, False).astype(
                jnp.bfloat16
            )
            scalars = sender_features[:width]
            vectors = sender_features[width:].reshape((3, width, length))
            radial_filters = edge_kernels(
                receivers, senders, receiver_codes, sender_codes, itself > 0, basis_count
            )
            first_term = jnp.einsum(
                "bij,cj->bci", radial_filters[:, 0], scalars, preferred_element_type=jnp.float32
            )
            second_term = jnp.einsum(
                "bdij,dcj->bci", radial_filters[:, 1:], vectors, preferred_element_type=jnp.float32
            )
            return ((running_totals[0] + first_term, running_totals[1] + second_term), None)

        empty_sum = jnp.zeros((basis_count, width, length), jnp.float32)
        sums, ignored = lax.scan(
            jax.checkpoint(visit_pair), (empty_sum, empty_sum), pair_lists(block_index)
        )
        message = (
            jnp.einsum("bc,bci->ci", radial_two[0], sums[0])
            + jnp.einsum("bc,bci->ci", radial_two[1], sums[1])
        ) / NEIGHBOUR_DIVISOR
        own_scalar = lax.dynamic_index_in_dim(ext_features, own_index, 0, False)[:width]
        combined = (own_scalar + message).astype(jnp.bfloat16)
        hidden = lax.dot_general(
            out_weight, combined, (((0,), (0,)), ((), ())), preferred_element_type=jnp.float32
        )
        present = (receiver_codes > -0.5).astype(jnp.float32)
        return present * jnp.sum(read_weight[:, None] * jax.nn.silu(hidden), axis=0)

    return lax.map(block_energy, jnp.arange(2, dtype=jnp.int32))


def send_home(ext_grid):
    summed = ext_grid[1:3, 1]
    for pair in STEPS_AROUND:
        slab_step, tile_step = pair
        if not (slab_step == 0 and tile_step == 0):
            rows_from = ROWS_FROM[slab_step]
            rows_to = ROWS_TO[slab_step]
            portion = ext_grid[rows_from[0] : rows_from[1], 1 + tile_step]
            if tile_step != 0:
                portion = shifted(portion, "tile", tile_step)
            if slab_step != 0:
                portion = shifted(portion, "slab", slab_step)
            summed = summed.at[rows_to[0] : rows_to[1]].add(portion)
    return summed


def on_device(
    positions,
    species,
    occupied,
    embedding,
    first_radial_weight,
    radial_two,
    mix_scalar,
    vector_channel_weight,
    out_weight,
    read_weight,
):
    length = positions.shape[3]
    width = embedding.shape[1]
    local_codes = jnp.where(occupied > 0, species, -1).astype(jnp.float32)
    packet = jnp.concatenate([positions, local_codes[:, :, None]], axis=2)
    arrived = extended(packet, (("slab", 0), ("tile", 1)), 1).reshape((12, 4, length))
    ext_positions = arrived[:, :3]
    ext_codes = arrived[:, 3]
    first_out, first_pull = jax.vjp(
        lambda moved_atoms: first_layer(
            moved_atoms,
            ext_codes,
            embedding,
            first_radial_weight,
            mix_scalar,
            vector_channel_weight,
        ),
        ext_positions,
    )
    new_scalar, new_vector = first_out
    features = jnp.concatenate([new_scalar[:, None], new_vector], axis=1).astype(jnp.bfloat16)
    features = features.reshape((2, 1, 4 * width, length))
    ext_features = extended(features, (("slab", 0), ("tile", 1)), 1)
    ext_features = ext_features.reshape((12, 4 * width, length)).astype(jnp.float32)
    energies, second_pull = jax.vjp(
        lambda moved_atoms, carried: second_layer(
            moved_atoms, ext_codes, carried, radial_two, out_weight, read_weight
        ),
        ext_positions,
        ext_features,
    )
    position_grad, feature_grad = second_pull(jnp.ones_like(energies))
    feature_total = send_home(feature_grad.reshape((4, 3, 4 * width, length)))
    feature_total = lax.optimization_barrier(feature_total.astype(jnp.bfloat16)).astype(jnp.float32)
    scalar_grad = feature_total[:, :width]
    vector_grad = feature_total[:, width:].reshape((2, 3, width, length))
    position_grad = position_grad + first_pull((scalar_grad, vector_grad))[0]
    forces = -send_home(position_grad.reshape((4, 3, 3, length)))
    return (energies[:, None], forces[:, None])


def solution(mesh):
    in_specs = (
        P("slab", "tile", None, None),
        P("slab", "tile", None),
        P("slab", "tile", None),
        P(),
        P(),
        P(),
        P(),
        P(),
        P(),
        P(),
    )
    out_specs = (P("slab", "tile", None), P("slab", "tile", None, None))
    return jax.shard_map(
        on_device, mesh=mesh, in_specs=in_specs, out_specs=out_specs, check_vma=False
    )
```

profile of v0, /device:TPU:24, one launch (start us, length us, event | category | flops | bytes accessed | tf_op | source)
XLA Modules:
  0.0 799.4 jit_solution(10249257784798864476)
XLA Ops:
  2.0 3.8 collective-permute-start
  5.9 6.8 collective-permute-start.1
  16.6 3.6 collective-permute-start.3
  20.3 5.8 collective-permute-done.3
  27.0 112.5 %while.274 = (s32[]{:T(128)}, bf16[2,128,128]{2,1,0:T(8,128)(2,1)S(1)}, bf16[2,3,128,128]{3,2,1,0:T(8,128)(2,1)S(1)}, s32[2]{0:T(128)S(1)}, f32[2,3,128]{2,1,0:T...) while((s32[]{:T(128)}, ...), condition=%wide.region_5.6_spmd.clone.clone.clone, body=%wide.region_0.5_spmd.sunk.clone.clone.clone.sunk | while | flops 34177696 | bytes 11217610 | solution.py:140
  34.3 46.4 %while.281 = (s32[]{:T(128)}, f32[8,4,128,6]{2,3,1,0:T(8,128)S(1)}, s32[9]{0:T(128)S(1)}, f32[12,3,128]{2,1,0:T(4,128)S(1)}, f32[9,3]{1,0:T(8,128)S(1)}, /*index...) while((s32[]{:T(128)}, f32[8,4,128,6]{2,3,1,0:T(8,128)S(1)}, ...), condition=%wide.region_3.3_spmd.clone.clone, body=%wide.region_1.2_spmd.clone.clone.sunk | while | flops 9404936 | bytes 4318425 | solution.py:112
  90.5 46.4 %while.281 = (s32[]{:T(128)}, f32[8,4,128,6]{2,3,1,0:T(8,128)S(1)}, s32[9]{0:T(128)S(1)}, f32[12,3,128]{2,1,0:T(4,128)S(1)}, f32[9,3]{1,0:T(8,128)S(1)}, /*index...) while((s32[]{:T(128)}, f32[8,4,128,6]{2,3,1,0:T(8,128)S(1)}, ...), condition=%wide.region_3.3_spmd.clone.clone, body=%wide.region_1.2_spmd.clone.clone.sunk | while | flops 9404936 | bytes 4318425 | solution.py:112
  141.5 8.1 %collective-permute-start.5 = (bf16[1,1,512,128]{3,2,0,1:T(8,128)(2,1)S(1)}, bf16[1,1,512,128]{3,2,0,1:T(8,128)(2,1)S(1)}, u32[]{:S(2)}, u32[]{:S(2)}) collective-permute-start(bf16[1,1,512,128]{3,2,0,1:T(8,128)(2,1)S(1)} %bitcast.799), channel_id=1, source_target_pairs={{32,0},{64,32},{96,64},{128,96},{160,128},{192,160},{224,192},{256... | collective-permute-start | bytes 393224 | tf_op jit(solution)/shard_map/ppermute | solution.py:48
  153.3 8.5 %collective-permute-start.6 = (bf16[4,1,512,128]{3,2,0,1:T(8,128)(2,1)S(1)}, bf16[4,1,512,128]{3,2,0,1:T(8,128)(2,1)S(1)}, u32[]{:S(2)}, u32[]{:S(2)}) collective-permute-start(bf16[4,1,512,128]{3,2,0,1:T(8,128)(2,1)S(1)} %pad_maximum_fusion), channel_id=1, source_target_pairs={{0,1},{1,2},{2,3},{3,4},{4,5},{5,6},{6,7},{7,8},{8,9},{9,10},{10,1... | collective-permute-start | bytes 1572872 | tf_op jit(solution)/shard_map/ppermute | solution.py:46
  163.9 6.5 collective-permute-done.7
  176.2 128.0 %while.276 = (s32[]{:T(128)}, f32[2,128]{1,0:T(2,128)S(1)}, s32[2]{0:T(128)S(1)}, f32[2,3,128]{2,1,0:T(4,128)S(1)}, f32[2,128]{1,0:T(2,128)S(1)}, /*index=5*/s32...) while((s32[]{:T(128)}, f32[2,128]{1,0:T(2,128)S(1)}, ...), condition=%wide.region_11.12_spmd.clone.clone.clone, body=%wide.region_6.11_spmd.sunk.clone.clone.clone.sunk | while | flops 143049744 | bytes 11183071 | solution.py:190
  184.8 52.8 %while.282 = (s32[]{:T(128)}, f32[8,128,128]{2,1,0:T(8,128)S(1)}, f32[8,128,128]{2,1,0:T(8,128)S(1)}, s32[9]{0:T(128)S(1)}, bf16[12,512,128]{2,1,0:T(8,128)(2,1)...) while((s32[]{:T(128)}, f32[8,128,128]{2,1,0:T(8,128)S(1)}, ...), condition=%wide.region_9.9_spmd.clone.clone, body=%wide.region_7.8_spmd.clone.clone.sunk | while | flops 137282048 | bytes 4677314 | solution.py:175
  248.8 52.8 %while.282 = (s32[]{:T(128)}, f32[8,128,128]{2,1,0:T(8,128)S(1)}, f32[8,128,128]{2,1,0:T(8,128)S(1)}, s32[9]{0:T(128)S(1)}, bf16[12,512,128]{2,1,0:T(8,128)(2,1)...) while((s32[]{:T(128)}, f32[8,128,128]{2,1,0:T(8,128)S(1)}, ...), condition=%wide.region_9.9_spmd.clone.clone, body=%wide.region_7.8_spmd.clone.clone.sunk | while | flops 137282048 | bytes 4677314 | solution.py:175
  304.8 195.5 %while.278 = (s32[]{:T(128)}, f32[12,3,128]{2,1,0:T(4,128)S(1)}, f32[12,512,128]{1,2,0:T(8,128)}, f32[128,1]{0,1:T(1,128)S(1)}, f32[2,128]{1,0:T(2,128)S(1)}, /*...) while((s32[]{:T(128)}, f32[12,3,128]{2,1,0:T(4,128)S(1)}, ...), condition=%wide.region_22.23_spmd.clone, body=%wide.region_12.22_spmd.clone.sunk | while | flops 283023616 | bytes 49305320 | solution.py:190
  307.7 88.7 %while.283 = (s32[]{:T(128)}, f32[12,3,128]{2,1,0:T(4,128)S(1)}, f32[12,512,128]{1,2,0:T(8,128)}, f32[3,128]{1,0:T(4,128)S(1)}, bf16[8,128,128]{2,1,0:T(8,128)(2...) while((s32[]{:T(128)}, f32[12,3,128]{2,1,0:T(4,128)S(1)}, ...), condition=%wide.region_21.21_spmd.clone, body=%wide.region_13.20_spmd.clone.sunk | while | flops 276530560 | bytes 16081602 | solution.py:175
  404.9 88.7 %while.283 = (s32[]{:T(128)}, f32[12,3,128]{2,1,0:T(4,128)S(1)}, f32[12,512,128]{1,2,0:T(8,128)}, f32[3,128]{1,0:T(4,128)S(1)}, bf16[8,128,128]{2,1,0:T(8,128)(2...) while((s32[]{:T(128)}, f32[12,3,128]{2,1,0:T(4,128)S(1)}, ...), condition=%wide.region_21.21_spmd.clone, body=%wide.region_13.20_spmd.clone.sunk | while | flops 276530560 | bytes 16081602 | solution.py:175
  506.4 3.8 collective-permute-start.8
  510.2 8.0 collective-permute-start.10
  518.2 25.5 %collective-permute-start.11 = (f32[1,512,128]{2,1,0:T(8,128)}, f32[1,512,128]{2,1,0:T(8,128)}, u32[]{:S(2)}, u32[]{:S(2)}) collective-permute-start(f32[1,512,128]{2,1,0:T(8,128)} %get-tuple-element.4222), channel_id=1, source_target_pairs={{31,0},{0,1},{1,2},{2,3},{3,4},{4,5},{5,6},{6,7},{7,8},{8,9},{9,10... | collective-permute-start | bytes 786440 | tf_op jit(solution)/shard_map/ppermute | solution.py:36
  551.8 17.9 %collective-permute-start.14 = (f32[2,512,128]{2,1,0:T(8,128)S(1)}, f32[2,512,128]{2,1,0:T(8,128)S(1)}, u32[]{:S(2)}, u32[]{:S(2)}) collective-permute-start(f32[2,512,128]{2,1,0:T(8,128)S(1)} %bitcast.782), channel_id=1, source_target_pairs={{31,0},{0,1},{1,2},{2,3},{3,4},{4,5},{5,6},{6,7},{7,8},{8,9},{9,10... | collective-permute-start | bytes 1572872 | tf_op jit(solution)/shard_map/ppermute | solution.py:36
  571.6 9.7 %collective-permute-start.18 = (f32[1,512,128]{2,1,0:T(8,128)}, f32[1,512,128]{2,1,0:T(8,128)S(1)}, u32[]{:S(2)}, u32[]{:S(2)}) collective-permute-start(f32[1,512,128]{2,1,0:T(8,128)} %get-tuple-element.4219), channel_id=1, source_target_pairs={{31,0},{0,1},{1,2},{2,3},{3,4},{4,5},{5,6},{6,7},{7,8},{8,9},{9,10... | collective-permute-start | bytes 786440 | tf_op jit(solution)/shard_map/ppermute | solution.py:36
  591.2 3.8 collective-permute-done.12
  598.4 11.2 %collective-permute-done.16 = f32[1,512,128]{2,1,0:T(8,128)S(1)} collective-permute-done((f32[1,512,128]{2,1,0:T(8,128)S(1)}, f32[1,512,128]{2,1,0:T(8,128)S(1)}, u32[]{:S(2)}, u32[]{:S(2)}) %collective-permute-start.16) | collective-permute-done | bytes 262176 | tf_op jit(solution)/shard_map/ppermute | solution.py:36
  609.8 5.4 collective-permute-done.19
  615.5 120.7 %while.280 = (s32[]{:T(128)}, f32[12,3,128]{2,1,0:T(4,128)S(1)}, bf16[2,3,128,128]{3,2,1,0:T(8,128)(2,1)S(1)}, bf16[128,128]{1,0:T(8,128)(2,1)S(1)}, f32[2,3,128...) while((s32[]{:T(128)}, f32[12,3,128]{2,1,0:T(4,128)S(1)}, ...), condition=%wide.region_33.34_spmd.clone.clone, body=%wide.region_23.33_spmd.clone.clone.sunk | while | flops 36153628 | bytes 15498379 | solution.py:140
  619.2 55.4 %while.284 = (s32[]{:T(128)}, f32[12,3,128]{2,1,0:T(4,128)S(1)}, f32[3,128]{1,0:T(4,128)S(1)}, bf16[8,4,128,6]{2,3,1,0:T(8,128)(2,1)S(1)}, s32[9]{0:T(128)S(1)},...) while((s32[]{:T(128)}, f32[12,3,128]{2,1,0:T(4,128)S(1)}, ...), condition=%wide.region_32.32_spmd.clone, body=%wide.region_24.31_spmd.clone.sunk | while | flops 11634073 | bytes 8153738 | solution.py:112
  679.5 55.4 %while.284 = (s32[]{:T(128)}, f32[12,3,128]{2,1,0:T(4,128)S(1)}, f32[3,128]{1,0:T(4,128)S(1)}, bf16[8,4,128,6]{2,3,1,0:T(8,128)(2,1)S(1)}, s32[9]{0:T(128)S(1)},...) while((s32[]{:T(128)}, f32[12,3,128]{2,1,0:T(4,128)S(1)}, ...), condition=%wide.region_32.32_spmd.clone, body=%wide.region_24.31_spmd.clone.sunk | while | flops 11634073 | bytes 8153738 | solution.py:112
  738.2 13.3 %collective-permute-start.23 = (f32[1,3,128]{2,0,1:T(1,128)S(1)}, f32[1,3,128]{2,0,1:T(1,128)S(1)}, u32[]{:S(2)}, u32[]{:S(2)}) collective-permute-start(f32[1,3,128]{2,0,1:T(1,128)S(1)} %bitcast.815), channel_id=1, source_target_pairs={{31,0},{0,1},{1,2},{2,3},{3,4},{4,5},{5,6},{6,7},{7,8},{8,9},{9,10... | collective-permute-start | bytes 4616 | tf_op jit(solution)/shard_map/ppermute | solution.py:36
  757.1 9.4 %collective-permute-start.30 = (f32[1,3,128]{2,0,1:T(1,128)S(1)}, f32[1,3,128]{2,0,1:T(1,128)S(1)}, u32[]{:S(2)}, u32[]{:S(2)}) collective-permute-start(f32[1,3,128]{2,0,1:T(1,128)S(1)} %bitcast.812), channel_id=1, source_target_pairs={{31,0},{0,1},{1,2},{2,3},{3,4},{4,5},{5,6},{6,7},{7,8},{8,9},{9,10... | collective-permute-start | bytes 4616 | tf_op jit(solution)/shard_map/ppermute | solution.py:36
  772.7 9.3 %collective-permute-start.26 = (f32[2,3,128]{2,0,1:T(2,128)S(1)}, f32[2,3,128]{2,0,1:T(2,128)S(1)}, u32[]{:S(2)}, u32[]{:S(2)}) collective-permute-start(f32[2,3,128]{2,0,1:T(2,128)S(1)} %bitcast.809), channel_id=1, source_target_pairs={{31,0},{0,1},{1,2},{2,3},{3,4},{4,5},{5,6},{6,7},{7,8},{8,9},{9,10... | collective-permute-start | bytes 9224 | tf_op jit(solution)/shard_map/ppermute | solution.py:36
  782.0 3.6 collective-permute-start.29
  795.1 3.7 collective-permute-done.31
  (1618 shorter events, 426.4 us)
Async XLA Ops:
  2.0 11.4 %collective-permute-start = (f32[1,1,4,128]{3,1,2,0:T(1,128)S(1)}, f32[1,1,4,128]{3,1,2,0:T(1,128)S(1)}, u32[]{:S(2)}, u32[]{:S(2)}) collective-permute-start(f32[1,1,4,128]{3,1,2,0:T(1,128)S(1)} %get-tuple-element.4244), channel_id=1, source_target_pairs={{0,32},{32,64},{64,96},{96,128},{128,160},{160,192},{192,224},{224... | collective-permute-start | bytes 6152 | tf_op jit(solution)/shard_map/ppermute | solution.py:46
  5.9 8.1 %collective-permute-start.1 = (f32[1,1,4,128]{3,1,2,0:T(1,128)S(1)}, f32[1,1,4,128]{3,1,2,0:T(1,128)S(1)}, u32[]{:S(2)}, u32[]{:S(2)}) collective-permute-start(f32[1,1,4,128]{3,1,2,0:T(1,128)S(1)} %get-tuple-element.4245), channel_id=1, source_target_pairs={{32,0},{64,32},{96,64},{128,96},{160,128},{192,160},{224,192},{256... | collective-permute-start | bytes 6152 | tf_op jit(solution)/shard_map/ppermute | solution.py:48
  14.7 5.6 collective-permute-start.2
  16.6 9.5 %collective-permute-start.3 = (f32[4,1,4,128]{3,1,2,0:T(1,128)S(1)}, f32[4,1,4,128]{3,1,2,0:T(1,128)S(1)}, u32[]{:S(2)}, u32[]{:S(2)}) collective-permute-start(f32[4,1,4,128]{3,1,2,0:T(1,128)S(1)} %pad_maximum_fusion.2), channel_id=1, source_target_pairs={{1,0},{2,1},{3,2},{4,3},{5,4},{6,5},{7,6},{8,7},{9,8},{10,9},{11,1... | collective-permute-start | bytes 24584 | tf_op jit(solution)/shard_map/ppermute | solution.py:48
  139.6 11.1 %collective-permute-start.4 = (bf16[1,1,512,128]{3,2,1,0:T(8,128)(2,1)S(1)}, bf16[1,1,512,128]{3,2,1,0:T(8,128)(2,1)S(1)}, u32[]{:S(2)}, u32[]{:S(2)}) collective-permute-start(bf16[1,1,512,128]{3,2,1,0:T(8,128)(2,1)S(1)} %bitcast.800), channel_id=1, source_target_pairs={{0,32},{32,64},{64,96},{96,128},{128,160},{160,192},{192,224},{224... | collective-permute-start | bytes 393224 | tf_op jit(solution)/shard_map/ppermute | solution.py:46
  141.5 11.6 %collective-permute-start.5 = (bf16[1,1,512,128]{3,2,0,1:T(8,128)(2,1)S(1)}, bf16[1,1,512,128]{3,2,0,1:T(8,128)(2,1)S(1)}, u32[]{:S(2)}, u32[]{:S(2)}) collective-permute-start(bf16[1,1,512,128]{3,2,0,1:T(8,128)(2,1)S(1)} %bitcast.799), channel_id=1, source_target_pairs={{32,0},{64,32},{96,64},{128,96},{160,128},{192,160},{224,192},{256... | collective-permute-start | bytes 393224 | tf_op jit(solution)/shard_map/ppermute | solution.py:48
  153.3 10.6 %collective-permute-start.6 = (bf16[4,1,512,128]{3,2,0,1:T(8,128)(2,1)S(1)}, bf16[4,1,512,128]{3,2,0,1:T(8,128)(2,1)S(1)}, u32[]{:S(2)}, u32[]{:S(2)}) collective-permute-start(bf16[4,1,512,128]{3,2,0,1:T(8,128)(2,1)S(1)} %pad_maximum_fusion), channel_id=1, source_target_pairs={{0,1},{1,2},{2,3},{3,4},{4,5},{5,6},{6,7},{7,8},{8,9},{9,10},{10,1... | collective-permute-start | bytes 1572872 | tf_op jit(solution)/shard_map/ppermute | solution.py:46
  161.7 8.6 %collective-permute-start.7 = (bf16[4,1,512,128]{3,2,0,1:T(8,128)(2,1)S(1)}, bf16[4,1,512,128]{3,2,0,1:T(8,128)(2,1)S(1)}, u32[]{:S(2)}, u32[]{:S(2)}) collective-permute-start(bf16[4,1,512,128]{3,2,0,1:T(8,128)(2,1)S(1)} %pad_maximum_fusion), channel_id=1, source_target_pairs={{1,0},{2,1},{3,2},{4,3},{5,4},{6,5},{7,6},{8,7},{9,8},{10,9},{11,1... | collective-permute-start | bytes 1572872 | tf_op jit(solution)/shard_map/ppermute | solution.py:48
  506.4 37.3 %collective-permute-start.8 = (f32[1,512,128]{2,1,0:T(8,128)S(1)}, f32[1,512,128]{2,1,0:T(8,128)}, u32[]{:S(2)}, u32[]{:S(2)}) collective-permute-start(f32[1,512,128]{2,1,0:T(8,128)S(1)} %get-tuple-element.4224), channel_id=1, source_target_pairs={{1,0},{2,1},{3,2},{4,3},{5,4},{6,5},{7,6},{8,7},{9,8},{10,9},{11,1... | collective-permute-start | bytes 786440 | tf_op jit(solution)/shard_map/ppermute | solution.py:36
  510.2 59.5 %collective-permute-start.10 = (f32[1,512,128]{2,1,0:T(8,128)}, f32[1,512,128]{2,1,0:T(8,128)}, u32[]{:S(2)}, u32[]{:S(2)}) collective-permute-start(f32[1,512,128]{2,1,0:T(8,128)} %get-tuple-element.4223), channel_id=1, source_target_pairs={{32,0},{64,32},{96,64},{128,96},{160,128},{192,160},{224,192},{256... | collective-permute-start | bytes 786440 | tf_op jit(solution)/shard_map/ppermute | solution.py:36
  518.2 53.4 %collective-permute-start.11 = (f32[1,512,128]{2,1,0:T(8,128)}, f32[1,512,128]{2,1,0:T(8,128)}, u32[]{:S(2)}, u32[]{:S(2)}) collective-permute-start(f32[1,512,128]{2,1,0:T(8,128)} %get-tuple-element.4222), channel_id=1, source_target_pairs={{31,0},{0,1},{1,2},{2,3},{3,4},{4,5},{5,6},{6,7},{7,8},{8,9},{9,10... | collective-permute-start | bytes 786440 | tf_op jit(solution)/shard_map/ppermute | solution.py:36
  543.7 37.6 %collective-permute-start.9 = (f32[1,512,128]{2,1,0:T(8,128)}, f32[1,512,128]{2,1,0:T(8,128)S(1)}, u32[]{:S(2)}, u32[]{:S(2)}) collective-permute-start(f32[1,512,128]{2,1,0:T(8,128)} %collective-permute-done.8), channel_id=1, source_target_pairs={{32,0},{64,32},{96,64},{128,96},{160,128},{192,160},{224,192},{256... | collective-permute-start | bytes 786440 | tf_op jit(solution)/shard_map/ppermute | solution.py:36
  549.6 48.6 %collective-permute-start.13 = (f32[2,512,128]{2,1,0:T(8,128)S(1)}, f32[2,512,128]{2,1,0:T(8,128)S(1)}, u32[]{:S(2)}, u32[]{:S(2)}) collective-permute-start(f32[2,512,128]{2,1,0:T(8,128)S(1)} %bitcast.781), channel_id=1, source_target_pairs={{1,0},{2,1},{3,2},{4,3},{5,4},{6,5},{7,6},{8,7},{9,8},{10,9},{11,1... | collective-permute-start | bytes 1572872 | tf_op jit(solution)/shard_map/ppermute | solution.py:36
  551.8 46.5 %collective-permute-start.14 = (f32[2,512,128]{2,1,0:T(8,128)S(1)}, f32[2,512,128]{2,1,0:T(8,128)S(1)}, u32[]{:S(2)}, u32[]{:S(2)}) collective-permute-start(f32[2,512,128]{2,1,0:T(8,128)S(1)} %bitcast.782), channel_id=1, source_target_pairs={{31,0},{0,1},{1,2},{2,3},{3,4},{4,5},{5,6},{6,7},{7,8},{8,9},{9,10... | collective-permute-start | bytes 1572872 | tf_op jit(solution)/shard_map/ppermute | solution.py:36
  569.7 15.9 %collective-permute-start.15 = (f32[1,512,128]{2,1,0:T(8,128)}, f32[1,512,128]{2,1,0:T(8,128)S(1)}, u32[]{:S(2)}, u32[]{:S(2)}) collective-permute-start(f32[1,512,128]{2,1,0:T(8,128)} %get-tuple-element.4220), channel_id=1, source_target_pairs={{1,0},{2,1},{3,2},{4,3},{5,4},{6,5},{7,6},{8,7},{9,8},{10,9},{11,1... | collective-permute-start | bytes 786440 | tf_op jit(solution)/shard_map/ppermute | solution.py:36
  571.6 17.6 %collective-permute-start.18 = (f32[1,512,128]{2,1,0:T(8,128)}, f32[1,512,128]{2,1,0:T(8,128)S(1)}, u32[]{:S(2)}, u32[]{:S(2)}) collective-permute-start(f32[1,512,128]{2,1,0:T(8,128)} %get-tuple-element.4219), channel_id=1, source_target_pairs={{31,0},{0,1},{1,2},{2,3},{3,4},{4,5},{5,6},{6,7},{7,8},{8,9},{9,10... | collective-permute-start | bytes 786440 | tf_op jit(solution)/shard_map/ppermute | solution.py:36
  581.3 13.7 %collective-permute-start.12 = (f32[1,512,128]{2,1,0:T(8,128)}, f32[1,512,128]{2,1,0:T(8,128)S(1)}, u32[]{:S(2)}, u32[]{:S(2)}) collective-permute-start(f32[1,512,128]{2,1,0:T(8,128)} %collective-permute-done.11), channel_id=1, source_target_pairs={{32,0},{64,32},{96,64},{128,96},{160,128},{192,160},{224,192},{256... | collective-permute-start | bytes 786440 | tf_op jit(solution)/shard_map/ppermute | solution.py:36
  585.6 24.2 %collective-permute-start.17 = (f32[1,512,128]{2,1,0:T(8,128)}, f32[1,512,128]{2,1,0:T(8,128)S(1)}, u32[]{:S(2)}, u32[]{:S(2)}) collective-permute-start(f32[1,512,128]{2,1,0:T(8,128)} %get-tuple-element.4221), channel_id=1, source_target_pairs={{480,0},{0,32},{32,64},{64,96},{96,128},{128,160},{160,192},{192,2... | collective-permute-start | bytes 786440 | tf_op jit(solution)/shard_map/ppermute | solution.py:36
  589.3 20.3 %collective-permute-start.16 = (f32[1,512,128]{2,1,0:T(8,128)S(1)}, f32[1,512,128]{2,1,0:T(8,128)S(1)}, u32[]{:S(2)}, u32[]{:S(2)}) collective-permute-start(f32[1,512,128]{2,1,0:T(8,128)S(1)} %collective-permute-done.15), channel_id=1, source_target_pairs={{480,0},{0,32},{32,64},{64,96},{96,128},{128,160},{160,192},{192,2... | collective-permute-start | bytes 786440 | tf_op jit(solution)/shard_map/ppermute | solution.py:36
  595.0 20.2 %collective-permute-start.19 = (f32[1,512,128]{2,1,0:T(8,128)S(1)}, f32[1,512,128]{2,1,0:T(8,128)S(1)}, u32[]{:S(2)}, u32[]{:S(2)}) collective-permute-start(f32[1,512,128]{2,1,0:T(8,128)S(1)} %collective-permute-done.18), channel_id=1, source_target_pairs={{480,0},{0,32},{32,64},{64,96},{96,128},{128,160},{160,192},{192,2... | collective-permute-start | bytes 786440 | tf_op jit(solution)/shard_map/ppermute | solution.py:36
  736.2 30.2 %collective-permute-start.20 = (f32[1,3,128]{2,0,1:T(1,128)S(1)}, f32[1,3,128]{2,0,1:T(1,128)S(1)}, u32[]{:S(2)}, u32[]{:S(2)}) collective-permute-start(f32[1,3,128]{2,0,1:T(1,128)S(1)} %bitcast.816), channel_id=1, source_target_pairs={{1,0},{2,1},{3,2},{4,3},{5,4},{6,5},{7,6},{8,7},{9,8},{10,9},{11,1... | collective-permute-start | bytes 4616 | tf_op jit(solution)/shard_map/ppermute | solution.py:36
  738.2 30.5 %collective-permute-start.23 = (f32[1,3,128]{2,0,1:T(1,128)S(1)}, f32[1,3,128]{2,0,1:T(1,128)S(1)}, u32[]{:S(2)}, u32[]{:S(2)}) collective-permute-start(f32[1,3,128]{2,0,1:T(1,128)S(1)} %bitcast.815), channel_id=1, source_target_pairs={{31,0},{0,1},{1,2},{2,3},{3,4},{4,5},{5,6},{6,7},{7,8},{8,9},{9,10... | collective-permute-start | bytes 4616 | tf_op jit(solution)/shard_map/ppermute | solution.py:36
  751.5 19.3 %collective-permute-start.22 = (f32[1,3,128]{2,0,1:T(1,128)S(1)}, f32[1,3,128]{2,0,1:T(1,128)S(1)}, u32[]{:S(2)}, u32[]{:S(2)}) collective-permute-start(f32[1,3,128]{2,0,1:T(1,128)S(1)} %bitcast.814), channel_id=1, source_target_pairs={{32,0},{64,32},{96,64},{128,96},{160,128},{192,160},{224,192},{256... | collective-permute-start | bytes 4616 | tf_op jit(solution)/shard_map/ppermute | solution.py:36
  755.1 17.6 %collective-permute-start.27 = (f32[1,3,128]{2,0,1:T(1,128)S(1)}, f32[1,3,128]{2,0,1:T(1,128)S(1)}, u32[]{:S(2)}, u32[]{:S(2)}) collective-permute-start(f32[1,3,128]{2,0,1:T(1,128)S(1)} %bitcast.813), channel_id=1, source_target_pairs={{1,0},{2,1},{3,2},{4,3},{5,4},{6,5},{7,6},{8,7},{9,8},{10,9},{11,1... | collective-permute-start | bytes 4616 | tf_op jit(solution)/shard_map/ppermute | solution.py:36
  757.1 24.9 %collective-permute-start.30 = (f32[1,3,128]{2,0,1:T(1,128)S(1)}, f32[1,3,128]{2,0,1:T(1,128)S(1)}, u32[]{:S(2)}, u32[]{:S(2)}) collective-permute-start(f32[1,3,128]{2,0,1:T(1,128)S(1)} %bitcast.812), channel_id=1, source_target_pairs={{31,0},{0,1},{1,2},{2,3},{3,4},{4,5},{5,6},{6,7},{7,8},{8,9},{9,10... | collective-permute-start | bytes 4616 | tf_op jit(solution)/shard_map/ppermute | solution.py:36
  766.5 19.2 %collective-permute-start.21 = (f32[1,3,128]{2,0,1:T(1,128)S(1)}, f32[1,3,128]{2,0,1:T(1,128)S(1)}, u32[]{:S(2)}, u32[]{:S(2)}) collective-permute-start(f32[1,3,128]{2,0,1:T(1,128)S(1)} %collective-permute-done.20), channel_id=1, source_target_pairs={{32,0},{64,32},{96,64},{128,96},{160,128},{192,160},{224,192},{256... | collective-permute-start | bytes 4616 | tf_op jit(solution)/shard_map/ppermute | solution.py:36
  768.7 20.6 %collective-permute-start.24 = (f32[1,3,128]{2,0,1:T(1,128)S(1)}, f32[1,3,128]{2,0,1:T(1,128)S(1)}, u32[]{:S(2)}, u32[]{:S(2)}) collective-permute-start(f32[1,3,128]{2,0,1:T(1,128)S(1)} %collective-permute-done.23), channel_id=1, source_target_pairs={{32,0},{64,32},{96,64},{128,96},{160,128},{192,160},{224,192},{256... | collective-permute-start | bytes 4616 | tf_op jit(solution)/shard_map/ppermute | solution.py:36
  770.8 20.9 %collective-permute-start.25 = (f32[2,3,128]{2,0,1:T(2,128)S(1)}, f32[2,3,128]{2,0,1:T(2,128)S(1)}, u32[]{:S(2)}, u32[]{:S(2)}) collective-permute-start(f32[2,3,128]{2,0,1:T(2,128)S(1)} %bitcast.810), channel_id=1, source_target_pairs={{1,0},{2,1},{3,2},{4,3},{5,4},{6,5},{7,6},{8,7},{9,8},{10,9},{11,1... | collective-permute-start | bytes 9224 | tf_op jit(solution)/shard_map/ppermute | solution.py:36
  772.7 18.9 %collective-permute-start.26 = (f32[2,3,128]{2,0,1:T(2,128)S(1)}, f32[2,3,128]{2,0,1:T(2,128)S(1)}, u32[]{:S(2)}, u32[]{:S(2)}) collective-permute-start(f32[2,3,128]{2,0,1:T(2,128)S(1)} %bitcast.809), channel_id=1, source_target_pairs={{31,0},{0,1},{1,2},{2,3},{3,4},{4,5},{5,6},{6,7},{7,8},{8,9},{9,10... | collective-permute-start | bytes 9224 | tf_op jit(solution)/shard_map/ppermute | solution.py:36
  782.0 9.7 %collective-permute-start.29 = (f32[1,3,128]{2,0,1:T(1,128)S(1)}, f32[1,3,128]{2,0,1:T(1,128)S(1)}, u32[]{:S(2)}, u32[]{:S(2)}) collective-permute-start(f32[1,3,128]{2,0,1:T(1,128)S(1)} %bitcast.811), channel_id=1, source_target_pairs={{480,0},{0,32},{32,64},{64,96},{96,128},{128,160},{160,192},{192,2... | collective-permute-start | bytes 4616 | tf_op jit(solution)/shard_map/ppermute | solution.py:36
  785.7 9.4 %collective-permute-start.28 = (f32[1,3,128]{2,0,1:T(1,128)S(1)}, f32[1,3,128]{2,0,1:T(1,128)S(1)}, u32[]{:S(2)}, u32[]{:S(2)}) collective-permute-start(f32[1,3,128]{2,0,1:T(1,128)S(1)} %collective-permute-done.27), channel_id=1, source_target_pairs={{480,0},{0,32},{32,64},{64,96},{96,128},{128,160},{160,192},{192,2... | collective-permute-start | bytes 4616 | tf_op jit(solution)/shard_map/ppermute | solution.py:36
  789.3 9.4 %collective-permute-start.31 = (f32[1,3,128]{2,0,1:T(1,128)S(1)}, f32[1,3,128]{2,0,1:T(1,128)S(1)}, u32[]{:S(2)}, u32[]{:S(2)}) collective-permute-start(f32[1,3,128]{2,0,1:T(1,128)S(1)} %collective-permute-done.30), channel_id=1, source_target_pairs={{480,0},{0,32},{32,64},{64,96},{96,128},{128,160},{160,192},{192,2... | collective-permute-start | bytes 4616 | tf_op jit(solution)/shard_map/ppermute | solution.py:36
  (39 other events, 405.2 us)
where the time goes:
time: 813 us; the launch traced here: 799 us
  loops' own time  204 us (25%)
  local copies, waits for them, and re-layouts  198 us (24%)
  starting transfers between devices  173 us (21%)
  other arithmetic  113 us (14%)
  matrix products  66.3 us (8%)
  waiting for transfers between devices  43.8 us (5%)
    ppermute x24, starting transfers between devices, shifted(): return lax.ppermute(block, axis, route)  136 us
    another operation x4, loops' own time, block_update(): lax.scan(jax.checkpoint(visit_pair), start_totals, pair_lists(block_index))  97.3 us
    another operation x4, loops' own time, block_energy(): lax.scan(jax.checkpoint(visit_pair), (empty_sum, empty_sum), pair_lists(b...  90.2 us
    dynamic_slice x144, local copies, waits for them, and re-layouts, block_update(): lax.scan(jax.checkpoint(visit_pair), start_totals, pair_lists(block_index))  90.2 us
    convert_element_type x36, local copies, waits for them, and re-layouts, visit_pair(): lax.dynamic_index_in_dim(ext_features, source, 0, False)  33 us
    ppermute x24, waiting for transfers between devices, shifted(): return lax.ppermute(block, axis, route)  27.4 us
    another operation x61, local copies, waits for them, and re-layouts  24 us
    dot_general x54, matrix products, visit_pair(): jnp.einsum('bdij,dcj->bci', radial_filters[:, 1:], vectors, preferred_ele...  20.7 us
  transfers between devices with their start and end apart: 32, of which 10 were waited for; matrix products, arithmetic and copies ran while one was open for 1% of the time, Pallas kernels for 0%

commit v1 on v0

v1 whole, which is shorter than its diff:
```python
import jax
import jax.numpy as jnp
import numpy as np
from jax import lax
from jax.experimental import pallas as pl
from jax.experimental.pallas import tpu as pltpu
from jax.sharding import PartitionSpec as P

F32 = jnp.float32
BF16 = jnp.bfloat16
LENGTH = 128
BASIS = 8
NEAR = 9
FAR = 1000.0
INV_CUTOFF = 0.2
CELL_SLAB = 5.0
CELL_TILE = 10.0
VMEM_LIMIT = 56 * 1024 * 1024
FOLD = np.exp(-0.5 * np.arange(BASIS) * (np.arange(BASIS) + 1)).astype(np.float32)


def silu_pair(value):
    gate = 1.0 / (1.0 + jnp.exp(-value))
    return value * gate, gate * (1.0 + value * (1.0 - gate))


def place_atoms(pos_refs, send_ref, recv_ref):
    for tile, ref in enumerate(pos_refs):
        for row in range(4):
            real = ref[row, 3:4, :] > -0.5
            shift = ((row - 1) * CELL_SLAB, (tile - 1) * CELL_TILE, 0.0)
            for d in range(3):
                coords = ref[row, d : d + 1, :]
                sender = jnp.where(real, coords + shift[d], -FAR) * INV_CUTOFF
                send_ref[row * 3 + tile, d : d + 1, :] = sender
                if tile == 1 and row in (1, 2):
                    receiver = jnp.where(real, coords + shift[d], FAR) * INV_CUTOFF
                    spread = jnp.broadcast_to(receiver, (LENGTH, LENGTH))
                    recv_ref[row - 1, d] = jnp.transpose(spread)


def species_column(code_row):
    return jnp.transpose(jnp.broadcast_to(code_row, (LENGTH, LENGTH)))


def species_hot(code_row):
    lanes = lax.broadcasted_iota(jnp.int32, (LENGTH, LENGTH), 1)
    species = (lanes & 7).astype(F32)
    return jnp.where(species_column(code_row) == species, 1.0, 0.0).astype(BF16)


def pair_geometry(send_ref, recv_ref, block, cell, first, rows):
    apart = [
        send_ref[cell, d : d + 1, :] - recv_ref[block, d, pl.ds(first, rows), :] for d in range(3)
    ]
    square = apart[0] * apart[0] + apart[1] * apart[1] + apart[2] * apart[2]
    square = jnp.minimum(square, 1.0)
    eight = 8.0 * square
    centred = eight - 0.5
    return apart, eight, centred, jnp.exp(-0.5 * centred * centred), jnp.exp(eight), 1.0 - square


def fill_kernels(send_ref, recv_ref, kern_ref, block):
    rows = 16

    def body(step, carry):
        first = pl.multiple_of(step * rows, rows)
        for tile in range(3):
            for near in range(3):
                cell = (block + near) * 3 + tile
                apart, _, _, gauss, ratio, rest = pair_geometry(
                    send_ref, recv_ref, block, cell, first, rows
                )
                value = gauss * (rest * rest)
                if tile == 1 and near == 1:
                    own = first + lax.broadcasted_iota(jnp.int32, (rows, LENGTH), 0)
                    other = lax.broadcasted_iota(jnp.int32, (rows, LENGTH), 1)
                    value = jnp.where(own == other, 0.0, value)
                narrow = [a.astype(BF16) for a in apart]
                column = (tile * 3 + near) * LENGTH
                for b in range(BASIS):
                    radial = value.astype(BF16)
                    kern_ref[pl.ds(b * LENGTH + first, rows), column : column + LENGTH] = radial
                    for d in range(3):
                        at = (d + 1) * BASIS * LENGTH + b * LENGTH
                        kern_ref[pl.ds(at + first, rows), column : column + LENGTH] = (
                            radial * narrow[d]
                        )
                    if b + 1 < BASIS:
                        value = value * ratio
        return carry

    lax.fori_loop(0, LENGTH // rows, body, 0)


def weighted_sum(kern_ref, part, rhs, weights):
    depth = BASIS * LENGTH
    product = jnp.dot(
        kern_ref[part * depth : (part + 1) * depth, :], rhs, preferred_element_type=F32
    )
    total = product[:LENGTH] * weights[0:1, :]
    for b in range(1, BASIS):
        total = total + product[b * LENGTH : (b + 1) * LENGTH] * weights[b : b + 1, :]
    return total


def nearby(refs, block, lo, width):
    return jnp.concatenate(
        [refs[tile][block + near, lo : lo + width, :] for tile in range(3) for near in range(3)],
        axis=0,
    )


def first_kernel(
    left, middle, right, table, weights, mix, mixv, feat_out, hidden_out, vector_out,
    send_ref, recv_ref, kern_ref, start_ref,
):
    pos_refs = (left, middle, right)
    place_atoms(pos_refs, send_ref, recv_ref)
    for tile in range(3):
        for row in range(4):
            hot = species_hot(pos_refs[tile][row, 3:4, :])
            start_ref[tile, row] = jnp.dot(hot, table[...], preferred_element_type=F32).astype(BF16)

    def body(block, carry):
        fill_kernels(send_ref, recv_ref, kern_ref, block)
        rhs = jnp.concatenate(
            [start_ref[tile, block + near] for tile in range(3) for near in range(3)], axis=0
        )
        scalar = weighted_sum(kern_ref, 0, rhs, weights[0])
        invariant = scalar
        for d in range(3):
            vector = weighted_sum(kern_ref, d + 1, rhs, weights[1])
            vector_out[block, d] = vector
            invariant = invariant + vector * vector
            mixed = jnp.dot(vector.astype(BF16), mixv[...], preferred_element_type=F32)
            feat_out[block, (d + 1) * LENGTH : (d + 2) * LENGTH, :] = mixed.astype(BF16)
        hidden = jnp.dot(invariant.astype(BF16), mix[...], preferred_element_type=F32)
        hidden_out[block] = hidden
        start = start_ref[1, block + 1].astype(F32)
        feat_out[block, :LENGTH, :] = (start + silu_pair(hidden)[0]).astype(BF16)
        return carry

    lax.fori_loop(0, 2, body, 0)


def second_kernel(
    left, middle, right, feat_left, feat_middle, feat_right, weights, out_weight, out_turned, read,
    energy_out, pull_out, send_ref, recv_ref, kern_ref,
):
    pos_refs = (left, middle, right)
    feats = (feat_left, feat_middle, feat_right)
    place_atoms(pos_refs, send_ref, recv_ref)

    def body(block, carry):
        fill_kernels(send_ref, recv_ref, kern_ref, block)
        message = weighted_sum(kern_ref, 0, nearby(feats, block, 0, LENGTH), weights[0])
        for d in range(3):
            rhs = nearby(feats, block, (d + 1) * LENGTH, LENGTH)
            message = message + weighted_sum(kern_ref, d + 1, rhs, weights[1])
        own = feat_middle[block + 1, :LENGTH, :].astype(F32)
        combined = (own + message).astype(BF16)
        hidden = jnp.dot(combined, out_weight[...], preferred_element_type=F32)
        value, slope = silu_pair(hidden)
        present = species_column(middle[block + 1, 3:4, :]) > -0.5
        energy = jnp.where(present, jnp.sum(value * read[...], axis=1, keepdims=True), 0.0)
        energy_out[block] = jnp.transpose(jnp.broadcast_to(energy, (LENGTH, LENGTH)))[:8]
        back = jnp.where(present, slope * read[...], 0.0).astype(BF16)
        pull = jnp.dot(back, out_turned[...], preferred_element_type=F32)
        pull_out[block] = pull.astype(BF16)
        return carry

    lax.fori_loop(0, 2, body, 0)


def third_kernel(
    left, middle, right, feat_left, feat_middle, feat_right, pull_left, pull_middle, pull_right,
    hidden, vectors, weights_two, mix_turned, mixv_turned, spread, force_out,
    send_ref, recv_ref, kern_ref, hot_ref, lhs_ref, deriv_ref, row_ref,
):
    pos_refs = (left, middle, right)
    feats = (feat_left, feat_middle, feat_right)
    pulls = (pull_left, pull_middle, pull_right)
    place_atoms(pos_refs, send_ref, recv_ref)
    for tile in range(3):
        for row in range(4):
            hot_ref[tile, row] = species_hot(pos_refs[tile][row, 3:4, :])
    force_out[...] = jnp.zeros(force_out.shape, F32)
    depth = BASIS * LENGTH

    def body(block, carry):
        fill_kernels(send_ref, recv_ref, kern_ref, block)
        rhs = nearby(pulls, block, 0, LENGTH)
        pull = pull_middle[block + 1].astype(F32)
        scalar_grad = pull + weighted_sum(kern_ref, 0, rhs, weights_two[0])
        scalar_grad = scalar_grad.astype(BF16).astype(F32)
        hidden_grad = (scalar_grad * silu_pair(hidden[block])[1]).astype(BF16)
        inv_grad = jnp.dot(hidden_grad, mix_turned[...], preferred_element_type=F32)
        inv_grad = inv_grad.astype(BF16).astype(F32)
        grads = [inv_grad]
        for d in range(3):
            vector_grad = -weighted_sum(kern_ref, d + 1, rhs, weights_two[1])
            passed = jnp.dot(
                vector_grad.astype(BF16), mixv_turned[...], preferred_element_type=F32
            )
            passed = passed.astype(BF16).astype(F32)
            grads.append(passed + 2.0 * vectors[block, d] * inv_grad)
        lane_basis = lax.broadcasted_iota(jnp.int32, (LENGTH, LENGTH), 1) >> 3
        for r in range(4):
            which = min(r, 1)
            table_grad = jnp.dot(
                grads[r],
                spread[which],
                preferred_element_type=F32,
                precision=lax.Precision.HIGHEST,
            )
            for b in range(BASIS):
                at = r * depth + b * LENGTH
                scaled = pull * weights_two[which, b : b + 1, :]
                lhs_ref[at : at + LENGTH, :LENGTH] = scaled.astype(BF16)
                lhs_ref[at : at + LENGTH, LENGTH:] = jnp.where(
                    lane_basis == b, table_grad, 0.0
                ).astype(BF16)
        row_ref[...] = jnp.zeros(row_ref.shape, F32)
        rows = 16
        for tile in range(3):
            for near in range(3):
                for r in range(4):
                    sender = jnp.concatenate(
                        [
                            feats[tile][block + near, r * LENGTH : (r + 1) * LENGTH, :],
                            hot_ref[tile, block + near],
                        ],
                        axis=1,
                    )
                    deriv_ref[r * depth : (r + 1) * depth, :] = lax.dot_general(
                        lhs_ref[r * depth : (r + 1) * depth, :],
                        sender,
                        (((1,), (1,)), ((), ())),
                        preferred_element_type=F32,
                    )
                cell = (block + near) * 3 + tile

                def chain(step, columns):
                    first = pl.multiple_of(step * rows, rows)
                    apart, eight, centred, gauss, ratio, rest = pair_geometry(
                        send_ref, recv_ref, block, cell, first, rows
                    )
                    if tile == 1 and near == 1:
                        own = first + lax.broadcasted_iota(jnp.int32, (rows, LENGTH), 0)
                        other = lax.broadcasted_iota(jnp.int32, (rows, LENGTH), 1)
                        rest = jnp.where(own == other, 0.0, rest)
                    along = [None, None, None]
                    value = None
                    slope = None
                    for b in range(BASIS - 1, -1, -1):
                        parts = [
                            deriv_ref[pl.ds(r * depth + b * LENGTH + first, rows), :]
                            for r in range(4)
                        ]
                        joint = parts[0]
                        for d in range(3):
                            joint = joint + apart[d] * parts[d + 1]
                            along[d] = (
                                parts[d + 1]
                                if along[d] is None
                                else along[d] * ratio + parts[d + 1]
                            )
                        if value is None:
                            value = joint
                        else:
                            slope = value if slope is None else slope * ratio + value
                            value = value * ratio + joint
                    slope = slope * ratio
                    scale = gauss * rest
                    radial = (
                        scale * (8.0 * rest * (slope - centred * value) - 2.0 * value)
                    ) * (2.0 * INV_CUTOFF)
                    envelope = scale * rest * INV_CUTOFF
                    out = []
                    for d in range(3):
                        pushed = envelope * along[d] + radial * apart[d]
                        row_ref[d, pl.ds(first, rows), :] = (
                            row_ref[d, pl.ds(first, rows), :] + pushed
                        )
                        out.append(columns[d] + pushed)
                    return tuple(out)

                zero = jnp.zeros((rows, LENGTH), F32)
                columns = lax.fori_loop(0, LENGTH // rows, chain, (zero, zero, zero))
                for d in range(3):
                    force_out[tile, block + near, d : d + 1, :] = force_out[
                        tile, block + near, d : d + 1, :
                    ] - jnp.sum(columns[d], axis=0, keepdims=True)
        for d in range(3):
            total = jnp.sum(jnp.transpose(row_ref[d]), axis=0, keepdims=True)
            force_out[1, block + 1, d : d + 1, :] = (
                force_out[1, block + 1, d : d + 1, :] + total
            )
        return carry

    lax.fori_loop(0, 2, body, 0)


def ring(block, axis, step):
    count = lax.axis_size(axis)
    return lax.ppermute(block, axis, [(i, (i + step) % count) for i in range(count)])


def gather_near(cells):
    above = ring(cells[1:], "slab", 1)
    below = ring(cells[:1], "slab", -1)
    column = jnp.concatenate([above, cells, below], axis=0)
    return ring(column, "tile", 1), column, ring(column, "tile", -1)


def send_home(parts):
    column = parts[1] + ring(parts[0], "tile", -1) + ring(parts[2], "tile", 1)
    from_next = ring(column[:1], "slab", -1)
    from_last = ring(column[3:], "slab", 1)
    return column[1:3] + jnp.concatenate([from_last, from_next], axis=0)


def kernel_call(body, outs, scratch, flops):
    return pl.pallas_call(
        body,
        out_shape=[jax.ShapeDtypeStruct(shape, kind) for shape, kind in outs],
        scratch_shapes=[pltpu.VMEM(shape, kind) for shape, kind in scratch],
        compiler_params=pltpu.CompilerParams(vmem_limit_bytes=VMEM_LIMIT),
        cost_estimate=pl.CostEstimate(flops=flops, bytes_accessed=1 << 20, transcendentals=0),
    )


def on_device(
    positions, species, occupied, embedding, first_radial_weight, radial_two, mix_scalar,
    vector_channel_weight, out_weight, read_weight,
):
    codes = jnp.where(occupied > 0, species, -1).astype(F32)
    packet = jnp.concatenate([positions, codes[:, :, None]], axis=2)[:, 0]
    fold = jnp.asarray(FOLD)[None, :, None] * 0.25
    weights_one = first_radial_weight * fold
    weights_two = radial_two * fold
    table = jnp.zeros((LENGTH, LENGTH), BF16).at[: embedding.shape[0]].set(embedding)
    padded = jnp.pad(embedding.astype(F32), ((0, 8 - embedding.shape[0]), (0, 0)))
    spread = weights_one[:, :, None, :] * padded[None, None]
    spread = spread.reshape((2, 64, LENGTH))
    spread = jnp.pad(spread, ((0, 0), (0, 64), (0, 0))).transpose((0, 2, 1))
    read = read_weight[None, :]

    places = gather_near(packet)
    geometry = [
        ((12, 3, LENGTH), F32),
        ((2, 3, LENGTH, LENGTH), F32),
        ((4 * BASIS * LENGTH, NEAR * LENGTH), BF16),
    ]
    features, hidden, vectors = kernel_call(
        first_kernel,
        [
            ((2, 4 * LENGTH, LENGTH), BF16),
            ((2, LENGTH, LENGTH), F32),
            ((2, 3, LENGTH, LENGTH), F32),
        ],
        geometry + [((3, 4, LENGTH, LENGTH), BF16)],
        2400000000,
    )(*places, table, weights_one, mix_scalar, vector_channel_weight)
    all_features = gather_near(features)
    energies, pull = kernel_call(
        second_kernel,
        [((2, 8, LENGTH), F32), ((2, LENGTH, LENGTH), BF16)],
        geometry,
        2400000000,
    )(*places, *all_features, weights_two, out_weight, out_weight.T, read)
    all_pulls = gather_near(pull)
    (parts,) = kernel_call(
        third_kernel,
        [((3, 4, 3, LENGTH), F32)],
        geometry
        + [
            ((3, 4, LENGTH, LENGTH), BF16),
            ((4 * BASIS * LENGTH, 2 * LENGTH), BF16),
            ((4 * BASIS * LENGTH, LENGTH), F32),
            ((3, LENGTH, LENGTH), F32),
        ],
        7200000000,
    )(
        *places, *all_features, *all_pulls, hidden, vectors, weights_two, mix_scalar.T,
        vector_channel_weight.T, spread,
    )
    forces = send_home(parts)
    return energies[:, :1], forces[:, None]


def solution(mesh):
    in_specs = (
        P("slab", "tile", None, None),
        P("slab", "tile", None),
        P("slab", "tile", None),
        P(),
        P(),
        P(),
        P(),
        P(),
        P(),
        P(),
    )
    out_specs = (P("slab", "tile", None), P("slab", "tile", None, None))
    return jax.shard_map(
        on_device, mesh=mesh, in_specs=in_specs, out_specs=out_specs, check_vma=False
    )
```

time: 813 us -> 211 us (0.26)
  the two profiles are of different devices: /device:TPU:24 before, /device:TPU:102 now
where the time goes in v1:
time: 211 us; the launch traced here: 210 us
  waiting for transfers between devices  77.3 us (37%)
  Pallas kernels  65.9 us (31%)
  starting transfers between devices  52.5 us (25%)
  local copies, waits for them, and re-layouts  11.6 us (5%)
    ppermute x16, waiting for transfers between devices, ring(): lax.ppermute(block, axis, [(i, (i + step) % count) for i in range(count)])  77.3 us
    ppermute x16, starting transfers between devices, ring(): lax.ppermute(block, axis, [(i, (i + step) % count) for i in range(count)])  52.5 us
    pallas_call x1, Pallas kernels, on_device(): kernel_call(third_kernel, [((3, 4, 3, LENGTH), F32)], geometry + [((3, 4,...  39.1 us
    pallas_call x1, Pallas kernels, on_device(): kernel_call(first_kernel, [((2, 4 * LENGTH, LENGTH), BF16), ((2, LENGTH,...  14.4 us
    pallas_call x1, Pallas kernels, on_device(): kernel_call(second_kernel, [((2, 8, LENGTH), F32), ((2, LENGTH, LENGTH),...  12.4 us
    unnamed x51, local copies, waits for them, and re-layouts  6.32 us
  transfers between devices with their start and end apart: 16, of which 11 were waited for; matrix products, arithmetic and copies ran while one was open for 3% of the time, Pallas kernels for 0%

profile of v1, /device:TPU:102, one launch (start us, length us, event | category | flops | bytes accessed | tf_op | source)
XLA Modules:
  0.0 209.7 jit_solution(10305532116537453665)
XLA Ops:
  2.0 6.4 %collective-permute-start = (f32[1,4,128]{2,1,0:T(4,128)S(1)}, f32[1,4,128]{2,1,0:T(4,128)S(1)}, u32[]{:S(2)}, u32[]{:S(2)}) collective-permute-start(f32[1,4,128]{2,1,0:T(4,128)S(1)} %get-tuple-element.36), channel_id=1, source_target_pairs={{0,32},{32,64},{64,96},{96,128},{128,160},{160,192},{192,224},{224... | collective-permute-start | bytes 6152 | tf_op jit(solution)/shard_map/ppermute | solution.py:307
  8.4 1.9 collective-permute-start.1
  10.4 7.4 %collective-permute-done.1 = f32[1,4,128]{2,1,0:T(4,128)S(1)} collective-permute-done((f32[1,4,128]{2,1,0:T(4,128)S(1)}, f32[1,4,128]{2,1,0:T(4,128)S(1)}, u32[]{:S(2)}, u32[]{:S(2)}) %collective-permute-start.1) | collective-permute-done | bytes 2080 | tf_op jit(solution)/shard_map/ppermute | solution.py:307
  17.8 8.0 %collective-permute-start.3 = (f32[4,4,128]{2,1,0:T(4,128)S(1)}, f32[4,4,128]{2,1,0:T(4,128)S(1)}, u32[]{:S(2)}, u32[]{:S(2)}) collective-permute-start(f32[4,4,128]{2,1,0:T(4,128)S(1)} %pad_maximum_fusion.middle), channel_id=1, source_target_pairs={{0,31},{1,0},{2,1},{3,2},{4,3},{5,4},{6,5},{7,6},{8,7},{9,8},{10,9... | collective-permute-start | bytes 24584 | tf_op jit(solution)/shard_map/ppermute | solution.py:307
  25.8 1.9 collective-permute-start.2
  29.1 7.7 %collective-permute-done.2.left = f32[4,4,128]{2,1,0:T(4,128)S(1)} collective-permute-done((f32[4,4,128]{2,1,0:T(4,128)S(1)}, f32[4,4,128]{2,1,0:T(4,128)S(1)}, u32[]{:S(2)}, u32[]{:S(2)}) %collective-permute-start.2) | collective-permute-done | bytes 8224 | tf_op jit(solution)/shard_map/ppermute | solution.py:307
  37.4 14.4 %shard_map.122 = (bf16[2,512,128]{2,1,0:T(8,128)(2,1)}, f32[2,128,128]{2,1,0:T(8,128)}, f32[2,3,128,128]{3,2,1,0:T(8,128)}) custom-call(f32[4,4,128]{2,1,0:T(4,128)} %copy-done.20, f32[4,4,128]{2,1,0:T(4,128)} %copy-done.9, f32[4,4,128]{2,1,0:T(4,128)} %copy-done.19, bf16[128,128]{1,0:T(8,128)(2,1)} %scatter.4.table, ...), custom_call_target="tpu_custom_call" | custom-call | flops 2400000000 | bytes 1048576 | tf_op jit(solution)/shard_map/pallas_call | solution.py:356
  51.7 1.0 fusion.9
  52.7 2.1 collective-permute-start.4
  54.8 3.9 %collective-permute-start.5 = (bf16[1,512,128]{2,1,0:T(8,128)(2,1)S(1)}, bf16[1,512,128]{2,1,0:T(8,128)(2,1)S(1)}, u32[]{:S(2)}, u32[]{:S(2)}) collective-permute-start(bf16[1,512,128]{2,1,0:T(8,128)(2,1)S(1)} %get-tuple-element.28), channel_id=1, source_target_pairs={{0,480},{32,0},{64,32},{96,64},{128,96},{160,128},{192,160},{224,1... | collective-permute-start | bytes 393224 | tf_op jit(solution)/shard_map/ppermute | solution.py:307
  58.7 1.0 collective-permute-done.4
  59.8 15.1 %collective-permute-done.5 = bf16[1,512,128]{2,1,0:T(8,128)(2,1)S(1)} collective-permute-done((bf16[1,512,128]{2,1,0:T(8,128)(2,1)S(1)}, bf16[1,512,128]{2,1,0:T(8,128)(2,1)S(1)}, u32[]{:S(2)}, u32[]{:S(2)}) %collective-permute-start.5) | collective-permute-done | bytes 131104 | tf_op jit(solution)/shard_map/ppermute | solution.py:307
  75.0 1.9 collective-permute-start.7
  76.9 2.4 %collective-permute-start.6 = (bf16[4,512,128]{2,1,0:T(8,128)(2,1)S(1)}, bf16[4,512,128]{2,1,0:T(8,128)(2,1)S(1)}, u32[]{:S(2)}, u32[]{:S(2)}) collective-permute-start(bf16[4,512,128]{2,1,0:T(8,128)(2,1)S(1)} %constant_dynamic-update-slice_fusion.feat_middle), channel_id=1, source_target_pairs={{0,1},{1,2},{2,3},{3,4},{4,5},{5,6},{6,7},{7,8},{8,9},{9,10},{10,1... | collective-permute-start | bytes 1572872 | tf_op jit(solution)/shard_map/ppermute | solution.py:307
  80.1 4.3 %collective-permute-done.7.feat_right = bf16[4,512,128]{2,1,0:T(8,128)(2,1)S(1)} collective-permute-done((bf16[4,512,128]{2,1,0:T(8,128)(2,1)S(1)}, bf16[4,512,128]{2,1,0:T(8,128)(2,1)S(1)}, u32[]{:S(2)}, u32[]{:S(2)}) %collective-permute-start.7) | collective-permute-done | bytes 524320 | tf_op jit(solution)/shard_map/ppermute | solution.py:307
  84.4 12.3 %collective-permute-done.6.feat_left = bf16[4,512,128]{2,1,0:T(8,128)(2,1)S(1)} collective-permute-done((bf16[4,512,128]{2,1,0:T(8,128)(2,1)S(1)}, bf16[4,512,128]{2,1,0:T(8,128)(2,1)S(1)}, u32[]{:S(2)}, u32[]{:S(2)}) %collective-permute-start.6) | collective-permute-done | bytes 524320 | tf_op jit(solution)/shard_map/ppermute | solution.py:307
  97.5 12.4 %shard_map.123 = (f32[2,8,128]{2,1,0:T(8,128)}, bf16[2,128,128]{2,1,0:T(8,128)(2,1)}) custom-call(f32[4,4,128]{2,1,0:T(4,128)} %copy-done.20, f32[4,4,128]{2,1,0:T(4,128)} %copy-done.9, f32[4,4,128]{2,1,0:T(4,128)} %copy-done.19, bf16[4,512,128]{2,1,0:T(8,128)(2,1)} %copy-done.16, bf16[4,512,128]{2,1,0:T(8,128)(2,1)} %copy-done.2, ...), custom_call_target="tpu_custom_call" | custom-call | flops 2400000000 | bytes 1048576 | tf_op jit(solution)/shard_map/pallas_call | solution.py:367
  110.7 5.7 %collective-permute-start.8 = (bf16[1,128,128]{2,1,0:T(8,128)(2,1)S(1)}, bf16[1,128,128]{2,1,0:T(8,128)(2,1)S(1)}, u32[]{:S(2)}, u32[]{:S(2)}) collective-permute-start(bf16[1,128,128]{2,1,0:T(8,128)(2,1)S(1)} %get-tuple-element.31), channel_id=1, source_target_pairs={{0,32},{32,64},{64,96},{96,128},{128,160},{160,192},{192,224},{224... | collective-permute-start | bytes 98312 | tf_op jit(solution)/shard_map/ppermute | solution.py:307
  116.7 3.6 %collective-permute-start.9 = (bf16[1,128,128]{2,1,0:T(8,128)(2,1)S(1)}, bf16[1,128,128]{2,1,0:T(8,128)(2,1)S(1)}, u32[]{:S(2)}, u32[]{:S(2)}) collective-permute-start(bf16[1,128,128]{2,1,0:T(8,128)(2,1)S(1)} %get-tuple-element.30), channel_id=1, source_target_pairs={{0,480},{32,0},{64,32},{96,64},{128,96},{160,128},{192,160},{224,1... | collective-permute-start | bytes 98312 | tf_op jit(solution)/shard_map/ppermute | solution.py:307
  120.3 1.1 collective-permute-done.8
  121.4 5.1 %collective-permute-done.9 = bf16[1,128,128]{2,1,0:T(8,128)(2,1)S(1)} collective-permute-done((bf16[1,128,128]{2,1,0:T(8,128)(2,1)S(1)}, bf16[1,128,128]{2,1,0:T(8,128)(2,1)S(1)}, u32[]{:S(2)}, u32[]{:S(2)}) %collective-permute-start.9) | collective-permute-done | bytes 32800 | tf_op jit(solution)/shard_map/ppermute | solution.py:307
  126.5 1.9 collective-permute-start.11
  128.5 2.6 %collective-permute-start.10 = (bf16[4,128,128]{2,1,0:T(8,128)(2,1)S(1)}, bf16[4,128,128]{2,1,0:T(8,128)(2,1)S(1)}, u32[]{:S(2)}, u32[]{:S(2)}) collective-permute-start(bf16[4,128,128]{2,1,0:T(8,128)(2,1)S(1)} %constant_dynamic-update-slice_fusion.3.pull_middle), channel_id=1, source_target_pairs={{0,1},{1,2},{2,3},{3,4},{4,5},{5,6},{6,7},{7,8},{8,9},{9,10},{10,1... | collective-permute-start | bytes 393224 | tf_op jit(solution)/shard_map/ppermute | solution.py:307
  133.3 8.9 %collective-permute-done.10.pull_left = bf16[4,128,128]{2,1,0:T(8,128)(2,1)S(1)} collective-permute-done((bf16[4,128,128]{2,1,0:T(8,128)(2,1)S(1)}, bf16[4,128,128]{2,1,0:T(8,128)(2,1)S(1)}, u32[]{:S(2)}, u32[]{:S(2)}) %collective-permute-start.10) | collective-permute-done | bytes 131104 | tf_op jit(solution)/shard_map/ppermute | solution.py:307
  142.8 39.1 %shard_map.124 = f32[3,4,3,128]{3,2,1,0:T(4,128)} custom-call(f32[4,4,128]{2,1,0:T(4,128)} %copy-done.20, f32[4,4,128]{2,1,0:T(4,128)} %copy-done.9, f32[4,4,128]{2,1,0:T(4,128)} %copy-done.19, bf16[4,512,128]{2,1,0:T(8,128)(2,1)} %copy-done.16, bf16[4,512,128]{2,1,0:T(8,128)(2,1)} %copy-done.2, bf16[4,512,128]{2,1,0:T(8,128)(2,1)} %copy-done.15, ...), custom_call_target="tpu_custom_call" | custom-call | flops 7200000000 | bytes 1048576 | tf_op jit(solution)/shard_map/pallas_call | solution.py:374
  182.7 1.9 collective-permute-start.12
  184.6 2.4 %collective-permute-start.13 = (f32[4,3,128]{2,1,0:T(4,128)S(1)}, f32[4,3,128]{2,1,0:T(4,128)S(1)}, u32[]{:S(2)}, u32[]{:S(2)}) collective-permute-start(f32[4,3,128]{2,1,0:T(4,128)S(1)} %get-tuple-element.33), channel_id=1, source_target_pairs={{0,1},{1,2},{2,3},{3,4},{4,5},{5,6},{6,7},{7,8},{8,9},{9,10},{10,1... | collective-permute-start | bytes 18440 | tf_op jit(solution)/shard_map/ppermute | solution.py:307
  187.0 8.6 %collective-permute-done.13 = f32[4,3,128]{2,1,0:T(4,128)S(1)} collective-permute-done((f32[4,3,128]{2,1,0:T(4,128)S(1)}, f32[4,3,128]{2,1,0:T(4,128)S(1)}, u32[]{:S(2)}, u32[]{:S(2)}) %collective-permute-start.13) | collective-permute-done | bytes 6176 | tf_op jit(solution)/shard_map/ppermute | solution.py:307
  196.3 3.4 %collective-permute-start.14 = (f32[1,3,128]{2,1,0:T(4,128)S(1)}, f32[1,3,128]{2,1,0:T(4,128)S(1)}, u32[]{:S(2)}, u32[]{:S(2)}) collective-permute-start(f32[1,3,128]{2,1,0:T(4,128)S(1)} %get-tuple-element.34), channel_id=1, source_target_pairs={{0,32},{32,64},{64,96},{96,128},{128,160},{160,192},{192,224},{224... | collective-permute-start | bytes 4616 | tf_op jit(solution)/shard_map/ppermute | solution.py:307
  199.7 2.4 %collective-permute-start.15 = (f32[1,3,128]{2,1,0:T(4,128)S(1)}, f32[1,3,128]{2,1,0:T(4,128)S(1)}, u32[]{:S(2)}, u32[]{:S(2)}) collective-permute-start(f32[1,3,128]{2,1,0:T(4,128)S(1)} %get-tuple-element.35), channel_id=1, source_target_pairs={{0,480},{32,0},{64,32},{96,64},{128,96},{160,128},{192,160},{224,1... | collective-permute-start | bytes 4616 | tf_op jit(solution)/shard_map/ppermute | solution.py:307
  202.1 1.3 slice.67
  203.4 5.7 %collective-permute-done.15 = f32[1,3,128]{2,1,0:T(4,128)S(1)} collective-permute-done((f32[1,3,128]{2,1,0:T(4,128)S(1)}, f32[1,3,128]{2,1,0:T(4,128)S(1)}, u32[]{:S(2)}, u32[]{:S(2)}) %collective-permute-start.15) | collective-permute-done | bytes 1568 | tf_op jit(solution)/shard_map/ppermute | solution.py:307
  (76 shorter events, 10.8 us)
Async XLA Ops:
  2.0 8.4 %collective-permute-start = (f32[1,4,128]{2,1,0:T(4,128)S(1)}, f32[1,4,128]{2,1,0:T(4,128)S(1)}, u32[]{:S(2)}, u32[]{:S(2)}) collective-permute-start(f32[1,4,128]{2,1,0:T(4,128)S(1)} %get-tuple-element.36), channel_id=1, source_target_pairs={{0,32},{32,64},{64,96},{96,128},{128,160},{160,192},{192,224},{224... | collective-permute-start | bytes 6152 | tf_op jit(solution)/shard_map/ppermute | solution.py:307
  8.4 9.4 %collective-permute-start.1 = (f32[1,4,128]{2,1,0:T(4,128)S(1)}, f32[1,4,128]{2,1,0:T(4,128)S(1)}, u32[]{:S(2)}, u32[]{:S(2)}) collective-permute-start(f32[1,4,128]{2,1,0:T(4,128)S(1)} %get-tuple-element.37), channel_id=1, source_target_pairs={{0,480},{32,0},{64,32},{96,64},{128,96},{160,128},{192,160},{224,1... | collective-permute-start | bytes 6152 | tf_op jit(solution)/shard_map/ppermute | solution.py:307
  10.4 17.4 %copy-start.14 = (f32[8]{0:T(128)S(1)}, f32[8]{0:T(128)}, u32[]{:S(2)}) copy-start(f32[8]{0:T(128)} %constant.50) | copy-start | bytes 100
  10.4 17.3 %copy-start.10 = (f32[2,8,128]{2,1,0:T(8,128)S(1)}, f32[2,8,128]{2,1,0:T(8,128)}, u32[]{:S(2)}) copy-start(f32[2,8,128]{2,1,0:T(8,128)} %param.18) | copy-start | bytes 24580
  10.4 17.3 %copy-start.11 = (f32[2,8,128]{2,1,0:T(8,128)S(1)}, f32[2,8,128]{2,1,0:T(8,128)}, u32[]{:S(2)}) copy-start(f32[2,8,128]{2,1,0:T(8,128)} %param.17) | copy-start | bytes 24580
  17.8 10.6 %copy-start.9 = (f32[4,4,128]{2,1,0:T(4,128)}, f32[4,4,128]{2,1,0:T(4,128)S(1)}, u32[]{:S(2)}) copy-start(f32[4,4,128]{2,1,0:T(4,128)S(1)} %pad_maximum_fusion.middle) | copy-start | bytes 24580
  17.8 10.6 %copy-start.7 = (bf16[6,128]{1,0:T(8,128)(2,1)S(1)}, bf16[6,128]{1,0:T(8,128)(2,1)}, u32[]{:S(2)}) copy-start(bf16[6,128]{1,0:T(8,128)(2,1)} %param.16) | copy-start | bytes 4612
  17.8 11.2 %collective-permute-start.3 = (f32[4,4,128]{2,1,0:T(4,128)S(1)}, f32[4,4,128]{2,1,0:T(4,128)S(1)}, u32[]{:S(2)}, u32[]{:S(2)}) collective-permute-start(f32[4,4,128]{2,1,0:T(4,128)S(1)} %pad_maximum_fusion.middle), channel_id=1, source_target_pairs={{0,31},{1,0},{2,1},{3,2},{4,3},{5,4},{6,5},{7,6},{8,7},{9,8},{10,9... | collective-permute-start | bytes 24584 | tf_op jit(solution)/shard_map/ppermute | solution.py:307
  25.8 11.0 %collective-permute-start.2 = (f32[4,4,128]{2,1,0:T(4,128)S(1)}, f32[4,4,128]{2,1,0:T(4,128)S(1)}, u32[]{:S(2)}, u32[]{:S(2)}) collective-permute-start(f32[4,4,128]{2,1,0:T(4,128)S(1)} %pad_maximum_fusion.middle), channel_id=1, source_target_pairs={{0,1},{1,2},{2,3},{3,4},{4,5},{5,6},{6,7},{7,8},{8,9},{9,10},{10,1... | collective-permute-start | bytes 24584 | tf_op jit(solution)/shard_map/ppermute | solution.py:307
  29.1 7.7 %copy-start.19 = (f32[4,4,128]{2,1,0:T(4,128)}, f32[4,4,128]{2,1,0:T(4,128)S(1)}, u32[]{:S(2)}) copy-start(f32[4,4,128]{2,1,0:T(4,128)S(1)} %collective-permute-done.3.right) | copy-start | bytes 24580
  52.7 7.0 %copy-start = (bf16[2,512,128]{2,1,0:T(8,128)(2,1)S(1)}, bf16[2,512,128]{2,1,0:T(8,128)(2,1)}, u32[]{:S(2)}) copy-start(bf16[2,512,128]{2,1,0:T(8,128)(2,1)} %get-tuple-element.19) | copy-start | bytes 786436
  52.7 7.0 %collective-permute-start.4 = (bf16[1,512,128]{2,1,0:T(8,128)(2,1)S(1)}, bf16[1,512,128]{2,1,0:T(8,128)(2,1)S(1)}, u32[]{:S(2)}, u32[]{:S(2)}) collective-permute-start(bf16[1,512,128]{2,1,0:T(8,128)(2,1)S(1)} %get-tuple-element.29), channel_id=1, source_target_pairs={{0,32},{32,64},{64,96},{96,128},{128,160},{160,192},{192,224},{224... | collective-permute-start | bytes 393224 | tf_op jit(solution)/shard_map/ppermute | solution.py:307
  54.8 20.1 %collective-permute-start.5 = (bf16[1,512,128]{2,1,0:T(8,128)(2,1)S(1)}, bf16[1,512,128]{2,1,0:T(8,128)(2,1)S(1)}, u32[]{:S(2)}, u32[]{:S(2)}) collective-permute-start(bf16[1,512,128]{2,1,0:T(8,128)(2,1)S(1)} %get-tuple-element.28), channel_id=1, source_target_pairs={{0,480},{32,0},{64,32},{96,64},{128,96},{160,128},{192,160},{224,1... | collective-permute-start | bytes 393224 | tf_op jit(solution)/shard_map/ppermute | solution.py:307
  59.8 19.5 %copy-start.3 = (bf16[128,128]{1,0:T(8,128)(2,1)S(1)}, bf16[128,128]{1,0:T(8,128)(2,1)}, u32[]{:S(2)}) copy-start(bf16[128,128]{1,0:T(8,128)(2,1)} %out_weight.1) | copy-start | bytes 98308
  75.0 5.1 %copy-start.6 = (f32[2,8,128]{2,1,0:T(8,128)S(1)}, f32[2,8,128]{2,1,0:T(8,128)}, u32[]{:S(2)}) copy-start(f32[2,8,128]{2,1,0:T(8,128)} %get-tuple-element.39.weights) | copy-start | bytes 24580
  75.0 21.8 %copy-start.2 = (bf16[4,512,128]{2,1,0:T(8,128)(2,1)}, bf16[4,512,128]{2,1,0:T(8,128)(2,1)S(1)}, u32[]{:S(2)}) copy-start(bf16[4,512,128]{2,1,0:T(8,128)(2,1)S(1)} %constant_dynamic-update-slice_fusion.feat_middle) | copy-start | bytes 1572868
  75.0 9.4 %collective-permute-start.7 = (bf16[4,512,128]{2,1,0:T(8,128)(2,1)S(1)}, bf16[4,512,128]{2,1,0:T(8,128)(2,1)S(1)}, u32[]{:S(2)}, u32[]{:S(2)}) collective-permute-start(bf16[4,512,128]{2,1,0:T(8,128)(2,1)S(1)} %constant_dynamic-update-slice_fusion.feat_middle), channel_id=1, source_target_pairs={{0,31},{1,0},{2,1},{3,2},{4,3},{5,4},{6,5},{7,6},{8,7},{9,8},{10,9... | collective-permute-start | bytes 1572872 | tf_op jit(solution)/shard_map/ppermute | solution.py:307
  76.9 19.8 %collective-permute-start.6 = (bf16[4,512,128]{2,1,0:T(8,128)(2,1)S(1)}, bf16[4,512,128]{2,1,0:T(8,128)(2,1)S(1)}, u32[]{:S(2)}, u32[]{:S(2)}) collective-permute-start(bf16[4,512,128]{2,1,0:T(8,128)(2,1)S(1)} %constant_dynamic-update-slice_fusion.feat_middle), channel_id=1, source_target_pairs={{0,1},{1,2},{2,3},{3,4},{4,5},{5,6},{6,7},{7,8},{8,9},{9,10},{10,1... | collective-permute-start | bytes 1572872 | tf_op jit(solution)/shard_map/ppermute | solution.py:307
  84.4 12.3 %copy-start.15 = (bf16[4,512,128]{2,1,0:T(8,128)(2,1)}, bf16[4,512,128]{2,1,0:T(8,128)(2,1)S(1)}, u32[]{:S(2)}) copy-start(bf16[4,512,128]{2,1,0:T(8,128)(2,1)S(1)} %collective-permute-done.7.feat_right) | copy-start | bytes 1572868
  96.7 0.8 copy-start.16
  110.7 10.6 %collective-permute-start.8 = (bf16[1,128,128]{2,1,0:T(8,128)(2,1)S(1)}, bf16[1,128,128]{2,1,0:T(8,128)(2,1)S(1)}, u32[]{:S(2)}, u32[]{:S(2)}) collective-permute-start(bf16[1,128,128]{2,1,0:T(8,128)(2,1)S(1)} %get-tuple-element.31), channel_id=1, source_target_pairs={{0,32},{32,64},{64,96},{96,128},{128,160},{160,192},{192,224},{224... | collective-permute-start | bytes 98312 | tf_op jit(solution)/shard_map/ppermute | solution.py:307
  116.7 4.7 %copy-start.1 = (bf16[2,128,128]{2,1,0:T(8,128)(2,1)S(1)}, bf16[2,128,128]{2,1,0:T(8,128)(2,1)}, u32[]{:S(2)}) copy-start(bf16[2,128,128]{2,1,0:T(8,128)(2,1)} %get-tuple-element.21) | copy-start | bytes 196612
  116.7 9.8 %collective-permute-start.9 = (bf16[1,128,128]{2,1,0:T(8,128)(2,1)S(1)}, bf16[1,128,128]{2,1,0:T(8,128)(2,1)S(1)}, u32[]{:S(2)}, u32[]{:S(2)}) collective-permute-start(bf16[1,128,128]{2,1,0:T(8,128)(2,1)S(1)} %get-tuple-element.30), channel_id=1, source_target_pairs={{0,480},{32,0},{64,32},{96,64},{128,96},{160,128},{192,160},{224,1... | collective-permute-start | bytes 98312 | tf_op jit(solution)/shard_map/ppermute | solution.py:307
  126.5 4.6 %copy-start.8 = (bf16[4,128,128]{2,1,0:T(8,128)(2,1)}, bf16[4,128,128]{2,1,0:T(8,128)(2,1)S(1)}, u32[]{:S(2)}) copy-start(bf16[4,128,128]{2,1,0:T(8,128)(2,1)S(1)} %constant_dynamic-update-slice_fusion.3.pull_middle) | copy-start | bytes 393220
  126.5 4.6 %copy-start.4 = (bf16[128,128]{1,0:T(8,128)(2,1)S(1)}, bf16[128,128]{1,0:T(8,128)(2,1)}, u32[]{:S(2)}) copy-start(bf16[128,128]{1,0:T(8,128)(2,1)} %mix.1) | copy-start | bytes 98308
  126.5 6.7 %collective-permute-start.11 = (bf16[4,128,128]{2,1,0:T(8,128)(2,1)S(1)}, bf16[4,128,128]{2,1,0:T(8,128)(2,1)S(1)}, u32[]{:S(2)}, u32[]{:S(2)}) collective-permute-start(bf16[4,128,128]{2,1,0:T(8,128)(2,1)S(1)} %constant_dynamic-update-slice_fusion.3.pull_middle), channel_id=1, source_target_pairs={{0,31},{1,0},{2,1},{3,2},{4,3},{5,4},{6,5},{7,6},{8,7},{9,8},{10,9... | collective-permute-start | bytes 393224 | tf_op jit(solution)/shard_map/ppermute | solution.py:307
  128.5 13.7 %collective-permute-start.10 = (bf16[4,128,128]{2,1,0:T(8,128)(2,1)S(1)}, bf16[4,128,128]{2,1,0:T(8,128)(2,1)S(1)}, u32[]{:S(2)}, u32[]{:S(2)}) collective-permute-start(bf16[4,128,128]{2,1,0:T(8,128)(2,1)S(1)} %constant_dynamic-update-slice_fusion.3.pull_middle), channel_id=1, source_target_pairs={{0,1},{1,2},{2,3},{3,4},{4,5},{5,6},{6,7},{7,8},{8,9},{9,10},{10,1... | collective-permute-start | bytes 393224 | tf_op jit(solution)/shard_map/ppermute | solution.py:307
  133.2 8.9 %copy-start.17 = (bf16[4,128,128]{2,1,0:T(8,128)(2,1)}, bf16[4,128,128]{2,1,0:T(8,128)(2,1)S(1)}, u32[]{:S(2)}) copy-start(bf16[4,128,128]{2,1,0:T(8,128)(2,1)S(1)} %collective-permute-done.11.pull_right) | copy-start | bytes 393220
  182.7 4.3 %collective-permute-start.12 = (f32[4,3,128]{2,1,0:T(4,128)S(1)}, f32[4,3,128]{2,1,0:T(4,128)S(1)}, u32[]{:S(2)}, u32[]{:S(2)}) collective-permute-start(f32[4,3,128]{2,1,0:T(4,128)S(1)} %get-tuple-element.32), channel_id=1, source_target_pairs={{0,31},{1,0},{2,1},{3,2},{4,3},{5,4},{6,5},{7,6},{8,7},{9,8},{10,9... | collective-permute-start | bytes 18440 | tf_op jit(solution)/shard_map/ppermute | solution.py:307
  184.6 11.0 %collective-permute-start.13 = (f32[4,3,128]{2,1,0:T(4,128)S(1)}, f32[4,3,128]{2,1,0:T(4,128)S(1)}, u32[]{:S(2)}, u32[]{:S(2)}) collective-permute-start(f32[4,3,128]{2,1,0:T(4,128)S(1)} %get-tuple-element.33), channel_id=1, source_target_pairs={{0,1},{1,2},{2,3},{3,4},{4,5},{5,6},{6,7},{7,8},{8,9},{9,10},{10,1... | collective-permute-start | bytes 18440 | tf_op jit(solution)/shard_map/ppermute | solution.py:307
  196.3 7.1 %collective-permute-start.14 = (f32[1,3,128]{2,1,0:T(4,128)S(1)}, f32[1,3,128]{2,1,0:T(4,128)S(1)}, u32[]{:S(2)}, u32[]{:S(2)}) collective-permute-start(f32[1,3,128]{2,1,0:T(4,128)S(1)} %get-tuple-element.34), channel_id=1, source_target_pairs={{0,32},{32,64},{64,96},{96,128},{128,160},{160,192},{192,224},{224... | collective-permute-start | bytes 4616 | tf_op jit(solution)/shard_map/ppermute | solution.py:307
  199.7 9.4 %collective-permute-start.15 = (f32[1,3,128]{2,1,0:T(4,128)S(1)}, f32[1,3,128]{2,1,0:T(4,128)S(1)}, u32[]{:S(2)}, u32[]{:S(2)}) collective-permute-start(f32[1,3,128]{2,1,0:T(4,128)S(1)} %get-tuple-element.35), channel_id=1, source_target_pairs={{0,480},{32,0},{64,32},{96,64},{128,96},{160,128},{192,160},{224,1... | collective-permute-start | bytes 4616 | tf_op jit(solution)/shard_map/ppermute | solution.py:307
  (5 other events, 3.4 us)

commit v2 on v1

v2 whole, which is shorter than its diff:
```python
import functools

import jax
import jax.numpy as jnp
from jax import lax
from jax.experimental import pallas as pl
from jax.experimental.pallas import tpu as pltpu
from jax.sharding import PartitionSpec as P

F32 = jnp.float32
BF16 = jnp.bfloat16
LENGTH = 128
BASIS = 8
NEAR = 9
FAR = 1000.0
INV_CUTOFF = 0.2
CELL_SLAB = 5.0
CELL_TILE = 10.0
VMEM_LIMIT = 32 * 1024 * 1024


def silu_pair(value):
    gate = 1.0 / (1.0 + jnp.exp(-value))
    return value * gate, gate * (1.0 + value * (1.0 - gate))


OWN_SLOTS = ((0, 0), (1, 0), (2, 0))


def slots_of(flag_ref):
    flag = flag_ref[0]
    turn = (2 * flag - 1).astype(F32) * CELL_TILE
    return ((0, flag), (0, 1 - flag), (1, 1 - flag)), (turn, 0.0, -turn)


def place_atoms(pairs, slots, turns, send_ref, recv_ref):
    for tile in range(3):
        ref, member = pairs[slots[tile][0]], slots[tile][1]
        for row in range(4):
            cell = ref[member, row]
            real = cell[3:4] > -0.5
            shift = ((row - 1) * CELL_SLAB, turns[tile], 0.0)
            for d in range(3):
                coords = cell[d : d + 1] + shift[d]
                sender = jnp.where(real, coords, -FAR) * INV_CUTOFF
                send_ref[row * 3 + tile, d : d + 1, :] = sender
                if tile == 1 and row in (1, 2):
                    receiver = jnp.where(real, coords, FAR) * INV_CUTOFF
                    spread = jnp.broadcast_to(receiver, (LENGTH, LENGTH))
                    recv_ref[row - 1, d] = jnp.transpose(spread)


def folded(weights, which):
    order = lax.broadcasted_iota(jnp.int32, (BASIS, LENGTH), 0).astype(F32)
    return weights[which] * (0.25 * jnp.exp(-0.5 * order * (order + 1.0)))


def species_rows(embedding):
    table = embedding[...].astype(F32)
    return jnp.concatenate([table, jnp.zeros((8 - table.shape[0], LENGTH), F32)], axis=0)


def turned_dot(lhs, rhs, **kinds):
    return lax.dot_general(
        lhs, rhs, (((1,), (1,)), ((), ())), preferred_element_type=F32, **kinds
    )


def species_column(code_row):
    return jnp.transpose(jnp.broadcast_to(code_row, (LENGTH, LENGTH)))


def species_hot(code_row):
    lanes = lax.broadcasted_iota(jnp.int32, (LENGTH, LENGTH), 1)
    species = (lanes & 7).astype(F32)
    return jnp.where(species_column(code_row) == species, 1.0, 0.0).astype(BF16)


def pair_geometry(send_ref, recv_ref, block, cell, first, rows):
    apart = [
        send_ref[cell, d : d + 1, :] - recv_ref[block, d, pl.ds(first, rows), :] for d in range(3)
    ]
    square = apart[0] * apart[0] + apart[1] * apart[1] + apart[2] * apart[2]
    square = jnp.minimum(square, 1.0)
    eight = 8.0 * square
    centred = eight - 0.5
    return apart, eight, centred, jnp.exp(-0.5 * centred * centred), jnp.exp(eight), 1.0 - square


def fill_kernels(send_ref, recv_ref, kern_ref, block):
    rows = 16

    def body(step, carry):
        first = pl.multiple_of(step * rows, rows)
        for tile in range(3):
            for near in range(3):
                cell = (block + near) * 3 + tile
                apart, _, _, gauss, ratio, rest = pair_geometry(
                    send_ref, recv_ref, block, cell, first, rows
                )
                value = gauss * (rest * rest)
                if tile == 1 and near == 1:
                    own = first + lax.broadcasted_iota(jnp.int32, (rows, LENGTH), 0)
                    other = lax.broadcasted_iota(jnp.int32, (rows, LENGTH), 1)
                    value = jnp.where(own == other, 0.0, value)
                narrow = [a.astype(BF16) for a in apart]
                column = (tile * 3 + near) * LENGTH
                for b in range(BASIS):
                    radial = value.astype(BF16)
                    kern_ref[pl.ds(b * LENGTH + first, rows), column : column + LENGTH] = radial
                    for d in range(3):
                        at = (d + 1) * BASIS * LENGTH + b * LENGTH
                        kern_ref[pl.ds(at + first, rows), column : column + LENGTH] = (
                            radial * narrow[d]
                        )
                    if b + 1 < BASIS:
                        value = value * ratio
        return carry

    lax.fori_loop(0, LENGTH // rows, body, 0)


def weighted_sum(kern_ref, part, rhs, weights):
    depth = BASIS * LENGTH
    product = jnp.dot(
        kern_ref[part * depth : (part + 1) * depth, :], rhs, preferred_element_type=F32
    )
    total = product[:LENGTH] * weights[0:1, :]
    for b in range(1, BASIS):
        total = total + product[b * LENGTH : (b + 1) * LENGTH] * weights[b : b + 1, :]
    return total


def nearby(pairs, slots, block, lo, width):
    return jnp.concatenate(
        [
            pairs[which][member, block + near, lo : lo + width, :]
            for which, member in slots
            for near in range(3)
        ],
        axis=0,
    )


def first_kernel(
    flag, even, odd, embedding, weights, mix, mixv, feat_out, hidden_out, vector_out,
    send_ref, recv_ref, kern_ref, start_ref,
):
    pairs = (even, odd)
    slots, turns = slots_of(flag)
    place_atoms(pairs, slots, turns, send_ref, recv_ref)
    table = jnp.concatenate([species_rows(embedding)] * 16, axis=0).astype(BF16)
    for tile in range(3):
        for row in range(4):
            hot = species_hot(pairs[slots[tile][0]][slots[tile][1], row][3:4])
            start = jnp.dot(hot, table, preferred_element_type=F32) * 0.0625
            start_ref[tile, row] = start.astype(BF16)
    scale = [folded(weights, which) for which in range(2)]

    def body(block, carry):
        fill_kernels(send_ref, recv_ref, kern_ref, block)
        rhs = jnp.concatenate(
            [start_ref[tile, block + near] for tile in range(3) for near in range(3)], axis=0
        )
        scalar = weighted_sum(kern_ref, 0, rhs, scale[0])
        invariant = scalar
        for d in range(3):
            vector = weighted_sum(kern_ref, d + 1, rhs, scale[1])
            vector_out[block, d] = vector
            invariant = invariant + vector * vector
            mixed = jnp.dot(vector.astype(BF16), mixv[...], preferred_element_type=F32)
            feat_out[block, (d + 1) * LENGTH : (d + 2) * LENGTH, :] = mixed.astype(BF16)
        hidden = jnp.dot(invariant.astype(BF16), mix[...], preferred_element_type=F32)
        hidden_out[block] = hidden
        start = start_ref[1, block + 1].astype(F32)
        feat_out[block, :LENGTH, :] = (start + silu_pair(hidden)[0]).astype(BF16)
        return carry

    lax.fori_loop(0, 2, body, 0)


def second_kernel(
    flag, even, odd, feat_even, feat_mine, feat_odd, weights, out_weight, read, energy_out,
    pull_out, send_ref, recv_ref, kern_ref,
):
    slots, turns = slots_of(flag)
    feats = (feat_even, feat_mine, feat_odd)
    place_atoms((even, odd), slots, turns, send_ref, recv_ref)
    mine = slots[1][1]
    scale = [folded(weights, which) for which in range(2)]

    def body(block, carry):
        fill_kernels(send_ref, recv_ref, kern_ref, block)
        message = weighted_sum(kern_ref, 0, nearby(feats, OWN_SLOTS, block, 0, LENGTH), scale[0])
        for d in range(3):
            rhs = nearby(feats, OWN_SLOTS, block, (d + 1) * LENGTH, LENGTH)
            message = message + weighted_sum(kern_ref, d + 1, rhs, scale[1])
        own = feat_mine[0, block + 1, :LENGTH, :].astype(F32)
        combined = (own + message).astype(BF16)
        hidden = jnp.dot(combined, out_weight[...], preferred_element_type=F32)
        value, slope = silu_pair(hidden)
        present = species_column(even[mine, block + 1][3:4]) > -0.5
        energy = jnp.where(present, jnp.sum(value * read[...], axis=1, keepdims=True), 0.0)
        energy_out[block] = jnp.transpose(jnp.broadcast_to(energy, (LENGTH, LENGTH)))[:1]
        back = jnp.where(present, slope * read[...], 0.0).astype(BF16)
        pull_out[block] = turned_dot(back, out_weight[...]).astype(BF16)
        return carry

    lax.fori_loop(0, 2, body, 0)


def third_kernel(
    flag, even, odd, feat_even, feat_mine, feat_odd, pull_even, pull_odd, hidden, vectors,
    energies, embedding, weights_one, weights_two, mix, mixv, force_out,
    send_ref, recv_ref, kern_ref, hot_ref, lhs_ref, deriv_ref, row_ref,
):
    pairs = (even, odd)
    feats = (feat_even, feat_mine, feat_odd)
    pulls = (pull_even, pull_odd)
    slots, turns = slots_of(flag)
    mine = slots[1][1]
    place_atoms(pairs, slots, turns, send_ref, recv_ref)
    for tile in range(3):
        for row in range(4):
            hot_ref[tile, row] = species_hot(pairs[slots[tile][0]][slots[tile][1], row][3:4])
    scale_one = [folded(weights_one, which) for which in range(2)]
    scale_two = [folded(weights_two, which) for which in range(2)]
    table = species_rows(embedding)
    force_out[...] = jnp.zeros(force_out.shape, F32)
    depth = BASIS * LENGTH

    def body(block, carry):
        fill_kernels(send_ref, recv_ref, kern_ref, block)
        force_out[1, block + 1, 3:4, :] = energies[block]
        rhs = nearby(pulls, slots, block, 0, LENGTH)
        pull = pull_even[mine, block + 1].astype(F32)
        scalar_grad = pull + weighted_sum(kern_ref, 0, rhs, scale_two[0])
        scalar_grad = scalar_grad.astype(BF16).astype(F32)
        hidden_grad = (scalar_grad * silu_pair(hidden[block])[1]).astype(BF16)
        inv_grad = turned_dot(hidden_grad, mix[...])
        inv_grad = inv_grad.astype(BF16).astype(F32)
        grads = [inv_grad]
        for d in range(3):
            vector_grad = -weighted_sum(kern_ref, d + 1, rhs, scale_two[1])
            passed = turned_dot(vector_grad.astype(BF16), mixv[...])
            passed = passed.astype(BF16).astype(F32)
            grads.append(passed + 2.0 * vectors[block, d] * inv_grad)
        lane_basis = lax.broadcasted_iota(jnp.int32, (LENGTH, LENGTH), 1) >> 3
        for r in range(4):
            which = min(r, 1)
            spread = jnp.concatenate(
                [table * scale_one[which][b : b + 1, :] for b in range(BASIS)]
                + [jnp.zeros((LENGTH - 8 * BASIS, LENGTH), F32)],
                axis=0,
            )
            table_grad = turned_dot(grads[r], spread, precision=lax.Precision.HIGHEST)
            for b in range(BASIS):
                at = r * depth + b * LENGTH
                scaled = pull * scale_two[which][b : b + 1, :]
                lhs_ref[at : at + LENGTH, :LENGTH] = scaled.astype(BF16)
                lhs_ref[at : at + LENGTH, LENGTH:] = jnp.where(
                    lane_basis == b, table_grad, 0.0
                ).astype(BF16)
        row_ref[...] = jnp.zeros(row_ref.shape, F32)
        rows = 16
        for tile in range(3):
            for near in range(3):
                for r in range(4):
                    sender = jnp.concatenate(
                        [
                            feats[tile][0, block + near, r * LENGTH : (r + 1) * LENGTH, :],
                            hot_ref[tile, block + near],
                        ],
                        axis=1,
                    )
                    deriv_ref[r * depth : (r + 1) * depth, :] = turned_dot(
                        lhs_ref[r * depth : (r + 1) * depth, :], sender
                    )
                cell = (block + near) * 3 + tile

                def chain(step, columns):
                    first = pl.multiple_of(step * rows, rows)
                    apart, eight, centred, gauss, ratio, rest = pair_geometry(
                        send_ref, recv_ref, block, cell, first, rows
                    )
                    if tile == 1 and near == 1:
                        own = first + lax.broadcasted_iota(jnp.int32, (rows, LENGTH), 0)
                        other = lax.broadcasted_iota(jnp.int32, (rows, LENGTH), 1)
                        rest = jnp.where(own == other, 0.0, rest)
                    along = [None, None, None]
                    value = None
                    slope = None
                    for b in range(BASIS - 1, -1, -1):
                        parts = [
                            deriv_ref[pl.ds(r * depth + b * LENGTH + first, rows), :]
                            for r in range(4)
                        ]
                        joint = parts[0]
                        for d in range(3):
                            joint = joint + apart[d] * parts[d + 1]
                            along[d] = (
                                parts[d + 1]
                                if along[d] is None
                                else along[d] * ratio + parts[d + 1]
                            )
                        if value is None:
                            value = joint
                        else:
                            slope = value if slope is None else slope * ratio + value
                            value = value * ratio + joint
                    slope = slope * ratio
                    scale = gauss * rest
                    radial = (
                        scale * (8.0 * rest * (slope - centred * value) - 2.0 * value)
                    ) * (2.0 * INV_CUTOFF)
                    envelope = scale * rest * INV_CUTOFF
                    out = []
                    for d in range(3):
                        pushed = envelope * along[d] + radial * apart[d]
                        row_ref[d, pl.ds(first, rows), :] = (
                            row_ref[d, pl.ds(first, rows), :] + pushed
                        )
                        out.append(columns[d] + pushed)
                    return tuple(out)

                zero = jnp.zeros((rows, LENGTH), F32)
                columns = lax.fori_loop(0, LENGTH // rows, chain, (zero, zero, zero))
                for d in range(3):
                    force_out[tile, block + near, d : d + 1, :] = force_out[
                        tile, block + near, d : d + 1, :
                    ] - jnp.sum(columns[d], axis=0, keepdims=True)
        for d in range(3):
            total = jnp.sum(jnp.transpose(row_ref[d]), axis=0, keepdims=True)
            force_out[1, block + 1, d : d + 1, :] = (
                force_out[1, block + 1, d : d + 1, :] + total
            )
        return carry

    lax.fori_loop(0, 2, body, 0)


AXES = ("slab", "tile")


class Grid:
    def __init__(self, slabs, tiles):
        self.slabs, self.tiles = slabs, tiles
        self.moved = (slabs, tiles) == (16, 32)
        self.cycle = [(x, y) for y in range(4) for x in ((1, 2, 3) if y % 2 == 0 else (3, 2, 1))]
        self.cycle += [(0, y) for y in (3, 2, 1, 0)]

    def device(self, slab, tile):
        slab, tile = slab % self.slabs, tile % self.tiles
        if self.moved:
            x, y = self.cycle[slab]
            z, core = tile // 2, (tile // 2 + tile) % 2
            slab, tile = x * 4 + z % 4, ((z // 4) * 4 + y) * 2 + core
        return slab * self.tiles + tile

    def places(self):
        return [(slab, tile) for slab in range(self.slabs) for tile in range(self.tiles)]

    def flag(self):
        odd = lax.axis_index("tile")
        if self.moved:
            odd = odd + lax.axis_index("slab")
        return (1 - odd % 2).astype(jnp.int32)

    def to_work(self, block):
        if not self.moved:
            return block
        route = [(s * self.tiles + t, self.device(s, t)) for s, t in self.places()]
        return lax.ppermute(block, AXES, route)

    def to_owner(self, block):
        if not self.moved:
            return block
        route = [(self.device(s, t), s * self.tiles + t) for s, t in self.places()]
        return lax.ppermute(block, AXES, route)

    def along_slab(self, block, step):
        route = [(self.device(s, t), self.device(s + step, t)) for s, t in self.places()]
        return lax.ppermute(block, AXES, route)

    def with_partner(self, block, odd):
        groups = [
            [self.device(s, t + odd), self.device(s, t + odd + 1)]
            for s, t in self.places()
            if t % 2 == 0
        ]
        return lax.all_gather(block, AXES, axis_index_groups=groups)

    def swap(self, block, odd):
        route = []
        for s, t in self.places():
            if t % 2 == 0:
                ends = self.device(s, t + odd), self.device(s, t + odd + 1)
                route += [ends, ends[::-1]]
        return lax.ppermute(block, AXES, route)

    def column(self, cells):
        above = self.along_slab(cells[1:], 1)
        below = self.along_slab(cells[:1], -1)
        return jnp.concatenate([above, cells, below], axis=0)

    def gather_near(self, cells):
        column = self.column(cells)
        return self.with_partner(column, 0), self.with_partner(column, 1)

    def swap_near(self, cells):
        column = self.column(cells)[None]
        return self.swap(column, 0), column, self.swap(column, 1)

    def send_home(self, parts, flag):
        even = self.with_partner(parts[0], 0)
        odd = self.with_partner(parts[2], 1)
        column = (
            parts[1]
            + lax.dynamic_index_in_dim(even, flag, 0, False)
            + lax.dynamic_index_in_dim(odd, 1 - flag, 0, False)
        )
        from_next = self.along_slab(column[:1], -1)
        from_last = self.along_slab(column[3:], 1)
        return column[1:3] + jnp.concatenate([from_last, from_next], axis=0)


def kernel_call(body, outs, scratch, flops, operands):
    in_specs = [pl.BlockSpec(memory_space=pltpu.SMEM)]
    in_specs += [pl.BlockSpec(memory_space=pltpu.VMEM)] * (operands - 1)
    return pl.pallas_call(
        body,
        out_shape=[jax.ShapeDtypeStruct(shape, kind) for shape, kind in outs],
        in_specs=in_specs,
        out_specs=[pl.BlockSpec(memory_space=pltpu.VMEM)] * len(outs),
        scratch_shapes=[pltpu.VMEM(shape, kind) for shape, kind in scratch],
        compiler_params=pltpu.CompilerParams(vmem_limit_bytes=VMEM_LIMIT),
        cost_estimate=pl.CostEstimate(flops=flops, bytes_accessed=1 << 20, transcendentals=0),
    )


GEOMETRY = [
    ((12, 3, LENGTH), F32),
    ((2, 3, LENGTH, LENGTH), F32),
    ((4 * BASIS * LENGTH, NEAR * LENGTH), BF16),
]


def first_call():
    outs = [
        ((2, 4 * LENGTH, LENGTH), BF16),
        ((2, LENGTH, LENGTH), F32),
        ((2, 3, LENGTH, LENGTH), F32),
    ]
    scratch = GEOMETRY + [((3, 4, LENGTH, LENGTH), BF16)]
    return kernel_call(first_kernel, outs, scratch, 2400000000, 7)


def second_call():
    outs = [((2, 1, LENGTH), F32), ((2, LENGTH, LENGTH), BF16)]
    return kernel_call(second_kernel, outs, GEOMETRY, 2400000000, 9)


def third_call():
    scratch = GEOMETRY + [
        ((3, 4, LENGTH, LENGTH), BF16),
        ((4 * BASIS * LENGTH, 2 * LENGTH), BF16),
        ((4 * BASIS * LENGTH, LENGTH), F32),
        ((3, LENGTH, LENGTH), F32),
    ]
    return kernel_call(third_kernel, [((3, 4, 4, LENGTH), F32)], scratch, 7200000000, 16)


def on_device(
    grid, positions, species, occupied, embedding, first_radial_weight, radial_two, mix_scalar,
    vector_channel_weight, out_weight, read_weight,
):
    codes = jnp.where(occupied > 0, species, -1).astype(F32)
    packet = jnp.concatenate([positions, codes[:, :, None]], axis=2)[:, 0]
    flag = grid.flag()
    places = (flag[None], *grid.gather_near(grid.to_work(packet)))
    features, hidden, vectors = first_call()(
        *places, embedding, first_radial_weight, mix_scalar, vector_channel_weight
    )
    near_features = grid.swap_near(features)
    energies, pull = second_call()(
        *places, *near_features, radial_two, out_weight, read_weight[None, :]
    )
    near_pulls = grid.gather_near(pull)
    (parts,) = third_call()(
        *places, *near_features, *near_pulls, hidden, vectors, energies, embedding,
        first_radial_weight, radial_two, mix_scalar, vector_channel_weight,
    )
    final = grid.to_owner(grid.send_home(parts, flag))
    return final[:, 3:], final[:, None, :3]


def solution(mesh):
    grid = Grid(mesh.shape["slab"], mesh.shape["tile"])
    in_specs = (
        P("slab", "tile", None, None),
        P("slab", "tile", None),
        P("slab", "tile", None),
        P(),
        P(),
        P(),
        P(),
        P(),
        P(),
        P(),
    )
    out_specs = (P("slab", "tile", None), P("slab", "tile", None, None))
    return jax.shard_map(
        functools.partial(on_device, grid), mesh=mesh, in_specs=in_specs, out_specs=out_specs, check_vma=False
    )
```

time: 211 us -> 163 us (0.77)
  the two profiles are of different devices: /device:TPU:102 before, /device:TPU:24 now
where the time goes in v2:
time: 163 us; the launch traced here: 161 us
  Pallas kernels  60 us (37%)
  starting transfers between devices  44.1 us (27%)
  blocking collectives  28.8 us (18%)
  waiting for transfers between devices  24.8 us (15%)
  local copies, waits for them, and re-layouts  2.66 us (2%)
    pallas_call x1, Pallas kernels, on_device(): third_call()  36.9 us
    all_gather x6, blocking collectives, with_partner(): return lax.all_gather(block, AXES, axis_index_groups=groups)  28.8 us
    ppermute x8, starting transfers between devices, along_slab(): return lax.ppermute(block, AXES, route)  24.3 us
    pallas_call x1, Pallas kernels, on_device(): first_call()  12.7 us
    ppermute x8, waiting for transfers between devices, along_slab(): return lax.ppermute(block, AXES, route)  11.8 us
    pallas_call x1, Pallas kernels, on_device(): second_call()  10.4 us
    ppermute x2, waiting for transfers between devices, swap(): return lax.ppermute(block, AXES, route)  7.14 us
    ppermute x2, starting transfers between devices, swap(): return lax.ppermute(block, AXES, route)  7.09 us
  transfers between devices with their start and end apart: 12, of which 8 were waited for; matrix products, arithmetic and copies ran while one was open for 0% of the time, Pallas kernels for 0%

profile of v2, /device:TPU:24, one launch (start us, length us, event | category | flops | bytes accessed | tf_op | source)
XLA Modules:
  0.0 161.4 jit_solution(4557529339737768944)
XLA Ops:
  0.6 0.7 copy.16
  1.3 0.7 copy-done.8
  2.0 6.6 %collective-permute-start = (f32[2,4,128]{2,1,0:T(4,128)S(1)}, f32[2,4,128]{2,1,0:T(4,128)S(1)}, u32[]{:S(2)}, u32[]{:S(2)}) collective-permute-start(f32[2,4,128]{2,1,0:T(4,128)S(1)} %maximum_bitcast_fusion.1), channel_id=1, source_target_pairs={{0,128},{1,129},{2,161},{3,160},{4,192},{5,193},{6,225},{7,224},{8... | collective-permute-start | bytes 12296 | tf_op jit(solution)/shard_map/ppermute | solution.py:373
  8.6 2.3 %collective-permute-done = f32[2,4,128]{2,1,0:T(4,128)S(1)} collective-permute-done((f32[2,4,128]{2,1,0:T(4,128)S(1)}, f32[2,4,128]{2,1,0:T(4,128)S(1)}, u32[]{:S(2)}, u32[]{:S(2)}) %collective-permute-start) | collective-permute-done | bytes 4128 | tf_op jit(solution)/shard_map/ppermute | solution.py:373
  10.9 3.8 %collective-permute-start.1 = (f32[1,4,128]{2,1,0:T(4,128)S(1)}, f32[1,4,128]{2,1,0:T(4,128)S(1)}, u32[]{:S(2)}, u32[]{:S(2)}) collective-permute-start(f32[1,4,128]{2,1,0:T(4,128)S(1)} %get-tuple-element.25), channel_id=1, source_target_pairs={{128,256},{129,257},{161,289},{160,288},{192,320},{193,321},{225,3... | collective-permute-start | bytes 6152 | tf_op jit(solution)/shard_map/ppermute | solution.py:383
  14.7 3.0 %collective-permute-start.2 = (f32[1,4,128]{2,1,0:T(4,128)S(1)}, f32[1,4,128]{2,1,0:T(4,128)S(1)}, u32[]{:S(2)}, u32[]{:S(2)}) collective-permute-start(f32[1,4,128]{2,1,0:T(4,128)S(1)} %get-tuple-element.24), channel_id=1, source_target_pairs={{128,0},{129,1},{161,33},{160,32},{192,64},{193,65},{225,97},{224,... | collective-permute-start | bytes 6152 | tf_op jit(solution)/shard_map/ppermute | solution.py:383
  17.8 2.5 %collective-permute-done.2 = f32[1,4,128]{2,1,0:T(4,128)S(1)} collective-permute-done((f32[1,4,128]{2,1,0:T(4,128)S(1)}, f32[1,4,128]{2,1,0:T(4,128)S(1)}, u32[]{:S(2)}, u32[]{:S(2)}) %collective-permute-start.2) | collective-permute-done | bytes 2080 | tf_op jit(solution)/shard_map/ppermute | solution.py:383
  20.2 1.8 %all-gather = f32[8,4,128]{2,1,0:T(4,128)S(1)} all-gather(f32[4,4,128]{2,1,0:T(4,128)S(1)} %constant_dynamic-update-slice_fusion), channel_id=2, replica_groups={{128,129},{161,160},{192,193},{225,224},{136,137},{169,168},{200,201},{..., dimensions={0}, use_global_device_ids=true | all-gather | bytes 24576 | tf_op jit(solution)/shard_map/all_gather | solution.py:391
  22.0 10.6 %all-gather.1 = f32[8,4,128]{2,1,0:T(4,128)S(1)} all-gather(f32[4,4,128]{2,1,0:T(4,128)S(1)} %constant_dynamic-update-slice_fusion), channel_id=3, replica_groups={{129,161},{160,192},{193,225},{224,136},{137,169},{168,200},{201,233},{..., dimensions={0}, use_global_device_ids=true | all-gather | bytes 24576 | tf_op jit(solution)/shard_map/all_gather | solution.py:391
  32.7 12.7 %shard_map.113 = (bf16[2,512,128]{2,1,0:T(8,128)(2,1)S(1)}, f32[2,128,128]{2,1,0:T(8,128)S(1)}, f32[2,3,128,128]{3,2,1,0:T(8,128)S(1)}) custom-call(s32[1]{0:T(128)} %bitcast.flag, f32[2,4,4,128]{3,2,1,0:T(4,128)S(1)} %bitcast.25, f32[2,4,4,128]{3,2,1,0:T(4,128)S(1)} %bitcast.28, bf16[6,128]{1,0:T(8,128)(2,1)S(1)} %copy-done.5, f32[2,8,128]{2,1,0:T(8,128)S(1)} %copy-done.3, ...), custom_call_target="tpu_custom_call" | custom-call | flops 2400000000 | bytes 1048576 | tf_op jit(solution)/shard_map/pallas_call | solution.py:481
  45.4 3.0 %collective-permute-start.3 = (bf16[1,512,128]{2,1,0:T(8,128)(2,1)S(1)}, bf16[1,512,128]{2,1,0:T(8,128)(2,1)S(1)}, u32[]{:S(2)}, u32[]{:S(2)}) collective-permute-start(bf16[1,512,128]{2,1,0:T(8,128)(2,1)S(1)} %get-tuple-element.16), channel_id=1, source_target_pairs={{128,256},{129,257},{161,289},{160,288},{192,320},{193,321},{225,3... | collective-permute-start | bytes 393224 | tf_op jit(solution)/shard_map/ppermute | solution.py:383
  48.4 2.9 %collective-permute-start.4 = (bf16[1,512,128]{2,1,0:T(8,128)(2,1)S(1)}, bf16[1,512,128]{2,1,0:T(8,128)(2,1)S(1)}, u32[]{:S(2)}, u32[]{:S(2)}) collective-permute-start(bf16[1,512,128]{2,1,0:T(8,128)(2,1)S(1)} %get-tuple-element.17), channel_id=1, source_target_pairs={{128,0},{129,1},{161,33},{160,32},{192,64},{193,65},{225,97},{224,... | collective-permute-start | bytes 393224 | tf_op jit(solution)/shard_map/ppermute | solution.py:383
  51.3 1.0 collective-permute-done.3
  52.3 3.0 %collective-permute-done.4 = bf16[1,512,128]{2,1,0:T(8,128)(2,1)S(1)} collective-permute-done((bf16[1,512,128]{2,1,0:T(8,128)(2,1)S(1)}, bf16[1,512,128]{2,1,0:T(8,128)(2,1)S(1)}, u32[]{:S(2)}, u32[]{:S(2)}) %collective-permute-start.4) | collective-permute-done | bytes 131104 | tf_op jit(solution)/shard_map/ppermute | solution.py:383
  55.3 1.9 %collective-permute-start.5 = (bf16[1,4,512,128]{3,2,1,0:T(8,128)(2,1)S(1)}, bf16[1,4,512,128]{3,2,1,0:T(8,128)(2,1)S(1)}, u32[]{:S(2)}, u32[]{:S(2)}) collective-permute-start(bf16[1,4,512,128]{3,2,1,0:T(8,128)(2,1)S(1)} %maximum_bitcast_fusion.feat_mine), channel_id=1, source_target_pairs={{128,129},{129,128},{161,160},{160,161},{192,193},{193,192},{225,2... | collective-permute-start | bytes 1572872 | tf_op jit(solution)/shard_map/ppermute | solution.py:399
  57.3 5.2 %collective-permute-start.6 = (bf16[1,4,512,128]{3,2,1,0:T(8,128)(2,1)S(1)}, bf16[1,4,512,128]{3,2,1,0:T(8,128)(2,1)S(1)}, u32[]{:S(2)}, u32[]{:S(2)}) collective-permute-start(bf16[1,4,512,128]{3,2,1,0:T(8,128)(2,1)S(1)} %maximum_bitcast_fusion.feat_mine), channel_id=1, source_target_pairs={{129,161},{161,129},{160,192},{192,160},{193,225},{225,193},{224,1... | collective-permute-start | bytes 1572872 | tf_op jit(solution)/shard_map/ppermute | solution.py:399
  62.5 7.1 %collective-permute-done.6.feat_odd = bf16[1,4,512,128]{3,2,1,0:T(8,128)(2,1)S(1)} collective-permute-done((bf16[1,4,512,128]{3,2,1,0:T(8,128)(2,1)S(1)}, bf16[1,4,512,128]{3,2,1,0:T(8,128)(2,1)S(1)}, u32[]{:S(2)}, u32[]{:S(2)}) %collective-permute-start.6) | collective-permute-done | bytes 524320 | tf_op jit(solution)/shard_map/ppermute | solution.py:399
  69.6 10.4 %shard_map.114 = (f32[2,1,128]{2,1,0:T(1,128)S(1)}, bf16[2,128,128]{2,1,0:T(8,128)(2,1)S(1)}) custom-call(s32[1]{0:T(128)} %bitcast.flag, f32[2,4,4,128]{3,2,1,0:T(4,128)S(1)} %bitcast.26, f32[2,4,4,128]{3,2,1,0:T(4,128)S(1)} %bitcast.29, bf16[1,4,512,128]{3,2,1,0:T(8,128)(2,1)S(1)} %collective-permute-done.5.feat_even, ...), custom_call_target="tpu_custom_call" | custom-call | flops 2400000000 | bytes 1048576 | tf_op jit(solution)/shard_map/pallas_call | solution.py:485
  80.0 2.2 %collective-permute-start.7 = (bf16[1,128,128]{2,1,0:T(8,128)(2,1)S(1)}, bf16[1,128,128]{2,1,0:T(8,128)(2,1)S(1)}, u32[]{:S(2)}, u32[]{:S(2)}) collective-permute-start(bf16[1,128,128]{2,1,0:T(8,128)(2,1)S(1)} %get-tuple-element.19), channel_id=1, source_target_pairs={{128,256},{129,257},{161,289},{160,288},{192,320},{193,321},{225,3... | collective-permute-start | bytes 98312 | tf_op jit(solution)/shard_map/ppermute | solution.py:383
  82.2 3.6 %collective-permute-start.8 = (bf16[1,128,128]{2,1,0:T(8,128)(2,1)S(1)}, bf16[1,128,128]{2,1,0:T(8,128)(2,1)S(1)}, u32[]{:S(2)}, u32[]{:S(2)}) collective-permute-start(bf16[1,128,128]{2,1,0:T(8,128)(2,1)S(1)} %get-tuple-element.18), channel_id=1, source_target_pairs={{128,0},{129,1},{161,33},{160,32},{192,64},{193,65},{225,97},{224,... | collective-permute-start | bytes 98312 | tf_op jit(solution)/shard_map/ppermute | solution.py:383
  85.9 2.1 %collective-permute-done.8 = bf16[1,128,128]{2,1,0:T(8,128)(2,1)S(1)} collective-permute-done((bf16[1,128,128]{2,1,0:T(8,128)(2,1)S(1)}, bf16[1,128,128]{2,1,0:T(8,128)(2,1)S(1)}, u32[]{:S(2)}, u32[]{:S(2)}) %collective-permute-start.8) | collective-permute-done | bytes 32800 | tf_op jit(solution)/shard_map/ppermute | solution.py:383
  88.1 6.8 %all-gather.3 = bf16[8,128,128]{2,1,0:T(8,128)(2,1)S(1)} all-gather(bf16[4,128,128]{2,1,0:T(8,128)(2,1)S(1)} %constant_dynamic-update-slice_fusion.3), channel_id=5, replica_groups={{129,161},{160,192},{193,225},{224,136},{137,169},{168,200},{201,233},{..., dimensions={0}, use_global_device_ids=true | all-gather | bytes 393216 | tf_op jit(solution)/shard_map/all_gather | solution.py:391
  94.9 2.2 %all-gather.2 = bf16[8,128,128]{2,1,0:T(8,128)(2,1)S(1)} all-gather(bf16[4,128,128]{2,1,0:T(8,128)(2,1)S(1)} %constant_dynamic-update-slice_fusion.3), channel_id=4, replica_groups={{128,129},{161,160},{192,193},{225,224},{136,137},{169,168},{200,201},{..., dimensions={0}, use_global_device_ids=true | all-gather | bytes 393216 | tf_op jit(solution)/shard_map/all_gather | solution.py:391
  97.1 36.9 %shard_map.115 = f32[3,4,4,128]{3,2,1,0:T(4,128)S(1)} custom-call(s32[1]{0:T(128)} %bitcast.flag, f32[2,4,4,128]{3,2,1,0:T(4,128)S(1)} %bitcast.27, f32[2,4,4,128]{3,2,1,0:T(4,128)S(1)} %bitcast.30, bf16[1,4,512,128]{3,2,1,0:T(8,128)(2,1)S(1)} %collective-permute-done.5.feat_even, bf16[1,4,512,128]{3,2,1,0:T(8,128)(2,1)S(1)} %maximum_bitcast_fusion.feat_mine, ...), custom_call_target="tpu_custom_call" | custom-call | flops 7200000000 | bytes 1048576 | tf_op jit(solution)/shard_map/pallas_call | solution.py:489
  134.0 1.8 %all_gather.32 = f32[2,4,4,128]{3,2,1,0:T(4,128)S(1)} all-gather(f32[1,4,4,128]{3,2,1,0:T(4,128)S(1)} %get-tuple-element.20), channel_id=1, replica_groups={{128,129},{161,160},{192,193},{225,224},{136,137},{169,168},{200,201},{..., dimensions={0}, use_global_device_ids=true | all-gather | bytes 24576 | tf_op jit(solution)/shard_map/all_gather | solution.py:391
  135.8 5.6 %all_gather.33 = f32[2,4,4,128]{3,2,1,0:T(4,128)S(1)} all-gather(f32[1,4,4,128]{3,2,1,0:T(4,128)S(1)} %get-tuple-element.21), channel_id=1, replica_groups={{129,161},{160,192},{193,225},{224,136},{137,169},{168,200},{201,233},{..., dimensions={0}, use_global_device_ids=true | all-gather | bytes 24576 | tf_op jit(solution)/shard_map/all_gather | solution.py:391
  141.4 3.6 %collective-permute-start.10 = (f32[1,4,128]{2,1,0:T(4,128)S(1)}, f32[1,4,128]{2,1,0:T(4,128)S(1)}, u32[]{:S(2)}, u32[]{:S(2)}) collective-permute-start(f32[1,4,128]{2,1,0:T(4,128)S(1)} %get-tuple-element.23), channel_id=1, source_target_pairs={{128,0},{129,1},{161,33},{160,32},{192,64},{193,65},{225,97},{224,... | collective-permute-start | bytes 6152 | tf_op jit(solution)/shard_map/ppermute | solution.py:383
  145.0 2.2 %collective-permute-start.9 = (f32[1,4,128]{2,1,0:T(4,128)S(1)}, f32[1,4,128]{2,1,0:T(4,128)S(1)}, u32[]{:S(2)}, u32[]{:S(2)}) collective-permute-start(f32[1,4,128]{2,1,0:T(4,128)S(1)} %get-tuple-element.22), channel_id=1, source_target_pairs={{128,256},{129,257},{161,289},{160,288},{192,320},{193,321},{225,3... | collective-permute-start | bytes 6152 | tf_op jit(solution)/shard_map/ppermute | solution.py:383
  147.3 3.2 %collective-permute-done.9 = f32[1,4,128]{2,1,0:T(4,128)S(1)} collective-permute-done((f32[1,4,128]{2,1,0:T(4,128)S(1)}, f32[1,4,128]{2,1,0:T(4,128)S(1)}, u32[]{:S(2)}, u32[]{:S(2)}) %collective-permute-start.9) | collective-permute-done | bytes 2080 | tf_op jit(solution)/shard_map/ppermute | solution.py:383
  150.5 6.1 %collective-permute-start.11 = (f32[2,4,128]{2,1,0:T(4,128)S(1)}, f32[2,4,128]{2,1,0:T(4,128)S(1)}, u32[]{:S(2)}, u32[]{:S(2)}) collective-permute-start(f32[2,4,128]{2,1,0:T(4,128)S(1)} %fusion.1), channel_id=1, source_target_pairs={{128,0},{129,1},{161,2},{160,3},{192,4},{193,5},{225,6},{224,7},{1... | collective-permute-start | bytes 12296 | tf_op jit(solution)/shard_map/ppermute | solution.py:379
  156.6 3.6 %collective-permute-done.11 = f32[2,4,128]{2,1,0:T(4,128)S(1)} collective-permute-done((f32[2,4,128]{2,1,0:T(4,128)S(1)}, f32[2,4,128]{2,1,0:T(4,128)S(1)}, u32[]{:S(2)}, u32[]{:S(2)}) %collective-permute-start.11) | collective-permute-done | bytes 4128 | tf_op jit(solution)/shard_map/ppermute | solution.py:379
  160.2 0.6 copy.17
  (39 shorter events, 0.8 us)
Async XLA Ops:
  1.3 0.7 copy-start.8
  1.3 0.7 copy-start.7
  2.0 8.8 %collective-permute-start = (f32[2,4,128]{2,1,0:T(4,128)S(1)}, f32[2,4,128]{2,1,0:T(4,128)S(1)}, u32[]{:S(2)}, u32[]{:S(2)}) collective-permute-start(f32[2,4,128]{2,1,0:T(4,128)S(1)} %maximum_bitcast_fusion.1), channel_id=1, source_target_pairs={{0,128},{1,129},{2,161},{3,160},{4,192},{5,193},{6,225},{7,224},{8... | collective-permute-start | bytes 12296 | tf_op jit(solution)/shard_map/ppermute | solution.py:373
  10.9 6.9 %collective-permute-start.1 = (f32[1,4,128]{2,1,0:T(4,128)S(1)}, f32[1,4,128]{2,1,0:T(4,128)S(1)}, u32[]{:S(2)}, u32[]{:S(2)}) collective-permute-start(f32[1,4,128]{2,1,0:T(4,128)S(1)} %get-tuple-element.25), channel_id=1, source_target_pairs={{128,256},{129,257},{161,289},{160,288},{192,320},{193,321},{225,3... | collective-permute-start | bytes 6152 | tf_op jit(solution)/shard_map/ppermute | solution.py:383
  14.7 18.0 %copy-start.5 = (bf16[6,128]{1,0:T(8,128)(2,1)S(1)}, bf16[6,128]{1,0:T(8,128)(2,1)}, u32[]{:S(2)}) copy-start(bf16[6,128]{1,0:T(8,128)(2,1)} %embedding.3) | copy-start | bytes 4612
  14.7 18.0 %copy-start.3 = (f32[2,8,128]{2,1,0:T(8,128)S(1)}, f32[2,8,128]{2,1,0:T(8,128)}, u32[]{:S(2)}) copy-start(f32[2,8,128]{2,1,0:T(8,128)} %weights_one.1) | copy-start | bytes 24580
  14.7 5.5 %collective-permute-start.2 = (f32[1,4,128]{2,1,0:T(4,128)S(1)}, f32[1,4,128]{2,1,0:T(4,128)S(1)}, u32[]{:S(2)}, u32[]{:S(2)}) collective-permute-start(f32[1,4,128]{2,1,0:T(4,128)S(1)} %get-tuple-element.24), channel_id=1, source_target_pairs={{128,0},{129,1},{161,33},{160,32},{192,64},{193,65},{225,97},{224,... | collective-permute-start | bytes 6152 | tf_op jit(solution)/shard_map/ppermute | solution.py:383
  17.7 14.9 %copy-start.1 = (bf16[128,128]{1,0:T(8,128)(2,1)S(1)}, bf16[128,128]{1,0:T(8,128)(2,1)}, u32[]{:S(2)}) copy-start(bf16[128,128]{1,0:T(8,128)(2,1)} %mix.3) | copy-start | bytes 98308
  17.7 14.9 %copy-start.2 = (bf16[128,128]{1,0:T(8,128)(2,1)S(1)}, bf16[128,128]{1,0:T(8,128)(2,1)}, u32[]{:S(2)}) copy-start(bf16[128,128]{1,0:T(8,128)(2,1)} %mixv.3) | copy-start | bytes 98308
  45.4 6.9 %collective-permute-start.3 = (bf16[1,512,128]{2,1,0:T(8,128)(2,1)S(1)}, bf16[1,512,128]{2,1,0:T(8,128)(2,1)S(1)}, u32[]{:S(2)}, u32[]{:S(2)}) collective-permute-start(bf16[1,512,128]{2,1,0:T(8,128)(2,1)S(1)} %get-tuple-element.16), channel_id=1, source_target_pairs={{128,256},{129,257},{161,289},{160,288},{192,320},{193,321},{225,3... | collective-permute-start | bytes 393224 | tf_op jit(solution)/shard_map/ppermute | solution.py:383
  48.4 21.2 %copy-start = (bf16[128,128]{1,0:T(8,128)(2,1)S(1)}, bf16[128,128]{1,0:T(8,128)(2,1)}, u32[]{:S(2)}) copy-start(bf16[128,128]{1,0:T(8,128)(2,1)} %out_weight.1) | copy-start | bytes 98308
  48.4 21.2 %copy-start.4 = (f32[2,8,128]{2,1,0:T(8,128)S(1)}, f32[2,8,128]{2,1,0:T(8,128)}, u32[]{:S(2)}) copy-start(f32[2,8,128]{2,1,0:T(8,128)} %weights_two.1) | copy-start | bytes 24580
  48.4 6.9 %collective-permute-start.4 = (bf16[1,512,128]{2,1,0:T(8,128)(2,1)S(1)}, bf16[1,512,128]{2,1,0:T(8,128)(2,1)S(1)}, u32[]{:S(2)}, u32[]{:S(2)}) collective-permute-start(bf16[1,512,128]{2,1,0:T(8,128)(2,1)S(1)} %get-tuple-element.17), channel_id=1, source_target_pairs={{128,0},{129,1},{161,33},{160,32},{192,64},{193,65},{225,97},{224,... | collective-permute-start | bytes 393224 | tf_op jit(solution)/shard_map/ppermute | solution.py:383
  55.3 14.3 %copy-start.6 = (f32[128]{0:T(128)S(1)}, f32[128]{0:T(128)}, u32[]{:S(2)}) copy-start(f32[128]{0:T(128)} %param.19) | copy-start | bytes 1540
  55.3 7.1 %collective-permute-start.5 = (bf16[1,4,512,128]{3,2,1,0:T(8,128)(2,1)S(1)}, bf16[1,4,512,128]{3,2,1,0:T(8,128)(2,1)S(1)}, u32[]{:S(2)}, u32[]{:S(2)}) collective-permute-start(bf16[1,4,512,128]{3,2,1,0:T(8,128)(2,1)S(1)} %maximum_bitcast_fusion.feat_mine), channel_id=1, source_target_pairs={{128,129},{129,128},{161,160},{160,161},{192,193},{193,192},{225,2... | collective-permute-start | bytes 1572872 | tf_op jit(solution)/shard_map/ppermute | solution.py:399
  57.3 12.3 %collective-permute-start.6 = (bf16[1,4,512,128]{3,2,1,0:T(8,128)(2,1)S(1)}, bf16[1,4,512,128]{3,2,1,0:T(8,128)(2,1)S(1)}, u32[]{:S(2)}, u32[]{:S(2)}) collective-permute-start(bf16[1,4,512,128]{3,2,1,0:T(8,128)(2,1)S(1)} %maximum_bitcast_fusion.feat_mine), channel_id=1, source_target_pairs={{129,161},{161,129},{160,192},{192,160},{193,225},{225,193},{224,1... | collective-permute-start | bytes 1572872 | tf_op jit(solution)/shard_map/ppermute | solution.py:399
  80.0 5.9 %collective-permute-start.7 = (bf16[1,128,128]{2,1,0:T(8,128)(2,1)S(1)}, bf16[1,128,128]{2,1,0:T(8,128)(2,1)S(1)}, u32[]{:S(2)}, u32[]{:S(2)}) collective-permute-start(bf16[1,128,128]{2,1,0:T(8,128)(2,1)S(1)} %get-tuple-element.19), channel_id=1, source_target_pairs={{128,256},{129,257},{161,289},{160,288},{192,320},{193,321},{225,3... | collective-permute-start | bytes 98312 | tf_op jit(solution)/shard_map/ppermute | solution.py:383
  82.2 5.8 %collective-permute-start.8 = (bf16[1,128,128]{2,1,0:T(8,128)(2,1)S(1)}, bf16[1,128,128]{2,1,0:T(8,128)(2,1)S(1)}, u32[]{:S(2)}, u32[]{:S(2)}) collective-permute-start(bf16[1,128,128]{2,1,0:T(8,128)(2,1)S(1)} %get-tuple-element.18), channel_id=1, source_target_pairs={{128,0},{129,1},{161,33},{160,32},{192,64},{193,65},{225,97},{224,... | collective-permute-start | bytes 98312 | tf_op jit(solution)/shard_map/ppermute | solution.py:383
  141.4 5.9 %collective-permute-start.10 = (f32[1,4,128]{2,1,0:T(4,128)S(1)}, f32[1,4,128]{2,1,0:T(4,128)S(1)}, u32[]{:S(2)}, u32[]{:S(2)}) collective-permute-start(f32[1,4,128]{2,1,0:T(4,128)S(1)} %get-tuple-element.23), channel_id=1, source_target_pairs={{128,0},{129,1},{161,33},{160,32},{192,64},{193,65},{225,97},{224,... | collective-permute-start | bytes 6152 | tf_op jit(solution)/shard_map/ppermute | solution.py:383
  145.0 5.5 %collective-permute-start.9 = (f32[1,4,128]{2,1,0:T(4,128)S(1)}, f32[1,4,128]{2,1,0:T(4,128)S(1)}, u32[]{:S(2)}, u32[]{:S(2)}) collective-permute-start(f32[1,4,128]{2,1,0:T(4,128)S(1)} %get-tuple-element.22), channel_id=1, source_target_pairs={{128,256},{129,257},{161,289},{160,288},{192,320},{193,321},{225,3... | collective-permute-start | bytes 6152 | tf_op jit(solution)/shard_map/ppermute | solution.py:383
  150.5 9.7 %collective-permute-start.11 = (f32[2,4,128]{2,1,0:T(4,128)S(1)}, f32[2,4,128]{2,1,0:T(4,128)S(1)}, u32[]{:S(2)}, u32[]{:S(2)}) collective-permute-start(f32[2,4,128]{2,1,0:T(4,128)S(1)} %fusion.1), channel_id=1, source_target_pairs={{128,0},{129,1},{161,2},{160,3},{192,4},{193,5},{225,6},{224,7},{1... | collective-permute-start | bytes 12296 | tf_op jit(solution)/shard_map/ppermute | solution.py:379

commit v3 on v2

v3 whole, which is shorter than its diff:
```python
import functools

import jax
import jax.numpy as jnp
from jax import lax
from jax.experimental import pallas as pl
from jax.experimental.pallas import tpu as pltpu
from jax.sharding import PartitionSpec as P

F32 = jnp.float32
BF16 = jnp.bfloat16
LENGTH = 128
BASIS = 8
NEAR = 9
FAR = 1000.0
INV_CUTOFF = 0.2
CELL_SLAB = 5.0
CELL_TILE = 10.0


def silu_pair(value):
    gate = 1.0 / (1.0 + jnp.exp(-value))
    return value * gate, gate * (1.0 + value * (1.0 - gate))


OWN_SLOTS = ((0, 0), (1, 0), (2, 0))


def slots_of(flag_ref):
    flag = flag_ref[0]
    turn = (2 * flag - 1).astype(F32) * CELL_TILE
    return ((0, flag), (0, 1 - flag), (1, 1 - flag)), (turn, 0.0, -turn)


def across_lanes(rows, count):
    turned = jnp.transpose(rows)
    return [jnp.broadcast_to(turned[:, k : k + 1], (LENGTH, LENGTH)) for k in range(count)]


def stacked(rows):
    filled = sum(row.shape[0] for row in rows)
    return jnp.concatenate(rows + [jnp.zeros((LENGTH - filled, LENGTH), F32)], axis=0)


def place_atoms(pairs, slots, turns, send_ref, recv_ref):
    rows = []
    for row in range(4):
        for tile in range(3):
            ref, member = pairs[slots[tile][0]], slots[tile][1]
            cell = ref[member, row]
            real = cell[3:4] > -0.5
            shift = ((row - 1) * CELL_SLAB, turns[tile], 0.0)
            for d in range(3):
                coords = cell[d : d + 1] + shift[d]
                rows.append(jnp.where(real, coords, -FAR) * INV_CUTOFF)
                if tile == 1 and row in (1, 2):
                    recv_ref[row - 1, d : d + 1, :] = jnp.where(real, coords, FAR) * INV_CUTOFF
    for k, column in enumerate(across_lanes(stacked(rows), 36)):
        send_ref[k // 3, k % 3] = column


def folded(weights, which):
    order = lax.broadcasted_iota(jnp.int32, (BASIS, LENGTH), 0).astype(F32)
    return weights[which] * jnp.exp(-0.5 * order * (order + 1.0))


def place_weights(weights, column_ref):
    rows = stacked([folded(weights, which) for which in range(2)])
    for k, column in enumerate(across_lanes(rows, 2 * BASIS)):
        column_ref[k] = column


def banked(bank):
    return bank.at[:LENGTH], bank.at[LENGTH : 2 * LENGTH], bank.at[2 * LENGTH :]


def species_rows(embedding):
    return embedding[...].astype(F32)[:8]


def species_hot(code_row):
    order = lax.broadcasted_iota(jnp.int32, (LENGTH, LENGTH), 0)
    species = (order & 7).astype(F32)
    return jnp.where(code_row == species, 1.0, 0.0).astype(BF16)


def plain_dot(lhs, rhs, **kinds):
    return jnp.dot(lhs, rhs, preferred_element_type=F32, **kinds)


def turned_dot(lhs, rhs):
    return lax.dot_general(lhs, rhs, (((0,), (0,)), ((), ())), preferred_element_type=F32)


def pair_geometry(send_ref, recv_ref, block, cell, first, rows, hidden_from):
    apart = [
        send_ref[cell, d, pl.ds(first, rows), :] - recv_ref[block, d : d + 1, :] for d in range(3)
    ]
    square = apart[0] * apart[0] + apart[1] * apart[1] + apart[2] * apart[2]
    square = jnp.minimum(square, 1.0)
    eight = 8.0 * square
    centred = eight - 0.5
    rest = 1.0 - square
    if hidden_from is not None:
        sender = first + lax.broadcasted_iota(jnp.int32, (rows, LENGTH), 0)
        receiver = hidden_from + lax.broadcasted_iota(jnp.int32, (rows, LENGTH), 1)
        rest = jnp.where(sender == receiver, 0.0, rest)
    return apart, centred, jnp.exp(-0.5 * centred * centred), jnp.exp(eight), rest


def fill_kernels(send_ref, recv_ref, kern_ref, block):
    rows = 16

    def body(step, carry):
        first = pl.multiple_of(step * rows, rows)
        for tile in range(3):
            for near in range(3):
                own = 0 if tile == 1 and near == 1 else None
                apart, _, gauss, ratio, rest = pair_geometry(
                    send_ref, recv_ref, block, (block + near) * 3 + tile, first, rows, own
                )
                value = gauss * (rest * rest)
                narrow = [a.astype(BF16) for a in apart]
                at = pl.ds(first + (tile * 3 + near) * LENGTH, rows)
                for b in range(BASIS):
                    radial = value.astype(BF16)
                    kern_ref[at, b * LENGTH : (b + 1) * LENGTH] = radial
                    for d in range(3):
                        column = ((d + 1) * BASIS + b) * LENGTH
                        kern_ref[at, column : column + LENGTH] = radial * narrow[d]
                    if b + 1 < BASIS:
                        value = value * ratio
        return carry

    lax.fori_loop(0, LENGTH // rows, body, 0)


def weighted_sum(kern_ref, part, lhs, column_ref):
    depth = BASIS * LENGTH
    product = plain_dot(lhs, kern_ref[:, part * depth : (part + 1) * depth])
    first = min(part, 1) * BASIS
    total = product[:, :LENGTH] * column_ref[first]
    for b in range(1, BASIS):
        total = total + product[:, b * LENGTH : (b + 1) * LENGTH] * column_ref[first + b]
    return total


def nearby(pairs, slots, block, lo):
    return jnp.concatenate(
        [
            pairs[which][member, block + near, lo : lo + LENGTH, :]
            for which, member in slots
            for near in range(3)
        ],
        axis=1,
    )


def first_kernel(
    flag, even, odd, bank, weights, feat_out, hidden_out, vector_out,
    kern_ref, send_ref, recv_ref, column_ref, start_ref,
):
    mix, mixv, embedding = banked(bank)
    pairs = (even, odd)
    slots, turns = slots_of(flag)
    place_atoms(pairs, slots, turns, send_ref, recv_ref)
    place_weights(weights, column_ref)
    table = jnp.concatenate([species_rows(embedding)] * 16, axis=0).astype(BF16)
    for tile in range(3):
        for row in range(4):
            hot = species_hot(pairs[slots[tile][0]][slots[tile][1], row][3:4])
            start_ref[tile, row] = (turned_dot(table, hot) * 0.0625).astype(BF16)

    def body(block, carry):
        fill_kernels(send_ref, recv_ref, kern_ref.at[block], block)
        lhs = jnp.concatenate(
            [start_ref[tile, block + near] for tile in range(3) for near in range(3)], axis=1
        )
        invariant = weighted_sum(kern_ref.at[block], 0, lhs, column_ref)
        for d in range(3):
            vector = weighted_sum(kern_ref.at[block], d + 1, lhs, column_ref)
            vector_out[block, d] = vector
            invariant = invariant + vector * vector
            mixed = turned_dot(mixv[...], vector.astype(BF16))
            feat_out[block, (d + 1) * LENGTH : (d + 2) * LENGTH, :] = mixed.astype(BF16)
        hidden = turned_dot(mix[...], invariant.astype(BF16))
        hidden_out[block] = hidden
        start = start_ref[1, block + 1].astype(F32)
        feat_out[block, :LENGTH, :] = (start + silu_pair(hidden)[0]).astype(BF16)
        return carry

    lax.fori_loop(0, 2, body, 0)


def second_kernel(
    flag, even, feat_even, feat_mine, feat_odd, kern_ref, weights, out_weight, read, energy_out,
    pull_out, column_ref,
):
    slots, _ = slots_of(flag)
    feats = (feat_even, feat_mine, feat_odd)
    place_weights(weights, column_ref)
    mine = slots[1][1]
    (read_column,) = across_lanes(jnp.broadcast_to(read[...], (LENGTH, LENGTH)), 1)

    def body(block, carry):
        message = feat_mine[0, block + 1, :LENGTH, :].astype(F32)
        for r in range(4):
            lhs = nearby(feats, OWN_SLOTS, block, r * LENGTH)
            message = message + weighted_sum(kern_ref.at[block], r, lhs, column_ref)
        hidden = turned_dot(out_weight[...], message.astype(BF16))
        value, slope = silu_pair(hidden)
        present = even[mine, block + 1][3:4] > -0.5
        energy = jnp.sum(value * read_column, axis=0, keepdims=True)
        energy_out[block] = jnp.where(present, energy, 0.0)
        back = jnp.where(present, slope * read_column, 0.0).astype(BF16)
        pull_out[block] = plain_dot(out_weight[...], back).astype(BF16)
        return carry

    lax.fori_loop(0, 2, body, 0)


def pair_kernel(block, send_ref, recv_ref, kern_ref):
    fill_kernels(send_ref, recv_ref, kern_ref, block)


def third_kernel(
    flag, even, odd, send_ref, recv_ref, feat_even, feat_mine, feat_odd, kern_one, kern_two, pull_even, pull_mine, pull_odd,
    hidden, vectors, energies, bank, weights_one, weights_two, force_out,
    column_ref, hot_ref, feat_ref, seed_ref, deriv_even, deriv_odd,
    push_ref, own_ref,
):
    mix, mixv, embedding = banked(bank)
    pairs = (even, odd)
    feats = (feat_even, feat_mine, feat_odd)
    pulls = (pull_even, pull_mine, pull_odd)
    slots, _ = slots_of(flag)
    depth = BASIS * LENGTH
    place_weights(weights_two, column_ref)
    for tile in range(3):
        for row in range(4):
            hot_ref[row * 3 + tile] = species_hot(pairs[slots[tile][0]][slots[tile][1], row][3:4])
    push_ref[...] = jnp.zeros(push_ref.shape, F32)
    own_ref[...] = jnp.zeros(own_ref.shape, F32)
    table = species_rows(embedding)
    spreads = []
    for which in range(2):
        scale = folded(weights_one, which)
        spreads.append(stacked([table * scale[b : b + 1, :] for b in range(BASIS)]))

    def pull_back(block, kern_ref):
        lhs = nearby(pulls, OWN_SLOTS, block, 0)
        pull = pull_mine[0, block + 1].astype(F32)
        scalar_grad = pull + weighted_sum(kern_ref, 0, lhs, column_ref)
        scalar_grad = scalar_grad.astype(BF16).astype(F32)
        hidden_grad = (scalar_grad * silu_pair(hidden[block])[1]).astype(BF16)
        inv_grad = plain_dot(mix[...], hidden_grad)
        inv_grad = inv_grad.astype(BF16).astype(F32)
        grads = [inv_grad]
        for d in range(3):
            vector_grad = -weighted_sum(kern_ref, d + 1, lhs, column_ref)
            passed = plain_dot(mixv[...], vector_grad.astype(BF16))
            passed = passed.astype(BF16).astype(F32)
            grads.append(passed + 2.0 * vectors[block, d] * inv_grad)
        basis = lax.broadcasted_iota(jnp.int32, (LENGTH, LENGTH), 0) >> 3
        for r in range(4):
            which = min(r, 1)
            table_grad = plain_dot(spreads[which], grads[r], precision=lax.Precision.HIGHEST)
            for b in range(BASIS):
                at = r * depth + b * LENGTH
                scaled = pull * column_ref[which * BASIS + b]
                seed_ref[block, :LENGTH, at : at + LENGTH] = scaled.astype(BF16)
                seed_ref[block, LENGTH:, at : at + LENGTH] = jnp.where(
                    basis == b, table_grad, 0.0
                ).astype(BF16)

    pull_back(0, kern_one)
    pull_back(1, kern_two)
    for tile in range(3):
        for row in range(4):
            feat_ref[row * 3 + tile] = feats[tile][0, row]

    def find(pair):
        block = pair // NEAR
        place = pair - block * NEAR
        return block, place, (block + place // 3) * 3 + place % 3

    def differentiate(pair, deriv_ref):
        block, _, cell = find(pair)
        for r in range(4):
            sender = jnp.concatenate(
                [feat_ref[cell, r * LENGTH : (r + 1) * LENGTH, :], hot_ref[cell]], axis=0
            )
            deriv_ref[:, r * depth : (r + 1) * depth] = turned_dot(
                sender, seed_ref[block, :, r * depth : (r + 1) * depth]
            )

    def chain(pair, deriv_ref):
        sums = [jnp.zeros((16, LENGTH), F32)] * 3
        block, place, cell = find(pair)
        hidden_from = jnp.where(place == 4, 0, 4 * LENGTH)
        rows = 16
        for step in range(LENGTH // rows):
            first = step * rows
            apart, centred, gauss, ratio, rest = pair_geometry(
                send_ref, recv_ref, block, cell, first, rows, hidden_from
            )
            along = [None, None, None]
            value = None
            slope = None
            for b in range(BASIS - 1, -1, -1):
                parts = []
                for r in range(4):
                    at = r * depth + b * LENGTH
                    parts.append(deriv_ref[first : first + rows, at : at + LENGTH])
                joint = parts[0]
                for d in range(3):
                    part = parts[d + 1]
                    joint = joint + apart[d] * part
                    along[d] = part if along[d] is None else along[d] * ratio + part
                if value is None:
                    value = joint
                else:
                    slope = value if slope is None else slope * ratio + value
                    value = value * ratio + joint
            slope = slope * ratio
            scale = gauss * rest
            radial = scale * (8.0 * rest * (slope - centred * value) - 2.0 * value)
            radial = radial * (2.0 * INV_CUTOFF)
            envelope = scale * rest * INV_CUTOFF
            for d in range(3):
                pushed = envelope * along[d] + radial * apart[d]
                push_ref[cell, d, first : first + rows, :] += pushed
                sums[d] = sums[d] + pushed
        for d in range(3):
            own_ref[block, d] += sums[d]

    differentiate(0, deriv_even)

    def pair_steps(step, carry):
        pair = step * 2
        differentiate(pair + 1, deriv_odd)
        chain(pair, deriv_even)
        differentiate(jnp.minimum(pair + 2, 2 * NEAR - 1), deriv_even)
        chain(pair + 1, deriv_odd)
        return carry

    lax.fori_loop(0, NEAR, pair_steps, 0)
    force_out[...] = jnp.zeros(force_out.shape, F32)
    ones = jnp.ones((16, 2 * LENGTH), BF16)
    for row in range(4):
        for tile in range(3):
            for d in range(3):
                total = push_ref[row * 3 + tile, d]
                high = total.astype(BF16)
                low = (total - high.astype(F32)).astype(BF16)
                parts = jnp.concatenate([high, low], axis=1)
                pushed = lax.dot_general(
                    ones, parts, (((1,), (1,)), ((), ())), preferred_element_type=F32
                )[:1]
                if tile == 1 and row in (1, 2):
                    pushed = pushed - jnp.sum(own_ref[row - 1, d], axis=0, keepdims=True)
                force_out[tile, row, d : d + 1, :] = -pushed
    for block in range(2):
        force_out[1, block + 1, 3:4, :] = energies[block]


AXES = ("slab", "tile")


class Grid:
    def __init__(self, slabs, tiles):
        self.slabs, self.tiles = slabs, tiles
        self.moved = (slabs, tiles) == (16, 32)
        self.cycle = [(x, y) for y in range(4) for x in ((1, 2, 3) if y % 2 == 0 else (3, 2, 1))]
        self.cycle += [(0, y) for y in (3, 2, 1, 0)]

    def device(self, slab, tile):
        slab, tile = slab % self.slabs, tile % self.tiles
        if self.moved:
            x, y = self.cycle[slab]
            z, core = tile // 2, (tile // 2 + tile) % 2
            slab, tile = x * 4 + z % 4, ((z // 4) * 4 + y) * 2 + core
        return slab * self.tiles + tile

    def places(self):
        return [(slab, tile) for slab in range(self.slabs) for tile in range(self.tiles)]

    def flag(self):
        odd = lax.axis_index("tile")
        if self.moved:
            odd = odd + lax.axis_index("slab")
        return (1 - odd % 2).astype(jnp.int32)

    def to_work(self, block):
        if not self.moved:
            return block
        route = [(s * self.tiles + t, self.device(s, t)) for s, t in self.places()]
        return lax.ppermute(block, AXES, route)

    def to_owner(self, block):
        if not self.moved:
            return block
        route = [(self.device(s, t), s * self.tiles + t) for s, t in self.places()]
        return lax.ppermute(block, AXES, route)

    def along_slab(self, block, step):
        route = [(self.device(s, t), self.device(s + step, t)) for s, t in self.places()]
        return lax.ppermute(block, AXES, route)

    def with_partner(self, block, odd):
        groups = [
            [self.device(s, t + odd), self.device(s, t + odd + 1)]
            for s, t in self.places()
            if t % 2 == 0
        ]
        return lax.all_gather(block, AXES, axis_index_groups=groups)

    def swap(self, block, odd):
        route = []
        for s, t in self.places():
            if t % 2 == 0:
                ends = self.device(s, t + odd), self.device(s, t + odd + 1)
                route += [ends, ends[::-1]]
        return lax.ppermute(block, AXES, route)

    def column(self, cells):
        above = self.along_slab(cells[1:], 1)
        below = self.along_slab(cells[:1], -1)
        return jnp.concatenate([above, cells, below], axis=0)

    def gather_near(self, cells):
        column = self.column(cells)
        return self.with_partner(column, 0), self.with_partner(column, 1)

    def swap_near(self, cells):
        column = self.column(cells)[None]
        return self.swap(column, 0), column, self.swap(column, 1)

    def send_home(self, parts, flag):
        even = self.with_partner(parts[0], 0)
        odd = self.with_partner(parts[2], 1)
        column = (
            parts[1]
            + lax.dynamic_index_in_dim(even, flag, 0, False)
            + lax.dynamic_index_in_dim(odd, 1 - flag, 0, False)
        )
        from_next = self.along_slab(column[:1], -1)
        from_last = self.along_slab(column[3:], 1)
        return column[1:3] + jnp.concatenate([from_last, from_next], axis=0)


def kernel_call(body, outs, scratch, flops, operands, room, flagged=True):
    in_specs = [pl.BlockSpec(memory_space=pltpu.VMEM)] * operands
    if flagged:
        in_specs[0] = pl.BlockSpec(memory_space=pltpu.SMEM)
    return pl.pallas_call(
        body,
        out_shape=[jax.ShapeDtypeStruct(shape, kind) for shape, kind in outs],
        in_specs=in_specs,
        out_specs=[pl.BlockSpec(memory_space=pltpu.VMEM)] * len(outs),
        scratch_shapes=[pltpu.VMEM(shape, kind) for shape, kind in scratch],
        compiler_params=pltpu.CompilerParams(vmem_limit_bytes=room * 1024 * 1024),
        cost_estimate=pl.CostEstimate(flops=flops, bytes_accessed=1 << 20, transcendentals=0),
    )


GEOMETRY = [
    ((12, 3, LENGTH, LENGTH), F32),
    ((2, 3, LENGTH), F32),
    ((2 * BASIS, LENGTH, LENGTH), F32),
]


def first_call():
    outs = [
        ((2, 4 * LENGTH, LENGTH), BF16),
        ((2, LENGTH, LENGTH), F32),
        ((2, 3, LENGTH, LENGTH), F32),
        ((2, NEAR * LENGTH, 4 * BASIS * LENGTH), BF16),
        ((12, 3, LENGTH, LENGTH), F32),
        ((2, 3, LENGTH), F32),
    ]
    scratch = GEOMETRY[2:] + [((3, 4, LENGTH, LENGTH), BF16)]
    return kernel_call(first_kernel, outs, scratch, 2400000000, 5, 18)


def second_call():
    outs = [((2, 1, LENGTH), F32), ((2, LENGTH, LENGTH), BF16)]
    return kernel_call(second_kernel, outs, GEOMETRY[2:], 2400000000, 9, 18)


def pair_call(block):
    outs = [((NEAR * LENGTH, 4 * BASIS * LENGTH), BF16)]
    body = functools.partial(pair_kernel, block)
    return kernel_call(body, outs, [], 900000000, 2, 18, False)


def third_call():
    scratch = GEOMETRY[2:] + [
        ((12, LENGTH, LENGTH), BF16),
        ((12, 4 * LENGTH, LENGTH), BF16),
        ((2, 2 * LENGTH, 4 * BASIS * LENGTH), BF16),
        ((LENGTH, 4 * BASIS * LENGTH), F32),
        ((LENGTH, 4 * BASIS * LENGTH), F32),
        ((12, 3, LENGTH, LENGTH), F32),
        ((2, 3, 16, LENGTH), F32),
    ]
    return kernel_call(third_kernel, [((3, 4, 4, LENGTH), F32)], scratch, 7200000000, 19, 18)


def on_device(
    grid, positions, species, occupied, embedding, first_radial_weight, radial_two, mix_scalar,
    vector_channel_weight, out_weight, read_weight,
):
    codes = jnp.where(occupied > 0, species, -1).astype(F32)
    packet = jnp.concatenate([positions, codes[:, :, None]], axis=2)[:, 0]
    flag = grid.flag()
    spare = jnp.zeros((16 - embedding.shape[0], LENGTH), BF16)
    bank = jnp.concatenate([mix_scalar, vector_channel_weight, embedding, spare], axis=0)
    weights_one = first_radial_weight * 0.25
    weights_two = radial_two * 0.25
    places = (flag[None], *grid.gather_near(grid.to_work(packet)))
    features, hidden, vectors, kernels, senders, receivers = first_call()(
        *places, bank, weights_one
    )
    near_features = grid.swap_near(features)
    energies, pull = second_call()(
        *places[:2], *near_features, kernels, weights_two, out_weight, read_weight[None, :]
    )
    pull, senders, receivers = lax.optimization_barrier((pull, senders, receivers))
    near_pulls = grid.swap_near(pull)
    again = [pair_call(block)(senders, receivers)[0] for block in range(2)]
    (parts,) = third_call()(
        *places, senders, receivers, *near_features, *again, *near_pulls, hidden, vectors, energies, bank,
        weights_one, weights_two,
    )
    final = grid.to_owner(grid.send_home(parts, flag))
    return final[:, 3:], final[:, None, :3]


def solution(mesh):
    grid = Grid(mesh.shape["slab"], mesh.shape["tile"])
    in_specs = (
        P("slab", "tile", None, None),
        P("slab", "tile", None),
        P("slab", "tile", None),
        P(),
        P(),
        P(),
        P(),
        P(),
        P(),
        P(),
    )
    out_specs = (P("slab", "tile", None), P("slab", "tile", None, None))
    return jax.shard_map(
        functools.partial(on_device, grid), mesh=mesh, in_specs=in_specs, out_specs=out_specs, check_vma=False
    )
```

time: 163 us -> 143 us (0.88)
  Pallas kernels: 60 us -> 37.2 us
  blocking collectives: 28.8 us -> 20 us
  starting transfers between devices: 44.1 us -> 49.3 us
  other arithmetic: 0.09 us -> 3.17 us
  waiting for transfers between devices: 24.8 us -> 26.7 us
    pallas_call x1, Pallas kernels: 36.9 us -> 19.4 us  [on_device(): third_call()]
    all_gather x6 -> x4, blocking collectives: 28.8 us -> 20 us  [with_partner(): return lax.all_gather(block, AXES, axis_index_groups=groups)]
    ppermute x2 -> x4, starting transfers between devices: 7.09 us -> 14.4 us  [swap(): return lax.ppermute(block, AXES, route)]
    pallas_call x1, Pallas kernels: 10.4 us -> 4.5 us  [on_device(): second_call()]
    ppermute x1, starting transfers between devices: 6.11 us -> 3.83 us  [to_owner(): return lax.ppermute(block, AXES, route)]
    ppermute x1, waiting for transfers between devices: 3.6 us -> 5.89 us  [to_owner(): return lax.ppermute(block, AXES, route)]
    pallas_call x1 -> x3, Pallas kernels: 12.7 us -> 13.3 us  [the longest x1 9.82 us: on_device(): first_call()(*places, bank, weights_one)]
    ppermute x2 -> x4, waiting for transfers between devices: 7.14 us -> 7.12 us  [swap(): return lax.ppermute(block, AXES, route)]
  transfers between devices with their start and end apart: 12 -> 14, of which waited for: 8 -> 9; matrix products, arithmetic and copies ran while one was open for 0% -> 1% of each run, Pallas kernels for 0% -> 2%
where the time goes in v3:
time: 143 us; the launch traced here: 141 us
  starting transfers between devices  49.3 us (34%)
  Pallas kernels  37.2 us (26%)
  waiting for transfers between devices  26.7 us (19%)
  blocking collectives  20 us (14%)
  local copies, waits for them, and re-layouts  3.22 us (2%)
  other arithmetic  3.17 us (2%)
    ppermute x8, starting transfers between devices, along_slab(): return lax.ppermute(block, AXES, route)  24.4 us
    all_gather x4, blocking collectives, with_partner(): return lax.all_gather(block, AXES, axis_index_groups=groups)  20 us
    pallas_call x1, Pallas kernels, on_device(): third_call()  19.4 us
    ppermute x4, starting transfers between devices, swap(): return lax.ppermute(block, AXES, route)  14.4 us
    ppermute x8, waiting for transfers between devices, along_slab(): return lax.ppermute(block, AXES, route)  12.5 us
    pallas_call x1, Pallas kernels, on_device(): first_call()(*places, bank, weights_one)  9.82 us
    ppermute x4, waiting for transfers between devices, swap(): return lax.ppermute(block, AXES, route)  7.12 us
    ppermute x1, starting transfers between devices, to_work(): return lax.ppermute(block, AXES, route)  6.56 us
  transfers between devices with their start and end apart: 14, of which 9 were waited for; matrix products, arithmetic and copies ran while one was open for 1% of the time, Pallas kernels for 2%

profile of v3, /device:TPU:24, one launch (start us, length us, event | category | flops | bytes accessed | tf_op | source)
XLA Modules:
  0.0 140.6 jit_solution(16158493132953910979)
XLA Ops:
  2.0 6.6 %collective-permute-start = (f32[2,4,128]{2,1,0:T(4,128)S(1)}, f32[2,4,128]{2,1,0:T(4,128)S(1)}, u32[]{:S(2)}, u32[]{:S(2)}) collective-permute-start(f32[2,4,128]{2,1,0:T(4,128)S(1)} %maximum_bitcast_fusion.2), channel_id=1, source_target_pairs={{0,128},{1,129},{2,161},{3,160},{4,192},{5,193},{6,225},{7,224},{8... | collective-permute-start | bytes 12296 | tf_op jit(solution)/shard_map/ppermute | solution.py:398
  8.7 0.9 maximum_maximum_fusion.bank
  9.6 1.3 collective-permute-done
  10.9 3.8 %collective-permute-start.1 = (f32[1,4,128]{2,1,0:T(4,128)S(1)}, f32[1,4,128]{2,1,0:T(4,128)S(1)}, u32[]{:S(2)}, u32[]{:S(2)}) collective-permute-start(f32[1,4,128]{2,1,0:T(4,128)S(1)} %get-tuple-element.37), channel_id=1, source_target_pairs={{128,256},{129,257},{161,289},{160,288},{192,320},{193,321},{225,3... | collective-permute-start | bytes 6152 | tf_op jit(solution)/shard_map/ppermute | solution.py:408
  15.4 3.1 %collective-permute-start.2 = (f32[1,4,128]{2,1,0:T(4,128)S(1)}, f32[1,4,128]{2,1,0:T(4,128)S(1)}, u32[]{:S(2)}, u32[]{:S(2)}) collective-permute-start(f32[1,4,128]{2,1,0:T(4,128)S(1)} %get-tuple-element.36), channel_id=1, source_target_pairs={{128,0},{129,1},{161,33},{160,32},{192,64},{193,65},{225,97},{224,... | collective-permute-start | bytes 6152 | tf_op jit(solution)/shard_map/ppermute | solution.py:408
  18.5 2.5 %collective-permute-done.2 = f32[1,4,128]{2,1,0:T(4,128)S(1)} collective-permute-done((f32[1,4,128]{2,1,0:T(4,128)S(1)}, f32[1,4,128]{2,1,0:T(4,128)S(1)}, u32[]{:S(2)}, u32[]{:S(2)}) %collective-permute-start.2) | collective-permute-done | bytes 2080 | tf_op jit(solution)/shard_map/ppermute | solution.py:408
  21.0 1.8 %all-gather = f32[8,4,128]{2,1,0:T(4,128)S(1)} all-gather(f32[4,4,128]{2,1,0:T(4,128)S(1)} %constant_dynamic-update-slice_fusion), channel_id=2, replica_groups={{128,129},{161,160},{192,193},{225,224},{136,137},{169,168},{200,201},{..., dimensions={0}, use_global_device_ids=true | all-gather | bytes 24576 | tf_op jit(solution)/shard_map/all_gather | solution.py:416
  22.8 10.6 %all-gather.1 = f32[8,4,128]{2,1,0:T(4,128)S(1)} all-gather(f32[4,4,128]{2,1,0:T(4,128)S(1)} %constant_dynamic-update-slice_fusion), channel_id=3, replica_groups={{129,161},{160,192},{193,225},{224,136},{137,169},{168,200},{201,233},{..., dimensions={0}, use_global_device_ids=true | all-gather | bytes 24576 | tf_op jit(solution)/shard_map/all_gather | solution.py:416
  33.5 9.8 %shard_map.113 = (bf16[2,512,128]{2,1,0:T(8,128)(2,1)S(1)}, f32[2,128,128]{2,1,0:T(8,128)S(1)}, f32[2,3,128,128]{3,2,1,0:T(8,128)S(1)}, bf16[2,1152,4096]{2,1,0:...) custom-call(s32[1]{0:T(128)} %bitcast.flag, f32[2,4,4,128]{3,2,1,0:T(4,128)S(1)} %bitcast.23, ...), custom_call_target="tpu_custom_call" | custom-call | flops 2400000000 | bytes 1048576 | tf_op jit(solution)/shard_map/pallas_call | solution.py:523
  43.3 3.0 %collective-permute-start.3 = (bf16[1,512,128]{2,1,0:T(8,128)(2,1)S(1)}, bf16[1,512,128]{2,1,0:T(8,128)(2,1)S(1)}, u32[]{:S(2)}, u32[]{:S(2)}) collective-permute-start(bf16[1,512,128]{2,1,0:T(8,128)(2,1)S(1)} %get-tuple-element.28), channel_id=1, source_target_pairs={{128,256},{129,257},{161,289},{160,288},{192,320},{193,321},{225,3... | collective-permute-start | bytes 393224 | tf_op jit(solution)/shard_map/ppermute | solution.py:408
  46.3 2.9 %collective-permute-start.4 = (bf16[1,512,128]{2,1,0:T(8,128)(2,1)S(1)}, bf16[1,512,128]{2,1,0:T(8,128)(2,1)S(1)}, u32[]{:S(2)}, u32[]{:S(2)}) collective-permute-start(bf16[1,512,128]{2,1,0:T(8,128)(2,1)S(1)} %get-tuple-element.29), channel_id=1, source_target_pairs={{128,0},{129,1},{161,33},{160,32},{192,64},{193,65},{225,97},{224,... | collective-permute-start | bytes 393224 | tf_op jit(solution)/shard_map/ppermute | solution.py:408
  49.2 1.0 collective-permute-done.3
  50.2 3.0 %collective-permute-done.4 = bf16[1,512,128]{2,1,0:T(8,128)(2,1)S(1)} collective-permute-done((bf16[1,512,128]{2,1,0:T(8,128)(2,1)S(1)}, bf16[1,512,128]{2,1,0:T(8,128)(2,1)S(1)}, u32[]{:S(2)}, u32[]{:S(2)}) %collective-permute-start.4) | collective-permute-done | bytes 131104 | tf_op jit(solution)/shard_map/ppermute | solution.py:408
  53.2 1.9 %collective-permute-start.5 = (bf16[1,4,512,128]{3,2,1,0:T(8,128)(2,1)S(1)}, bf16[1,4,512,128]{3,2,1,0:T(8,128)(2,1)S(1)}, u32[]{:S(2)}, u32[]{:S(2)}) collective-permute-start(bf16[1,4,512,128]{3,2,1,0:T(8,128)(2,1)S(1)} %maximum_bitcast_fusion.feat_mine), channel_id=1, source_target_pairs={{128,129},{129,128},{161,160},{160,161},{192,193},{193,192},{225,2... | collective-permute-start | bytes 1572872 | tf_op jit(solution)/shard_map/ppermute | solution.py:424
  55.2 5.2 %collective-permute-start.6 = (bf16[1,4,512,128]{3,2,1,0:T(8,128)(2,1)S(1)}, bf16[1,4,512,128]{3,2,1,0:T(8,128)(2,1)S(1)}, u32[]{:S(2)}, u32[]{:S(2)}) collective-permute-start(bf16[1,4,512,128]{3,2,1,0:T(8,128)(2,1)S(1)} %maximum_bitcast_fusion.feat_mine), channel_id=1, source_target_pairs={{129,161},{161,129},{160,192},{192,160},{193,225},{225,193},{224,1... | collective-permute-start | bytes 1572872 | tf_op jit(solution)/shard_map/ppermute | solution.py:424
  60.4 7.1 %collective-permute-done.6.feat_odd = bf16[1,4,512,128]{3,2,1,0:T(8,128)(2,1)S(1)} collective-permute-done((bf16[1,4,512,128]{3,2,1,0:T(8,128)(2,1)S(1)}, bf16[1,4,512,128]{3,2,1,0:T(8,128)(2,1)S(1)}, u32[]{:S(2)}, u32[]{:S(2)}) %collective-permute-start.6) | collective-permute-done | bytes 524320 | tf_op jit(solution)/shard_map/ppermute | solution.py:424
  67.5 4.5 %shard_map.114 = (f32[2,1,128]{2,1,0:T(1,128)S(1)}, bf16[2,128,128]{2,1,0:T(8,128)(2,1)S(1)}) custom-call(s32[1]{0:T(128)} %bitcast.flag, f32[2,4,4,128]{3,2,1,0:T(4,128)S(1)} %bitcast.24, bf16[1,4,512,128]{3,2,1,0:T(8,128)(2,1)S(1)} %collective-permute-done.5.feat_even, bf16[1,4,512,128]{3,2,1,0:T(8,128)(2,1)S(1)} %maximum_bitcast_fusion.feat_mine, ...), custom_call_target="tpu_custom_call" | custom-call | flops 2400000000 | bytes 1048576 | tf_op jit(solution)/shard_map/pallas_call | solution.py:527
  73.2 2.2 %collective-permute-start.7 = (bf16[1,128,128]{2,1,0:T(8,128)(2,1)}, bf16[1,128,128]{2,1,0:T(8,128)(2,1)}, u32[]{:S(2)}, u32[]{:S(2)}) collective-permute-start(bf16[1,128,128]{2,1,0:T(8,128)(2,1)} %get-tuple-element.30), channel_id=1, source_target_pairs={{128,256},{129,257},{161,289},{160,288},{192,320},{193,321},{225,3... | collective-permute-start | bytes 98312 | tf_op jit(solution)/shard_map/ppermute | solution.py:408
  75.4 3.6 %collective-permute-start.8 = (bf16[1,128,128]{2,1,0:T(8,128)(2,1)}, bf16[1,128,128]{2,1,0:T(8,128)(2,1)}, u32[]{:S(2)}, u32[]{:S(2)}) collective-permute-start(bf16[1,128,128]{2,1,0:T(8,128)(2,1)} %get-tuple-element.31), channel_id=1, source_target_pairs={{128,0},{129,1},{161,33},{160,32},{192,64},{193,65},{225,97},{224,... | collective-permute-start | bytes 98312 | tf_op jit(solution)/shard_map/ppermute | solution.py:408
  79.3 2.2 %collective-permute-done.8 = bf16[1,128,128]{2,1,0:T(8,128)(2,1)} collective-permute-done((bf16[1,128,128]{2,1,0:T(8,128)(2,1)}, bf16[1,128,128]{2,1,0:T(8,128)(2,1)}, u32[]{:S(2)}, u32[]{:S(2)}) %collective-permute-start.8) | collective-permute-done | bytes 32800 | tf_op jit(solution)/shard_map/ppermute | solution.py:408
  82.4 5.3 %collective-permute-start.10 = (bf16[1,4,128,128]{3,2,1,0:T(8,128)(2,1)S(1)}, bf16[1,4,128,128]{3,2,1,0:T(8,128)(2,1)S(1)}, u32[]{:S(2)}, u32[]{:S(2)}) collective-permute-start(bf16[1,4,128,128]{3,2,1,0:T(8,128)(2,1)S(1)} %maximum_bitcast_fusion.1.pull_mine), channel_id=1, source_target_pairs={{129,161},{161,129},{160,192},{192,160},{193,225},{225,193},{224,1... | collective-permute-start | bytes 393224 | tf_op jit(solution)/shard_map/ppermute | solution.py:424
  87.7 2.1 %collective-permute-start.9 = (bf16[1,4,128,128]{3,2,1,0:T(8,128)(2,1)S(1)}, bf16[1,4,128,128]{3,2,1,0:T(8,128)(2,1)S(1)}, u32[]{:S(2)}, u32[]{:S(2)}) collective-permute-start(bf16[1,4,128,128]{3,2,1,0:T(8,128)(2,1)S(1)} %maximum_bitcast_fusion.1.pull_mine), channel_id=1, source_target_pairs={{128,129},{129,128},{161,160},{160,161},{192,193},{193,192},{225,2... | collective-permute-start | bytes 393224 | tf_op jit(solution)/shard_map/ppermute | solution.py:424
  89.8 1.7 %shard_map.116.kern_two = bf16[1152,4096]{1,0:T(8,128)(2,1)S(1)} custom-call(f32[12,3,128,128]{3,2,1,0:T(8,128)S(1)} %get-tuple-element.18.send_ref, f32[2,3,128]{2,1,0:T(4,128)S(1)} %get-tuple-element.19.recv_ref), custom_call_target="tpu_custom_call" | custom-call | flops 900000000 | bytes 1048576 | tf_op jit(solution)/shard_map/pallas_call | solution.py:532
  91.6 1.7 %shard_map.115.kern_one = bf16[1152,4096]{1,0:T(8,128)(2,1)S(1)} custom-call(f32[12,3,128,128]{3,2,1,0:T(8,128)S(1)} %get-tuple-element.18.send_ref, f32[2,3,128]{2,1,0:T(4,128)S(1)} %get-tuple-element.19.recv_ref), custom_call_target="tpu_custom_call" | custom-call | flops 900000000 | bytes 1048576 | tf_op jit(solution)/shard_map/pallas_call | solution.py:532
  93.4 19.4 %shard_map.117 = f32[3,4,4,128]{3,2,1,0:T(4,128)S(1)} custom-call(s32[1]{0:T(128)} %bitcast.flag, f32[2,4,4,128]{3,2,1,0:T(4,128)S(1)} %bitcast.25, f32[2,4,4,128]{3,2,1,0:T(4,128)S(1)} %bitcast.27, f32[12,3,128,128]{3,2,1,0:T(8,128)S(1)} %get-tuple-element.18.send_ref, f32[2,3,128]{2,1,0:T(4,128)S(1)} %get-tuple-element.19.recv_ref, ...), custom_call_target="tpu_custom_call" | custom-call | flops 7200000000 | bytes 1048576 | tf_op jit(solution)/shard_map/pallas_call | solution.py:533
  112.8 2.0 %all_gather.19 = f32[2,4,4,128]{3,2,1,0:T(4,128)S(1)} all-gather(f32[1,4,4,128]{3,2,1,0:T(4,128)S(1)} %get-tuple-element.32), channel_id=1, replica_groups={{128,129},{161,160},{192,193},{225,224},{136,137},{169,168},{200,201},{..., dimensions={0}, use_global_device_ids=true | all-gather | bytes 24576 | tf_op jit(solution)/shard_map/all_gather | solution.py:416
  114.8 5.6 %all_gather.20 = f32[2,4,4,128]{3,2,1,0:T(4,128)S(1)} all-gather(f32[1,4,4,128]{3,2,1,0:T(4,128)S(1)} %get-tuple-element.33), channel_id=1, replica_groups={{129,161},{160,192},{193,225},{224,136},{137,169},{168,200},{201,233},{..., dimensions={0}, use_global_device_ids=true | all-gather | bytes 24576 | tf_op jit(solution)/shard_map/all_gather | solution.py:416
  120.3 3.9 %collective-permute-start.11 = (f32[1,4,128]{2,1,0:T(4,128)S(1)}, f32[1,4,128]{2,1,0:T(4,128)S(1)}, u32[]{:S(2)}, u32[]{:S(2)}) collective-permute-start(f32[1,4,128]{2,1,0:T(4,128)S(1)} %get-tuple-element.34), channel_id=1, source_target_pairs={{128,256},{129,257},{161,289},{160,288},{192,320},{193,321},{225,3... | collective-permute-start | bytes 6152 | tf_op jit(solution)/shard_map/ppermute | solution.py:408
  124.3 1.9 %collective-permute-start.12 = (f32[1,4,128]{2,1,0:T(4,128)S(1)}, f32[1,4,128]{2,1,0:T(4,128)S(1)}, u32[]{:S(2)}, u32[]{:S(2)}) collective-permute-start(f32[1,4,128]{2,1,0:T(4,128)S(1)} %get-tuple-element.35), channel_id=1, source_target_pairs={{128,0},{129,1},{161,33},{160,32},{192,64},{193,65},{225,97},{224,... | collective-permute-start | bytes 6152 | tf_op jit(solution)/shard_map/ppermute | solution.py:408
  126.2 3.5 %collective-permute-done.12 = f32[1,4,128]{2,1,0:T(4,128)S(1)} collective-permute-done((f32[1,4,128]{2,1,0:T(4,128)S(1)}, f32[1,4,128]{2,1,0:T(4,128)S(1)}, u32[]{:S(2)}, u32[]{:S(2)}) %collective-permute-start.12) | collective-permute-done | bytes 2080 | tf_op jit(solution)/shard_map/ppermute | solution.py:408
  129.8 3.8 %collective-permute-start.13 = (f32[2,4,128]{2,1,0:T(4,128)S(1)}, f32[2,4,128]{2,1,0:T(4,128)S(1)}, u32[]{:S(2)}, u32[]{:S(2)}) collective-permute-start(f32[2,4,128]{2,1,0:T(4,128)S(1)} %fusion.1), channel_id=1, source_target_pairs={{128,0},{129,1},{161,2},{160,3},{192,4},{193,5},{225,6},{224,7},{1... | collective-permute-start | bytes 12296 | tf_op jit(solution)/shard_map/ppermute | solution.py:404
  133.6 5.9 %collective-permute-done.13 = f32[2,4,128]{2,1,0:T(4,128)S(1)} collective-permute-done((f32[2,4,128]{2,1,0:T(4,128)S(1)}, f32[2,4,128]{2,1,0:T(4,128)S(1)}, u32[]{:S(2)}, u32[]{:S(2)}) %collective-permute-start.13) | collective-permute-done | bytes 4128 | tf_op jit(solution)/shard_map/ppermute | solution.py:404
  (62 shorter events, 5.8 us)
Async XLA Ops:
  0.6 59.7 %copy-start.16 = (f32[2,8,128]{2,1,0:T(8,128)S(1)}, f32[2,8,128]{2,1,0:T(8,128)}, u32[]{:S(2)}) copy-start(f32[2,8,128]{2,1,0:T(8,128)} %param.15) | copy-start | bytes 24580
  2.0 8.8 %collective-permute-start = (f32[2,4,128]{2,1,0:T(4,128)S(1)}, f32[2,4,128]{2,1,0:T(4,128)S(1)}, u32[]{:S(2)}, u32[]{:S(2)}) collective-permute-start(f32[2,4,128]{2,1,0:T(4,128)S(1)} %maximum_bitcast_fusion.2), channel_id=1, source_target_pairs={{0,128},{1,129},{2,161},{3,160},{4,192},{5,193},{6,225},{7,224},{8... | collective-permute-start | bytes 12296 | tf_op jit(solution)/shard_map/ppermute | solution.py:398
  10.9 7.6 %collective-permute-start.1 = (f32[1,4,128]{2,1,0:T(4,128)S(1)}, f32[1,4,128]{2,1,0:T(4,128)S(1)}, u32[]{:S(2)}, u32[]{:S(2)}) collective-permute-start(f32[1,4,128]{2,1,0:T(4,128)S(1)} %get-tuple-element.37), channel_id=1, source_target_pairs={{128,256},{129,257},{161,289},{160,288},{192,320},{193,321},{225,3... | collective-permute-start | bytes 6152 | tf_op jit(solution)/shard_map/ppermute | solution.py:408
  15.4 39.8 %copy-start.7 = (f32[2,8,128]{2,1,0:T(8,128)}, f32[2,8,128]{2,1,0:T(8,128)S(1)}, u32[]{:S(2)}) copy-start(f32[2,8,128]{2,1,0:T(8,128)S(1)} %broadcast_multiply_fusion.1.weights.weights_one) | copy-start | bytes 24580
  15.4 52.1 %copy-start.4 = (bf16[128,128]{1,0:T(8,128)(2,1)S(1)}, bf16[128,128]{1,0:T(8,128)(2,1)}, u32[]{:S(2)}) copy-start(bf16[128,128]{1,0:T(8,128)(2,1)} %out_weight.1) | copy-start | bytes 98308
  15.4 52.1 %copy-start.9 = (f32[128]{0:T(128)S(1)}, f32[128]{0:T(128)}, u32[]{:S(2)}) copy-start(f32[128]{0:T(128)} %param.19) | copy-start | bytes 1540
  15.4 5.6 %collective-permute-start.2 = (f32[1,4,128]{2,1,0:T(4,128)S(1)}, f32[1,4,128]{2,1,0:T(4,128)S(1)}, u32[]{:S(2)}, u32[]{:S(2)}) collective-permute-start(f32[1,4,128]{2,1,0:T(4,128)S(1)} %get-tuple-element.36), channel_id=1, source_target_pairs={{128,0},{129,1},{161,33},{160,32},{192,64},{193,65},{225,97},{224,... | collective-permute-start | bytes 6152 | tf_op jit(solution)/shard_map/ppermute | solution.py:408
  22.8 49.2 %copy-start.2 = (f32[8,4,128]{2,1,0:T(4,128)}, f32[8,4,128]{2,1,0:T(4,128)S(1)}, u32[]{:S(2)}) copy-start(f32[8,4,128]{2,1,0:T(4,128)S(1)} %all-gather) | copy-start | bytes 49156
  33.5 38.6 %copy-start.5 = (f32[8,4,128]{2,1,0:T(4,128)}, f32[8,4,128]{2,1,0:T(4,128)S(1)}, u32[]{:S(2)}) copy-start(f32[8,4,128]{2,1,0:T(4,128)S(1)} %all-gather.1) | copy-start | bytes 49156
  43.3 6.9 %copy-start.12 = (f32[2,3,128,128]{3,2,1,0:T(8,128)}, f32[2,3,128,128]{3,2,1,0:T(8,128)S(1)}, u32[]{:S(2)}) copy-start(f32[2,3,128,128]{3,2,1,0:T(8,128)S(1)} %get-tuple-element.22.vectors) | copy-start | bytes 1179652
  43.3 6.9 %copy-start.14 = (f32[2,128,128]{2,1,0:T(8,128)}, f32[2,128,128]{2,1,0:T(8,128)S(1)}, u32[]{:S(2)}) copy-start(f32[2,128,128]{2,1,0:T(8,128)S(1)} %get-tuple-element.21.hidden) | copy-start | bytes 393220
  43.3 6.9 %collective-permute-start.3 = (bf16[1,512,128]{2,1,0:T(8,128)(2,1)S(1)}, bf16[1,512,128]{2,1,0:T(8,128)(2,1)S(1)}, u32[]{:S(2)}, u32[]{:S(2)}) collective-permute-start(bf16[1,512,128]{2,1,0:T(8,128)(2,1)S(1)} %get-tuple-element.28), channel_id=1, source_target_pairs={{128,256},{129,257},{161,289},{160,288},{192,320},{193,321},{225,3... | collective-permute-start | bytes 393224 | tf_op jit(solution)/shard_map/ppermute | solution.py:408
  46.3 6.9 %collective-permute-start.4 = (bf16[1,512,128]{2,1,0:T(8,128)(2,1)S(1)}, bf16[1,512,128]{2,1,0:T(8,128)(2,1)S(1)}, u32[]{:S(2)}, u32[]{:S(2)}) collective-permute-start(bf16[1,512,128]{2,1,0:T(8,128)(2,1)S(1)} %get-tuple-element.29), channel_id=1, source_target_pairs={{128,0},{129,1},{161,33},{160,32},{192,64},{193,65},{225,97},{224,... | collective-permute-start | bytes 393224 | tf_op jit(solution)/shard_map/ppermute | solution.py:408
  53.2 7.1 %collective-permute-start.5 = (bf16[1,4,512,128]{3,2,1,0:T(8,128)(2,1)S(1)}, bf16[1,4,512,128]{3,2,1,0:T(8,128)(2,1)S(1)}, u32[]{:S(2)}, u32[]{:S(2)}) collective-permute-start(bf16[1,4,512,128]{3,2,1,0:T(8,128)(2,1)S(1)} %maximum_bitcast_fusion.feat_mine), channel_id=1, source_target_pairs={{128,129},{129,128},{161,160},{160,161},{192,193},{193,192},{225,2... | collective-permute-start | bytes 1572872 | tf_op jit(solution)/shard_map/ppermute | solution.py:424
  55.2 12.3 %collective-permute-start.6 = (bf16[1,4,512,128]{3,2,1,0:T(8,128)(2,1)S(1)}, bf16[1,4,512,128]{3,2,1,0:T(8,128)(2,1)S(1)}, u32[]{:S(2)}, u32[]{:S(2)}) collective-permute-start(bf16[1,4,512,128]{3,2,1,0:T(8,128)(2,1)S(1)} %maximum_bitcast_fusion.feat_mine), channel_id=1, source_target_pairs={{129,161},{161,129},{160,192},{192,160},{193,225},{225,193},{224,1... | collective-permute-start | bytes 1572872 | tf_op jit(solution)/shard_map/ppermute | solution.py:424
  67.5 4.5 %copy-start = (bf16[1,4,512,128]{3,2,1,0:T(8,128)(2,1)}, bf16[1,4,512,128]{3,2,1,0:T(8,128)(2,1)S(1)}, u32[]{:S(2)}) copy-start(bf16[1,4,512,128]{3,2,1,0:T(8,128)(2,1)S(1)} %collective-permute-done.6.feat_odd) | copy-start | bytes 1572868
  72.0 0.6 copy-start.10
  73.2 6.1 %collective-permute-start.7 = (bf16[1,128,128]{2,1,0:T(8,128)(2,1)}, bf16[1,128,128]{2,1,0:T(8,128)(2,1)}, u32[]{:S(2)}, u32[]{:S(2)}) collective-permute-start(bf16[1,128,128]{2,1,0:T(8,128)(2,1)} %get-tuple-element.30), channel_id=1, source_target_pairs={{128,256},{129,257},{161,289},{160,288},{192,320},{193,321},{225,3... | collective-permute-start | bytes 98312 | tf_op jit(solution)/shard_map/ppermute | solution.py:408
  75.4 6.1 %collective-permute-start.8 = (bf16[1,128,128]{2,1,0:T(8,128)(2,1)}, bf16[1,128,128]{2,1,0:T(8,128)(2,1)}, u32[]{:S(2)}, u32[]{:S(2)}) collective-permute-start(bf16[1,128,128]{2,1,0:T(8,128)(2,1)} %get-tuple-element.31), channel_id=1, source_target_pairs={{128,0},{129,1},{161,33},{160,32},{192,64},{193,65},{225,97},{224,... | collective-permute-start | bytes 98312 | tf_op jit(solution)/shard_map/ppermute | solution.py:408
  82.4 11.0 %copy-start.1 = (bf16[1,4,512,128]{3,2,1,0:T(8,128)(2,1)S(1)}, bf16[1,4,512,128]{3,2,1,0:T(8,128)(2,1)}, u32[]{:S(2)}) copy-start(bf16[1,4,512,128]{3,2,1,0:T(8,128)(2,1)} %copy-done) | copy-start | bytes 1572868
  82.4 11.0 %copy-start.3 = (f32[8,4,128]{2,1,0:T(4,128)S(1)}, f32[8,4,128]{2,1,0:T(4,128)}, u32[]{:S(2)}) copy-start(f32[8,4,128]{2,1,0:T(4,128)} %copy-done.2) | copy-start | bytes 49156
  82.4 11.0 %copy-start.6 = (f32[8,4,128]{2,1,0:T(4,128)S(1)}, f32[8,4,128]{2,1,0:T(4,128)}, u32[]{:S(2)}) copy-start(f32[8,4,128]{2,1,0:T(4,128)} %copy-done.5) | copy-start | bytes 49156
  82.4 11.0 %copy-start.8 = (f32[2,8,128]{2,1,0:T(8,128)S(1)}, f32[2,8,128]{2,1,0:T(8,128)}, u32[]{:S(2)}) copy-start(f32[2,8,128]{2,1,0:T(8,128)} %copy-done.7) | copy-start | bytes 24580
  82.4 11.0 %copy-start.11 = (f32[2,1,128]{2,1,0:T(1,128)S(1)}, f32[2,1,128]{2,1,0:T(1,128)}, u32[]{:S(2)}) copy-start(f32[2,1,128]{2,1,0:T(1,128)} %copy-done.10) | copy-start | bytes 3076
  82.4 11.0 %copy-start.13 = (f32[2,3,128,128]{3,2,1,0:T(8,128)S(1)}, f32[2,3,128,128]{3,2,1,0:T(8,128)}, u32[]{:S(2)}) copy-start(f32[2,3,128,128]{3,2,1,0:T(8,128)} %copy-done.12) | copy-start | bytes 1179652
  82.4 11.0 %copy-start.15 = (f32[2,128,128]{2,1,0:T(8,128)S(1)}, f32[2,128,128]{2,1,0:T(8,128)}, u32[]{:S(2)}) copy-start(f32[2,128,128]{2,1,0:T(8,128)} %copy-done.14) | copy-start | bytes 393220
  82.4 10.9 %collective-permute-start.10 = (bf16[1,4,128,128]{3,2,1,0:T(8,128)(2,1)S(1)}, bf16[1,4,128,128]{3,2,1,0:T(8,128)(2,1)S(1)}, u32[]{:S(2)}, u32[]{:S(2)}) collective-permute-start(bf16[1,4,128,128]{3,2,1,0:T(8,128)(2,1)S(1)} %maximum_bitcast_fusion.1.pull_mine), channel_id=1, source_target_pairs={{129,161},{161,129},{160,192},{192,160},{193,225},{225,193},{224,1... | collective-permute-start | bytes 393224 | tf_op jit(solution)/shard_map/ppermute | solution.py:424
  87.7 5.6 %collective-permute-start.9 = (bf16[1,4,128,128]{3,2,1,0:T(8,128)(2,1)S(1)}, bf16[1,4,128,128]{3,2,1,0:T(8,128)(2,1)S(1)}, u32[]{:S(2)}, u32[]{:S(2)}) collective-permute-start(bf16[1,4,128,128]{3,2,1,0:T(8,128)(2,1)S(1)} %maximum_bitcast_fusion.1.pull_mine), channel_id=1, source_target_pairs={{128,129},{129,128},{161,160},{160,161},{192,193},{193,192},{225,2... | collective-permute-start | bytes 393224 | tf_op jit(solution)/shard_map/ppermute | solution.py:424
  120.3 5.9 %collective-permute-start.11 = (f32[1,4,128]{2,1,0:T(4,128)S(1)}, f32[1,4,128]{2,1,0:T(4,128)S(1)}, u32[]{:S(2)}, u32[]{:S(2)}) collective-permute-start(f32[1,4,128]{2,1,0:T(4,128)S(1)} %get-tuple-element.34), channel_id=1, source_target_pairs={{128,256},{129,257},{161,289},{160,288},{192,320},{193,321},{225,3... | collective-permute-start | bytes 6152 | tf_op jit(solution)/shard_map/ppermute | solution.py:408
  124.3 5.5 %collective-permute-start.12 = (f32[1,4,128]{2,1,0:T(4,128)S(1)}, f32[1,4,128]{2,1,0:T(4,128)S(1)}, u32[]{:S(2)}, u32[]{:S(2)}) collective-permute-start(f32[1,4,128]{2,1,0:T(4,128)S(1)} %get-tuple-element.35), channel_id=1, source_target_pairs={{128,0},{129,1},{161,33},{160,32},{192,64},{193,65},{225,97},{224,... | collective-permute-start | bytes 6152 | tf_op jit(solution)/shard_map/ppermute | solution.py:408
  129.8 9.7 %collective-permute-start.13 = (f32[2,4,128]{2,1,0:T(4,128)S(1)}, f32[2,4,128]{2,1,0:T(4,128)S(1)}, u32[]{:S(2)}, u32[]{:S(2)}) collective-permute-start(f32[2,4,128]{2,1,0:T(4,128)S(1)} %fusion.1), channel_id=1, source_target_pairs={{128,0},{129,1},{161,2},{160,3},{192,4},{193,5},{225,6},{224,7},{1... | collective-permute-start | bytes 12296 | tf_op jit(solution)/shard_map/ppermute | solution.py:404

commit v4 on v3

--- a/solution.py
+++ b/solution.py
@@ -371,8 +371,8 @@
     def __init__(self, slabs, tiles):
         self.slabs, self.tiles = slabs, tiles
         self.moved = (slabs, tiles) == (16, 32)
-        self.cycle = [(x, y) for y in range(4) for x in ((1, 2, 3) if y % 2 == 0 else (3, 2, 1))]
-        self.cycle += [(0, y) for y in (3, 2, 1, 0)]
+        self.cycle = [(0, 0), (0, 1), (0, 2), (0, 3), (1, 3), (1, 2), (1, 1), (2, 1)]
+        self.cycle += [(2, 2), (2, 3), (3, 3), (3, 2), (3, 1), (3, 0), (2, 0), (1, 0)]
 
     def device(self, slab, tile):
         slab, tile = slab % self.slabs, tile % self.tiles

time: 143 us -> 139 us (0.972); the launches traced: 141 us -> 138 us
  starting transfers between devices: 49.3 us -> 45.7 us
    ppermute x1, starting transfers between devices: 3.83 us -> 2.15 us  [to_owner(): return lax.ppermute(block, AXES, route)]
    ppermute x1, waiting for transfers between devices: 1.27 us -> 2.79 us  [to_work(): return lax.ppermute(block, AXES, route)]
  transfers between devices with their start and end apart: 14 -> 14, of which waited for: 9 -> 9; matrix products, arithmetic and copies ran while one was open for 1% -> 1% of each run, Pallas kernels for 2% -> 3%
where the time goes in v4:
time: 139 us; the launch traced here: 138 us
  starting transfers between devices  45.7 us (33%)
  Pallas kernels  37.2 us (27%)
  waiting for transfers between devices  28 us (20%)
  blocking collectives  20 us (14%)
  local copies, waits for them, and re-layouts  3.22 us (2%)
  other arithmetic  3.17 us (2%)
    ppermute x8, starting transfers between devices, along_slab(): return lax.ppermute(block, AXES, route)  23.5 us
    all_gather x4, blocking collectives, with_partner(): return lax.all_gather(block, AXES, axis_index_groups=groups)  20 us
    pallas_call x1, Pallas kernels, on_device(): third_call()  19.4 us
    ppermute x4, starting transfers between devices, swap(): return lax.ppermute(block, AXES, route)  14.5 us
    ppermute x8, waiting for transfers between devices, along_slab(): return lax.ppermute(block, AXES, route)  11.4 us
    pallas_call x1, Pallas kernels, on_device(): first_call()(*places, bank, weights_one)  9.83 us
    ppermute x4, waiting for transfers between devices, swap(): return lax.ppermute(block, AXES, route)  7.12 us
    ppermute x1, waiting for transfers between devices, to_owner(): return lax.ppermute(block, AXES, route)  6.67 us
  transfers between devices with their start and end apart: 14, of which 9 were waited for; matrix products, arithmetic and copies ran while one was open for 1% of the time, Pallas kernels for 3%

profile of v4, /device:TPU:24, one launch (start us, length us, event | category | flops | bytes accessed | tf_op | source)
XLA Modules:
  0.0 138.3 jit_solution(15923139381787731367)
XLA Ops:
  2.0 5.6 %collective-permute-start = (f32[2,4,128]{2,1,0:T(4,128)S(1)}, f32[2,4,128]{2,1,0:T(4,128)S(1)}, u32[]{:S(2)}, u32[]{:S(2)}) collective-permute-start(f32[2,4,128]{2,1,0:T(4,128)S(1)} %maximum_bitcast_fusion.2), channel_id=1, source_target_pairs={{0,0},{1,1},{2,33},{3,32},{4,64},{5,65},{6,97},{7,96},{8,8},{9,9},... | collective-permute-start | bytes 12296 | tf_op jit(solution)/shard_map/ppermute | solution.py:398
  7.8 0.9 maximum_maximum_fusion.bank
  8.7 2.8 %collective-permute-done = f32[2,4,128]{2,1,0:T(4,128)S(1)} collective-permute-done((f32[2,4,128]{2,1,0:T(4,128)S(1)}, f32[2,4,128]{2,1,0:T(4,128)S(1)}, u32[]{:S(2)}, u32[]{:S(2)}) %collective-permute-start) | collective-permute-done | bytes 4128 | tf_op jit(solution)/shard_map/ppermute | solution.py:398
  11.4 1.9 %collective-permute-start.1 = (f32[1,4,128]{2,1,0:T(4,128)S(1)}, f32[1,4,128]{2,1,0:T(4,128)S(1)}, u32[]{:S(2)}, u32[]{:S(2)}) collective-permute-start(f32[1,4,128]{2,1,0:T(4,128)S(1)} %get-tuple-element.37), channel_id=1, source_target_pairs={{0,2},{1,3},{33,35},{32,34},{64,66},{65,67},{97,99},{96,98},{8,10}... | collective-permute-start | bytes 6152 | tf_op jit(solution)/shard_map/ppermute | solution.py:408
  14.1 4.0 %collective-permute-start.2 = (f32[1,4,128]{2,1,0:T(4,128)S(1)}, f32[1,4,128]{2,1,0:T(4,128)S(1)}, u32[]{:S(2)}, u32[]{:S(2)}) collective-permute-start(f32[1,4,128]{2,1,0:T(4,128)S(1)} %get-tuple-element.36), channel_id=1, source_target_pairs={{0,128},{1,129},{33,161},{32,160},{64,192},{65,193},{97,225},{96,2... | collective-permute-start | bytes 6152 | tf_op jit(solution)/shard_map/ppermute | solution.py:408
  18.2 1.5 %collective-permute-done.2 = f32[1,4,128]{2,1,0:T(4,128)S(1)} collective-permute-done((f32[1,4,128]{2,1,0:T(4,128)S(1)}, f32[1,4,128]{2,1,0:T(4,128)S(1)}, u32[]{:S(2)}, u32[]{:S(2)}) %collective-permute-start.2) | collective-permute-done | bytes 2080 | tf_op jit(solution)/shard_map/ppermute | solution.py:408
  19.7 1.8 %all-gather = f32[8,4,128]{2,1,0:T(4,128)S(1)} all-gather(f32[4,4,128]{2,1,0:T(4,128)S(1)} %constant_dynamic-update-slice_fusion), channel_id=2, replica_groups={{0,1},{33,32},{64,65},{97,96},{8,9},{41,40},{72,73},{105,104},{16,17},{..., dimensions={0}, use_global_device_ids=true | all-gather | bytes 24576 | tf_op jit(solution)/shard_map/all_gather | solution.py:416
  21.5 10.6 %all-gather.1 = f32[8,4,128]{2,1,0:T(4,128)S(1)} all-gather(f32[4,4,128]{2,1,0:T(4,128)S(1)} %constant_dynamic-update-slice_fusion), channel_id=3, replica_groups={{1,33},{32,64},{65,97},{96,8},{9,41},{40,72},{73,105},{104,16},{17,49},..., dimensions={0}, use_global_device_ids=true | all-gather | bytes 24576 | tf_op jit(solution)/shard_map/all_gather | solution.py:416
  32.1 9.8 %shard_map.113 = (bf16[2,512,128]{2,1,0:T(8,128)(2,1)S(1)}, f32[2,128,128]{2,1,0:T(8,128)S(1)}, f32[2,3,128,128]{3,2,1,0:T(8,128)S(1)}, bf16[2,1152,4096]{2,1,0:...) custom-call(s32[1]{0:T(128)} %bitcast.flag, f32[2,4,4,128]{3,2,1,0:T(4,128)S(1)} %bitcast.23, ...), custom_call_target="tpu_custom_call" | custom-call | flops 2400000000 | bytes 1048576 | tf_op jit(solution)/shard_map/pallas_call | solution.py:523
  42.0 2.6 %collective-permute-start.3 = (bf16[1,512,128]{2,1,0:T(8,128)(2,1)S(1)}, bf16[1,512,128]{2,1,0:T(8,128)(2,1)S(1)}, u32[]{:S(2)}, u32[]{:S(2)}) collective-permute-start(bf16[1,512,128]{2,1,0:T(8,128)(2,1)S(1)} %get-tuple-element.28), channel_id=1, source_target_pairs={{0,2},{1,3},{33,35},{32,34},{64,66},{65,67},{97,99},{96,98},{8,10}... | collective-permute-start | bytes 393224 | tf_op jit(solution)/shard_map/ppermute | solution.py:408
  44.6 3.2 %collective-permute-start.4 = (bf16[1,512,128]{2,1,0:T(8,128)(2,1)S(1)}, bf16[1,512,128]{2,1,0:T(8,128)(2,1)S(1)}, u32[]{:S(2)}, u32[]{:S(2)}) collective-permute-start(bf16[1,512,128]{2,1,0:T(8,128)(2,1)S(1)} %get-tuple-element.29), channel_id=1, source_target_pairs={{0,128},{1,129},{33,161},{32,160},{64,192},{65,193},{97,225},{96,2... | collective-permute-start | bytes 393224 | tf_op jit(solution)/shard_map/ppermute | solution.py:408
  47.8 1.0 collective-permute-done.3
  48.9 2.6 %collective-permute-done.4 = bf16[1,512,128]{2,1,0:T(8,128)(2,1)S(1)} collective-permute-done((bf16[1,512,128]{2,1,0:T(8,128)(2,1)S(1)}, bf16[1,512,128]{2,1,0:T(8,128)(2,1)S(1)}, u32[]{:S(2)}, u32[]{:S(2)}) %collective-permute-start.4) | collective-permute-done | bytes 131104 | tf_op jit(solution)/shard_map/ppermute | solution.py:408
  51.6 1.9 %collective-permute-start.5 = (bf16[1,4,512,128]{3,2,1,0:T(8,128)(2,1)S(1)}, bf16[1,4,512,128]{3,2,1,0:T(8,128)(2,1)S(1)}, u32[]{:S(2)}, u32[]{:S(2)}) collective-permute-start(bf16[1,4,512,128]{3,2,1,0:T(8,128)(2,1)S(1)} %maximum_bitcast_fusion.feat_mine), channel_id=1, source_target_pairs={{0,1},{1,0},{33,32},{32,33},{64,65},{65,64},{97,96},{96,97},{8,9},... | collective-permute-start | bytes 1572872 | tf_op jit(solution)/shard_map/ppermute | solution.py:424
  53.5 5.2 %collective-permute-start.6 = (bf16[1,4,512,128]{3,2,1,0:T(8,128)(2,1)S(1)}, bf16[1,4,512,128]{3,2,1,0:T(8,128)(2,1)S(1)}, u32[]{:S(2)}, u32[]{:S(2)}) collective-permute-start(bf16[1,4,512,128]{3,2,1,0:T(8,128)(2,1)S(1)} %maximum_bitcast_fusion.feat_mine), channel_id=1, source_target_pairs={{1,33},{33,1},{32,64},{64,32},{65,97},{97,65},{96,8},{8,96},{9,41}... | collective-permute-start | bytes 1572872 | tf_op jit(solution)/shard_map/ppermute | solution.py:424
  58.7 7.1 %collective-permute-done.6.feat_odd = bf16[1,4,512,128]{3,2,1,0:T(8,128)(2,1)S(1)} collective-permute-done((bf16[1,4,512,128]{3,2,1,0:T(8,128)(2,1)S(1)}, bf16[1,4,512,128]{3,2,1,0:T(8,128)(2,1)S(1)}, u32[]{:S(2)}, u32[]{:S(2)}) %collective-permute-start.6) | collective-permute-done | bytes 524320 | tf_op jit(solution)/shard_map/ppermute | solution.py:424
  65.8 4.5 %shard_map.114 = (f32[2,1,128]{2,1,0:T(1,128)S(1)}, bf16[2,128,128]{2,1,0:T(8,128)(2,1)S(1)}) custom-call(s32[1]{0:T(128)} %bitcast.flag, f32[2,4,4,128]{3,2,1,0:T(4,128)S(1)} %bitcast.24, bf16[1,4,512,128]{3,2,1,0:T(8,128)(2,1)S(1)} %collective-permute-done.5.feat_even, bf16[1,4,512,128]{3,2,1,0:T(8,128)(2,1)S(1)} %maximum_bitcast_fusion.feat_mine, ...), custom_call_target="tpu_custom_call" | custom-call | flops 2400000000 | bytes 1048576 | tf_op jit(solution)/shard_map/pallas_call | solution.py:527
  71.6 3.0 %collective-permute-start.7 = (bf16[1,128,128]{2,1,0:T(8,128)(2,1)}, bf16[1,128,128]{2,1,0:T(8,128)(2,1)}, u32[]{:S(2)}, u32[]{:S(2)}) collective-permute-start(bf16[1,128,128]{2,1,0:T(8,128)(2,1)} %get-tuple-element.30), channel_id=1, source_target_pairs={{0,2},{1,3},{33,35},{32,34},{64,66},{65,67},{97,99},{96,98},{8,10}... | collective-permute-start | bytes 98312 | tf_op jit(solution)/shard_map/ppermute | solution.py:408
  74.5 2.9 %collective-permute-start.8 = (bf16[1,128,128]{2,1,0:T(8,128)(2,1)}, bf16[1,128,128]{2,1,0:T(8,128)(2,1)}, u32[]{:S(2)}, u32[]{:S(2)}) collective-permute-start(bf16[1,128,128]{2,1,0:T(8,128)(2,1)} %get-tuple-element.31), channel_id=1, source_target_pairs={{0,128},{1,129},{33,161},{32,160},{64,192},{65,193},{97,225},{96,2... | collective-permute-start | bytes 98312 | tf_op jit(solution)/shard_map/ppermute | solution.py:408
  77.7 3.0 %collective-permute-done.8 = bf16[1,128,128]{2,1,0:T(8,128)(2,1)} collective-permute-done((bf16[1,128,128]{2,1,0:T(8,128)(2,1)}, bf16[1,128,128]{2,1,0:T(8,128)(2,1)}, u32[]{:S(2)}, u32[]{:S(2)}) %collective-permute-start.8) | collective-permute-done | bytes 32800 | tf_op jit(solution)/shard_map/ppermute | solution.py:408
  81.5 5.3 %collective-permute-start.10 = (bf16[1,4,128,128]{3,2,1,0:T(8,128)(2,1)S(1)}, bf16[1,4,128,128]{3,2,1,0:T(8,128)(2,1)S(1)}, u32[]{:S(2)}, u32[]{:S(2)}) collective-permute-start(bf16[1,4,128,128]{3,2,1,0:T(8,128)(2,1)S(1)} %maximum_bitcast_fusion.1.pull_mine), channel_id=1, source_target_pairs={{1,33},{33,1},{32,64},{64,32},{65,97},{97,65},{96,8},{8,96},{9,41}... | collective-permute-start | bytes 393224 | tf_op jit(solution)/shard_map/ppermute | solution.py:424
  86.8 2.1 %collective-permute-start.9 = (bf16[1,4,128,128]{3,2,1,0:T(8,128)(2,1)S(1)}, bf16[1,4,128,128]{3,2,1,0:T(8,128)(2,1)S(1)}, u32[]{:S(2)}, u32[]{:S(2)}) collective-permute-start(bf16[1,4,128,128]{3,2,1,0:T(8,128)(2,1)S(1)} %maximum_bitcast_fusion.1.pull_mine), channel_id=1, source_target_pairs={{0,1},{1,0},{33,32},{32,33},{64,65},{65,64},{97,96},{96,97},{8,9},... | collective-permute-start | bytes 393224 | tf_op jit(solution)/shard_map/ppermute | solution.py:424
  88.9 1.7 %shard_map.116.kern_two = bf16[1152,4096]{1,0:T(8,128)(2,1)S(1)} custom-call(f32[12,3,128,128]{3,2,1,0:T(8,128)S(1)} %get-tuple-element.18.send_ref, f32[2,3,128]{2,1,0:T(4,128)S(1)} %get-tuple-element.19.recv_ref), custom_call_target="tpu_custom_call" | custom-call | flops 900000000 | bytes 1048576 | tf_op jit(solution)/shard_map/pallas_call | solution.py:532
  90.6 1.7 %shard_map.115.kern_one = bf16[1152,4096]{1,0:T(8,128)(2,1)S(1)} custom-call(f32[12,3,128,128]{3,2,1,0:T(8,128)S(1)} %get-tuple-element.18.send_ref, f32[2,3,128]{2,1,0:T(4,128)S(1)} %get-tuple-element.19.recv_ref), custom_call_target="tpu_custom_call" | custom-call | flops 900000000 | bytes 1048576 | tf_op jit(solution)/shard_map/pallas_call | solution.py:532
  92.5 19.4 %shard_map.117 = f32[3,4,4,128]{3,2,1,0:T(4,128)S(1)} custom-call(s32[1]{0:T(128)} %bitcast.flag, f32[2,4,4,128]{3,2,1,0:T(4,128)S(1)} %bitcast.25, f32[2,4,4,128]{3,2,1,0:T(4,128)S(1)} %bitcast.27, f32[12,3,128,128]{3,2,1,0:T(8,128)S(1)} %get-tuple-element.18.send_ref, f32[2,3,128]{2,1,0:T(4,128)S(1)} %get-tuple-element.19.recv_ref, ...), custom_call_target="tpu_custom_call" | custom-call | flops 7200000000 | bytes 1048576 | tf_op jit(solution)/shard_map/pallas_call | solution.py:533
  111.9 2.0 %all_gather.19 = f32[2,4,4,128]{3,2,1,0:T(4,128)S(1)} all-gather(f32[1,4,4,128]{3,2,1,0:T(4,128)S(1)} %get-tuple-element.32), channel_id=1, replica_groups={{0,1},{33,32},{64,65},{97,96},{8,9},{41,40},{72,73},{105,104},{16,17},{..., dimensions={0}, use_global_device_ids=true | all-gather | bytes 24576 | tf_op jit(solution)/shard_map/all_gather | solution.py:416
  113.9 5.6 %all_gather.20 = f32[2,4,4,128]{3,2,1,0:T(4,128)S(1)} all-gather(f32[1,4,4,128]{3,2,1,0:T(4,128)S(1)} %get-tuple-element.33), channel_id=1, replica_groups={{1,33},{32,64},{65,97},{96,8},{9,41},{40,72},{73,105},{104,16},{17,49},..., dimensions={0}, use_global_device_ids=true | all-gather | bytes 24576 | tf_op jit(solution)/shard_map/all_gather | solution.py:416
  119.4 3.4 %collective-permute-start.11 = (f32[1,4,128]{2,1,0:T(4,128)S(1)}, f32[1,4,128]{2,1,0:T(4,128)S(1)}, u32[]{:S(2)}, u32[]{:S(2)}) collective-permute-start(f32[1,4,128]{2,1,0:T(4,128)S(1)} %get-tuple-element.34), channel_id=1, source_target_pairs={{0,2},{1,3},{33,35},{32,34},{64,66},{65,67},{97,99},{96,98},{8,10}... | collective-permute-start | bytes 6152 | tf_op jit(solution)/shard_map/ppermute | solution.py:408
  122.8 2.4 %collective-permute-start.12 = (f32[1,4,128]{2,1,0:T(4,128)S(1)}, f32[1,4,128]{2,1,0:T(4,128)S(1)}, u32[]{:S(2)}, u32[]{:S(2)}) collective-permute-start(f32[1,4,128]{2,1,0:T(4,128)S(1)} %get-tuple-element.35), channel_id=1, source_target_pairs={{0,128},{1,129},{33,161},{32,160},{64,192},{65,193},{97,225},{96,2... | collective-permute-start | bytes 6152 | tf_op jit(solution)/shard_map/ppermute | solution.py:408
  125.3 3.0 %collective-permute-done.12 = f32[1,4,128]{2,1,0:T(4,128)S(1)} collective-permute-done((f32[1,4,128]{2,1,0:T(4,128)S(1)}, f32[1,4,128]{2,1,0:T(4,128)S(1)}, u32[]{:S(2)}, u32[]{:S(2)}) %collective-permute-start.12) | collective-permute-done | bytes 2080 | tf_op jit(solution)/shard_map/ppermute | solution.py:408
  128.3 2.1 %collective-permute-start.13 = (f32[2,4,128]{2,1,0:T(4,128)S(1)}, f32[2,4,128]{2,1,0:T(4,128)S(1)}, u32[]{:S(2)}, u32[]{:S(2)}) collective-permute-start(f32[2,4,128]{2,1,0:T(4,128)S(1)} %fusion.1), channel_id=1, source_target_pairs={{0,0},{1,1},{33,2},{32,3},{64,4},{65,5},{97,6},{96,7},{8,8},{9,9},... | collective-permute-start | bytes 12296 | tf_op jit(solution)/shard_map/ppermute | solution.py:404
  130.5 6.7 %collective-permute-done.13 = f32[2,4,128]{2,1,0:T(4,128)S(1)} collective-permute-done((f32[2,4,128]{2,1,0:T(4,128)S(1)}, f32[2,4,128]{2,1,0:T(4,128)S(1)}, u32[]{:S(2)}, u32[]{:S(2)}) %collective-permute-start.13) | collective-permute-done | bytes 4128 | tf_op jit(solution)/shard_map/ppermute | solution.py:404
  (62 shorter events, 5.8 us)
Async XLA Ops:
  0.6 58.1 %copy-start.16 = (f32[2,8,128]{2,1,0:T(8,128)S(1)}, f32[2,8,128]{2,1,0:T(8,128)}, u32[]{:S(2)}) copy-start(f32[2,8,128]{2,1,0:T(8,128)} %param.15) | copy-start | bytes 24580
  2.0 9.4 %collective-permute-start = (f32[2,4,128]{2,1,0:T(4,128)S(1)}, f32[2,4,128]{2,1,0:T(4,128)S(1)}, u32[]{:S(2)}, u32[]{:S(2)}) collective-permute-start(f32[2,4,128]{2,1,0:T(4,128)S(1)} %maximum_bitcast_fusion.2), channel_id=1, source_target_pairs={{0,0},{1,1},{2,33},{3,32},{4,64},{5,65},{6,97},{7,96},{8,8},{9,9},... | collective-permute-start | bytes 12296 | tf_op jit(solution)/shard_map/ppermute | solution.py:398
  11.4 6.7 %collective-permute-start.1 = (f32[1,4,128]{2,1,0:T(4,128)S(1)}, f32[1,4,128]{2,1,0:T(4,128)S(1)}, u32[]{:S(2)}, u32[]{:S(2)}) collective-permute-start(f32[1,4,128]{2,1,0:T(4,128)S(1)} %get-tuple-element.37), channel_id=1, source_target_pairs={{0,2},{1,3},{33,35},{32,34},{64,66},{65,67},{97,99},{96,98},{8,10}... | collective-permute-start | bytes 6152 | tf_op jit(solution)/shard_map/ppermute | solution.py:408
  14.1 39.4 %copy-start.7 = (f32[2,8,128]{2,1,0:T(8,128)}, f32[2,8,128]{2,1,0:T(8,128)S(1)}, u32[]{:S(2)}) copy-start(f32[2,8,128]{2,1,0:T(8,128)S(1)} %broadcast_multiply_fusion.1.weights.weights_one) | copy-start | bytes 24580
  14.1 51.8 %copy-start.4 = (bf16[128,128]{1,0:T(8,128)(2,1)S(1)}, bf16[128,128]{1,0:T(8,128)(2,1)}, u32[]{:S(2)}) copy-start(bf16[128,128]{1,0:T(8,128)(2,1)} %out_weight.1) | copy-start | bytes 98308
  14.1 51.8 %copy-start.9 = (f32[128]{0:T(128)S(1)}, f32[128]{0:T(128)}, u32[]{:S(2)}) copy-start(f32[128]{0:T(128)} %param.19) | copy-start | bytes 1540
  14.1 5.6 %collective-permute-start.2 = (f32[1,4,128]{2,1,0:T(4,128)S(1)}, f32[1,4,128]{2,1,0:T(4,128)S(1)}, u32[]{:S(2)}, u32[]{:S(2)}) collective-permute-start(f32[1,4,128]{2,1,0:T(4,128)S(1)} %get-tuple-element.36), channel_id=1, source_target_pairs={{0,128},{1,129},{33,161},{32,160},{64,192},{65,193},{97,225},{96,2... | collective-permute-start | bytes 6152 | tf_op jit(solution)/shard_map/ppermute | solution.py:408
  21.5 48.9 %copy-start.2 = (f32[8,4,128]{2,1,0:T(4,128)}, f32[8,4,128]{2,1,0:T(4,128)S(1)}, u32[]{:S(2)}) copy-start(f32[8,4,128]{2,1,0:T(4,128)S(1)} %all-gather) | copy-start | bytes 49156
  32.1 38.3 %copy-start.5 = (f32[8,4,128]{2,1,0:T(4,128)}, f32[8,4,128]{2,1,0:T(4,128)S(1)}, u32[]{:S(2)}) copy-start(f32[8,4,128]{2,1,0:T(4,128)S(1)} %all-gather.1) | copy-start | bytes 49156
  41.9 6.9 %copy-start.12 = (f32[2,3,128,128]{3,2,1,0:T(8,128)}, f32[2,3,128,128]{3,2,1,0:T(8,128)S(1)}, u32[]{:S(2)}) copy-start(f32[2,3,128,128]{3,2,1,0:T(8,128)S(1)} %get-tuple-element.22.vectors) | copy-start | bytes 1179652
  42.0 6.9 %copy-start.14 = (f32[2,128,128]{2,1,0:T(8,128)}, f32[2,128,128]{2,1,0:T(8,128)S(1)}, u32[]{:S(2)}) copy-start(f32[2,128,128]{2,1,0:T(8,128)S(1)} %get-tuple-element.21.hidden) | copy-start | bytes 393220
  42.0 6.9 %collective-permute-start.3 = (bf16[1,512,128]{2,1,0:T(8,128)(2,1)S(1)}, bf16[1,512,128]{2,1,0:T(8,128)(2,1)S(1)}, u32[]{:S(2)}, u32[]{:S(2)}) collective-permute-start(bf16[1,512,128]{2,1,0:T(8,128)(2,1)S(1)} %get-tuple-element.28), channel_id=1, source_target_pairs={{0,2},{1,3},{33,35},{32,34},{64,66},{65,67},{97,99},{96,98},{8,10}... | collective-permute-start | bytes 393224 | tf_op jit(solution)/shard_map/ppermute | solution.py:408
  44.6 6.9 %collective-permute-start.4 = (bf16[1,512,128]{2,1,0:T(8,128)(2,1)S(1)}, bf16[1,512,128]{2,1,0:T(8,128)(2,1)S(1)}, u32[]{:S(2)}, u32[]{:S(2)}) collective-permute-start(bf16[1,512,128]{2,1,0:T(8,128)(2,1)S(1)} %get-tuple-element.29), channel_id=1, source_target_pairs={{0,128},{1,129},{33,161},{32,160},{64,192},{65,193},{97,225},{96,2... | collective-permute-start | bytes 393224 | tf_op jit(solution)/shard_map/ppermute | solution.py:408
  51.6 7.1 %collective-permute-start.5 = (bf16[1,4,512,128]{3,2,1,0:T(8,128)(2,1)S(1)}, bf16[1,4,512,128]{3,2,1,0:T(8,128)(2,1)S(1)}, u32[]{:S(2)}, u32[]{:S(2)}) collective-permute-start(bf16[1,4,512,128]{3,2,1,0:T(8,128)(2,1)S(1)} %maximum_bitcast_fusion.feat_mine), channel_id=1, source_target_pairs={{0,1},{1,0},{33,32},{32,33},{64,65},{65,64},{97,96},{96,97},{8,9},... | collective-permute-start | bytes 1572872 | tf_op jit(solution)/shard_map/ppermute | solution.py:424
  53.5 12.3 %collective-permute-start.6 = (bf16[1,4,512,128]{3,2,1,0:T(8,128)(2,1)S(1)}, bf16[1,4,512,128]{3,2,1,0:T(8,128)(2,1)S(1)}, u32[]{:S(2)}, u32[]{:S(2)}) collective-permute-start(bf16[1,4,512,128]{3,2,1,0:T(8,128)(2,1)S(1)} %maximum_bitcast_fusion.feat_mine), channel_id=1, source_target_pairs={{1,33},{33,1},{32,64},{64,32},{65,97},{97,65},{96,8},{8,96},{9,41}... | collective-permute-start | bytes 1572872 | tf_op jit(solution)/shard_map/ppermute | solution.py:424
  65.8 4.5 %copy-start = (bf16[1,4,512,128]{3,2,1,0:T(8,128)(2,1)}, bf16[1,4,512,128]{3,2,1,0:T(8,128)(2,1)S(1)}, u32[]{:S(2)}) copy-start(bf16[1,4,512,128]{3,2,1,0:T(8,128)(2,1)S(1)} %collective-permute-done.6.feat_odd) | copy-start | bytes 1572868
  70.4 0.6 copy-start.10
  71.6 6.1 %collective-permute-start.7 = (bf16[1,128,128]{2,1,0:T(8,128)(2,1)}, bf16[1,128,128]{2,1,0:T(8,128)(2,1)}, u32[]{:S(2)}, u32[]{:S(2)}) collective-permute-start(bf16[1,128,128]{2,1,0:T(8,128)(2,1)} %get-tuple-element.30), channel_id=1, source_target_pairs={{0,2},{1,3},{33,35},{32,34},{64,66},{65,67},{97,99},{96,98},{8,10}... | collective-permute-start | bytes 98312 | tf_op jit(solution)/shard_map/ppermute | solution.py:408
  74.5 6.1 %collective-permute-start.8 = (bf16[1,128,128]{2,1,0:T(8,128)(2,1)}, bf16[1,128,128]{2,1,0:T(8,128)(2,1)}, u32[]{:S(2)}, u32[]{:S(2)}) collective-permute-start(bf16[1,128,128]{2,1,0:T(8,128)(2,1)} %get-tuple-element.31), channel_id=1, source_target_pairs={{0,128},{1,129},{33,161},{32,160},{64,192},{65,193},{97,225},{96,2... | collective-permute-start | bytes 98312 | tf_op jit(solution)/shard_map/ppermute | solution.py:408
  81.4 11.0 %copy-start.1 = (bf16[1,4,512,128]{3,2,1,0:T(8,128)(2,1)S(1)}, bf16[1,4,512,128]{3,2,1,0:T(8,128)(2,1)}, u32[]{:S(2)}) copy-start(bf16[1,4,512,128]{3,2,1,0:T(8,128)(2,1)} %copy-done) | copy-start | bytes 1572868
  81.5 11.0 %copy-start.3 = (f32[8,4,128]{2,1,0:T(4,128)S(1)}, f32[8,4,128]{2,1,0:T(4,128)}, u32[]{:S(2)}) copy-start(f32[8,4,128]{2,1,0:T(4,128)} %copy-done.2) | copy-start | bytes 49156
  81.5 11.0 %copy-start.6 = (f32[8,4,128]{2,1,0:T(4,128)S(1)}, f32[8,4,128]{2,1,0:T(4,128)}, u32[]{:S(2)}) copy-start(f32[8,4,128]{2,1,0:T(4,128)} %copy-done.5) | copy-start | bytes 49156
  81.5 11.0 %copy-start.8 = (f32[2,8,128]{2,1,0:T(8,128)S(1)}, f32[2,8,128]{2,1,0:T(8,128)}, u32[]{:S(2)}) copy-start(f32[2,8,128]{2,1,0:T(8,128)} %copy-done.7) | copy-start | bytes 24580
  81.5 11.0 %copy-start.11 = (f32[2,1,128]{2,1,0:T(1,128)S(1)}, f32[2,1,128]{2,1,0:T(1,128)}, u32[]{:S(2)}) copy-start(f32[2,1,128]{2,1,0:T(1,128)} %copy-done.10) | copy-start | bytes 3076
  81.5 11.0 %copy-start.13 = (f32[2,3,128,128]{3,2,1,0:T(8,128)S(1)}, f32[2,3,128,128]{3,2,1,0:T(8,128)}, u32[]{:S(2)}) copy-start(f32[2,3,128,128]{3,2,1,0:T(8,128)} %copy-done.12) | copy-start | bytes 1179652
  81.5 11.0 %copy-start.15 = (f32[2,128,128]{2,1,0:T(8,128)S(1)}, f32[2,128,128]{2,1,0:T(8,128)}, u32[]{:S(2)}) copy-start(f32[2,128,128]{2,1,0:T(8,128)} %copy-done.14) | copy-start | bytes 393220
  81.5 10.9 %collective-permute-start.10 = (bf16[1,4,128,128]{3,2,1,0:T(8,128)(2,1)S(1)}, bf16[1,4,128,128]{3,2,1,0:T(8,128)(2,1)S(1)}, u32[]{:S(2)}, u32[]{:S(2)}) collective-permute-start(bf16[1,4,128,128]{3,2,1,0:T(8,128)(2,1)S(1)} %maximum_bitcast_fusion.1.pull_mine), channel_id=1, source_target_pairs={{1,33},{33,1},{32,64},{64,32},{65,97},{97,65},{96,8},{8,96},{9,41}... | collective-permute-start | bytes 393224 | tf_op jit(solution)/shard_map/ppermute | solution.py:424
  86.8 5.6 %collective-permute-start.9 = (bf16[1,4,128,128]{3,2,1,0:T(8,128)(2,1)S(1)}, bf16[1,4,128,128]{3,2,1,0:T(8,128)(2,1)S(1)}, u32[]{:S(2)}, u32[]{:S(2)}) collective-permute-start(bf16[1,4,128,128]{3,2,1,0:T(8,128)(2,1)S(1)} %maximum_bitcast_fusion.1.pull_mine), channel_id=1, source_target_pairs={{0,1},{1,0},{33,32},{32,33},{64,65},{65,64},{97,96},{96,97},{8,9},... | collective-permute-start | bytes 393224 | tf_op jit(solution)/shard_map/ppermute | solution.py:424
  119.4 5.9 %collective-permute-start.11 = (f32[1,4,128]{2,1,0:T(4,128)S(1)}, f32[1,4,128]{2,1,0:T(4,128)S(1)}, u32[]{:S(2)}, u32[]{:S(2)}) collective-permute-start(f32[1,4,128]{2,1,0:T(4,128)S(1)} %get-tuple-element.34), channel_id=1, source_target_pairs={{0,2},{1,3},{33,35},{32,34},{64,66},{65,67},{97,99},{96,98},{8,10}... | collective-permute-start | bytes 6152 | tf_op jit(solution)/shard_map/ppermute | solution.py:408
  122.8 5.5 %collective-permute-start.12 = (f32[1,4,128]{2,1,0:T(4,128)S(1)}, f32[1,4,128]{2,1,0:T(4,128)S(1)}, u32[]{:S(2)}, u32[]{:S(2)}) collective-permute-start(f32[1,4,128]{2,1,0:T(4,128)S(1)} %get-tuple-element.35), channel_id=1, source_target_pairs={{0,128},{1,129},{33,161},{32,160},{64,192},{65,193},{97,225},{96,2... | collective-permute-start | bytes 6152 | tf_op jit(solution)/shard_map/ppermute | solution.py:408
  128.3 8.8 %collective-permute-start.13 = (f32[2,4,128]{2,1,0:T(4,128)S(1)}, f32[2,4,128]{2,1,0:T(4,128)S(1)}, u32[]{:S(2)}, u32[]{:S(2)}) collective-permute-start(f32[2,4,128]{2,1,0:T(4,128)S(1)} %fusion.1), channel_id=1, source_target_pairs={{0,0},{1,1},{33,2},{32,3},{64,4},{65,5},{97,6},{96,7},{8,8},{9,9},... | collective-permute-start | bytes 12296 | tf_op jit(solution)/shard_map/ppermute | solution.py:404

commit v5 on v4

--- a/solution.py
+++ b/solution.py
@@ -245,7 +245,8 @@
     spreads = []
     for which in range(2):
         scale = folded(weights_one, which)
-        spreads.append(stacked([table * scale[b : b + 1, :] for b in range(BASIS)]))
+        spread = jnp.concatenate([table * scale[b : b + 1, :] for b in range(BASIS)], axis=0)
+        spreads.append(spread.astype(BF16))
 
     def pull_back(block, kern_ref):
         lhs = nearby(pulls, OWN_SLOTS, block, 0)
@@ -261,15 +262,17 @@
             passed = plain_dot(mixv[...], vector_grad.astype(BF16))
             passed = passed.astype(BF16).astype(F32)
             grads.append(passed + 2.0 * vectors[block, d] * inv_grad)
-        basis = lax.broadcasted_iota(jnp.int32, (LENGTH, LENGTH), 0) >> 3
+        used = 8 * BASIS
+        basis = lax.broadcasted_iota(jnp.int32, (used, LENGTH), 0) >> 3
+        seed_ref[block, LENGTH + used :, :] = jnp.zeros((LENGTH - used, 4 * depth), BF16)
         for r in range(4):
             which = min(r, 1)
-            table_grad = plain_dot(spreads[which], grads[r], precision=lax.Precision.HIGHEST)
+            table_grad = plain_dot(spreads[which], grads[r].astype(BF16))
             for b in range(BASIS):
                 at = r * depth + b * LENGTH
                 scaled = pull * column_ref[which * BASIS + b]
                 seed_ref[block, :LENGTH, at : at + LENGTH] = scaled.astype(BF16)
-                seed_ref[block, LENGTH:, at : at + LENGTH] = jnp.where(
+                seed_ref[block, LENGTH : LENGTH + used, at : at + LENGTH] = jnp.where(
                     basis == b, table_grad, 0.0
                 ).astype(BF16)
 

time: 139 us -> 139 us (level)
  no operation moved by 1% of the time
where the time goes in v5:
time: 139 us; the launch traced here: 138 us
  starting transfers between devices  45.7 us (33%)
  Pallas kernels  36.8 us (26%)
  waiting for transfers between devices  28 us (20%)
  blocking collectives  20 us (14%)
  local copies, waits for them, and re-layouts  3.22 us (2%)
  other arithmetic  3.17 us (2%)
    ppermute x8, starting transfers between devices, along_slab(): return lax.ppermute(block, AXES, route)  23.5 us
    all_gather x4, blocking collectives, with_partner(): return lax.all_gather(block, AXES, axis_index_groups=groups)  20 us
    pallas_call x1, Pallas kernels, on_device(): third_call()  19 us
    ppermute x4, starting transfers between devices, swap(): return lax.ppermute(block, AXES, route)  14.5 us
    ppermute x8, waiting for transfers between devices, along_slab(): return lax.ppermute(block, AXES, route)  11.4 us
    pallas_call x1, Pallas kernels, on_device(): first_call()(*places, bank, weights_one)  9.83 us
    ppermute x4, waiting for transfers between devices, swap(): return lax.ppermute(block, AXES, route)  7.12 us
    ppermute x1, waiting for transfers between devices, to_owner(): return lax.ppermute(block, AXES, route)  6.66 us
  transfers between devices with their start and end apart: 14, of which 9 were waited for; matrix products, arithmetic and copies ran while one was open for 1% of the time, Pallas kernels for 3%

profile of v5, /device:TPU:24, one launch (start us, length us, event | category | flops | bytes accessed | tf_op | source)
XLA Modules:
  0.0 137.9 jit_solution(11385397791436629648)
XLA Ops:
  2.0 5.6 %collective-permute-start = (f32[2,4,128]{2,1,0:T(4,128)S(1)}, f32[2,4,128]{2,1,0:T(4,128)S(1)}, u32[]{:S(2)}, u32[]{:S(2)}) collective-permute-start(f32[2,4,128]{2,1,0:T(4,128)S(1)} %maximum_bitcast_fusion.2), channel_id=1, source_target_pairs={{0,0},{1,1},{2,33},{3,32},{4,64},{5,65},{6,97},{7,96},{8,8},{9,9},... | collective-permute-start | bytes 12296 | tf_op jit(solution)/shard_map/ppermute | solution.py:401
  7.8 0.9 maximum_maximum_fusion.bank
  8.7 2.8 %collective-permute-done = f32[2,4,128]{2,1,0:T(4,128)S(1)} collective-permute-done((f32[2,4,128]{2,1,0:T(4,128)S(1)}, f32[2,4,128]{2,1,0:T(4,128)S(1)}, u32[]{:S(2)}, u32[]{:S(2)}) %collective-permute-start) | collective-permute-done | bytes 4128 | tf_op jit(solution)/shard_map/ppermute | solution.py:401
  11.4 1.9 %collective-permute-start.1 = (f32[1,4,128]{2,1,0:T(4,128)S(1)}, f32[1,4,128]{2,1,0:T(4,128)S(1)}, u32[]{:S(2)}, u32[]{:S(2)}) collective-permute-start(f32[1,4,128]{2,1,0:T(4,128)S(1)} %get-tuple-element.37), channel_id=1, source_target_pairs={{0,2},{1,3},{33,35},{32,34},{64,66},{65,67},{97,99},{96,98},{8,10}... | collective-permute-start | bytes 6152 | tf_op jit(solution)/shard_map/ppermute | solution.py:411
  14.1 4.0 %collective-permute-start.2 = (f32[1,4,128]{2,1,0:T(4,128)S(1)}, f32[1,4,128]{2,1,0:T(4,128)S(1)}, u32[]{:S(2)}, u32[]{:S(2)}) collective-permute-start(f32[1,4,128]{2,1,0:T(4,128)S(1)} %get-tuple-element.36), channel_id=1, source_target_pairs={{0,128},{1,129},{33,161},{32,160},{64,192},{65,193},{97,225},{96,2... | collective-permute-start | bytes 6152 | tf_op jit(solution)/shard_map/ppermute | solution.py:411
  18.2 1.5 %collective-permute-done.2 = f32[1,4,128]{2,1,0:T(4,128)S(1)} collective-permute-done((f32[1,4,128]{2,1,0:T(4,128)S(1)}, f32[1,4,128]{2,1,0:T(4,128)S(1)}, u32[]{:S(2)}, u32[]{:S(2)}) %collective-permute-start.2) | collective-permute-done | bytes 2080 | tf_op jit(solution)/shard_map/ppermute | solution.py:411
  19.7 1.8 %all-gather = f32[8,4,128]{2,1,0:T(4,128)S(1)} all-gather(f32[4,4,128]{2,1,0:T(4,128)S(1)} %constant_dynamic-update-slice_fusion), channel_id=2, replica_groups={{0,1},{33,32},{64,65},{97,96},{8,9},{41,40},{72,73},{105,104},{16,17},{..., dimensions={0}, use_global_device_ids=true | all-gather | bytes 24576 | tf_op jit(solution)/shard_map/all_gather | solution.py:419
  21.5 10.6 %all-gather.1 = f32[8,4,128]{2,1,0:T(4,128)S(1)} all-gather(f32[4,4,128]{2,1,0:T(4,128)S(1)} %constant_dynamic-update-slice_fusion), channel_id=3, replica_groups={{1,33},{32,64},{65,97},{96,8},{9,41},{40,72},{73,105},{104,16},{17,49},..., dimensions={0}, use_global_device_ids=true | all-gather | bytes 24576 | tf_op jit(solution)/shard_map/all_gather | solution.py:419
  32.1 9.8 %shard_map.113 = (bf16[2,512,128]{2,1,0:T(8,128)(2,1)S(1)}, f32[2,128,128]{2,1,0:T(8,128)S(1)}, f32[2,3,128,128]{3,2,1,0:T(8,128)S(1)}, bf16[2,1152,4096]{2,1,0:...) custom-call(s32[1]{0:T(128)} %bitcast.flag, f32[2,4,4,128]{3,2,1,0:T(4,128)S(1)} %bitcast.23, ...), custom_call_target="tpu_custom_call" | custom-call | flops 2400000000 | bytes 1048576 | tf_op jit(solution)/shard_map/pallas_call | solution.py:526
  42.0 2.6 %collective-permute-start.3 = (bf16[1,512,128]{2,1,0:T(8,128)(2,1)S(1)}, bf16[1,512,128]{2,1,0:T(8,128)(2,1)S(1)}, u32[]{:S(2)}, u32[]{:S(2)}) collective-permute-start(bf16[1,512,128]{2,1,0:T(8,128)(2,1)S(1)} %get-tuple-element.28), channel_id=1, source_target_pairs={{0,2},{1,3},{33,35},{32,34},{64,66},{65,67},{97,99},{96,98},{8,10}... | collective-permute-start | bytes 393224 | tf_op jit(solution)/shard_map/ppermute | solution.py:411
  44.6 3.2 %collective-permute-start.4 = (bf16[1,512,128]{2,1,0:T(8,128)(2,1)S(1)}, bf16[1,512,128]{2,1,0:T(8,128)(2,1)S(1)}, u32[]{:S(2)}, u32[]{:S(2)}) collective-permute-start(bf16[1,512,128]{2,1,0:T(8,128)(2,1)S(1)} %get-tuple-element.29), channel_id=1, source_target_pairs={{0,128},{1,129},{33,161},{32,160},{64,192},{65,193},{97,225},{96,2... | collective-permute-start | bytes 393224 | tf_op jit(solution)/shard_map/ppermute | solution.py:411
  47.8 1.0 collective-permute-done.3
  48.9 2.6 %collective-permute-done.4 = bf16[1,512,128]{2,1,0:T(8,128)(2,1)S(1)} collective-permute-done((bf16[1,512,128]{2,1,0:T(8,128)(2,1)S(1)}, bf16[1,512,128]{2,1,0:T(8,128)(2,1)S(1)}, u32[]{:S(2)}, u32[]{:S(2)}) %collective-permute-start.4) | collective-permute-done | bytes 131104 | tf_op jit(solution)/shard_map/ppermute | solution.py:411
  51.6 1.9 %collective-permute-start.5 = (bf16[1,4,512,128]{3,2,1,0:T(8,128)(2,1)S(1)}, bf16[1,4,512,128]{3,2,1,0:T(8,128)(2,1)S(1)}, u32[]{:S(2)}, u32[]{:S(2)}) collective-permute-start(bf16[1,4,512,128]{3,2,1,0:T(8,128)(2,1)S(1)} %maximum_bitcast_fusion.feat_mine), channel_id=1, source_target_pairs={{0,1},{1,0},{33,32},{32,33},{64,65},{65,64},{97,96},{96,97},{8,9},... | collective-permute-start | bytes 1572872 | tf_op jit(solution)/shard_map/ppermute | solution.py:427
  53.5 5.2 %collective-permute-start.6 = (bf16[1,4,512,128]{3,2,1,0:T(8,128)(2,1)S(1)}, bf16[1,4,512,128]{3,2,1,0:T(8,128)(2,1)S(1)}, u32[]{:S(2)}, u32[]{:S(2)}) collective-permute-start(bf16[1,4,512,128]{3,2,1,0:T(8,128)(2,1)S(1)} %maximum_bitcast_fusion.feat_mine), channel_id=1, source_target_pairs={{1,33},{33,1},{32,64},{64,32},{65,97},{97,65},{96,8},{8,96},{9,41}... | collective-permute-start | bytes 1572872 | tf_op jit(solution)/shard_map/ppermute | solution.py:427
  58.7 7.1 %collective-permute-done.6.feat_odd = bf16[1,4,512,128]{3,2,1,0:T(8,128)(2,1)S(1)} collective-permute-done((bf16[1,4,512,128]{3,2,1,0:T(8,128)(2,1)S(1)}, bf16[1,4,512,128]{3,2,1,0:T(8,128)(2,1)S(1)}, u32[]{:S(2)}, u32[]{:S(2)}) %collective-permute-start.6) | collective-permute-done | bytes 524320 | tf_op jit(solution)/shard_map/ppermute | solution.py:427
  65.8 4.5 %shard_map.114 = (f32[2,1,128]{2,1,0:T(1,128)S(1)}, bf16[2,128,128]{2,1,0:T(8,128)(2,1)S(1)}) custom-call(s32[1]{0:T(128)} %bitcast.flag, f32[2,4,4,128]{3,2,1,0:T(4,128)S(1)} %bitcast.24, bf16[1,4,512,128]{3,2,1,0:T(8,128)(2,1)S(1)} %collective-permute-done.5.feat_even, bf16[1,4,512,128]{3,2,1,0:T(8,128)(2,1)S(1)} %maximum_bitcast_fusion.feat_mine, ...), custom_call_target="tpu_custom_call" | custom-call | flops 2400000000 | bytes 1048576 | tf_op jit(solution)/shard_map/pallas_call | solution.py:530
  71.6 3.0 %collective-permute-start.7 = (bf16[1,128,128]{2,1,0:T(8,128)(2,1)}, bf16[1,128,128]{2,1,0:T(8,128)(2,1)}, u32[]{:S(2)}, u32[]{:S(2)}) collective-permute-start(bf16[1,128,128]{2,1,0:T(8,128)(2,1)} %get-tuple-element.30), channel_id=1, source_target_pairs={{0,2},{1,3},{33,35},{32,34},{64,66},{65,67},{97,99},{96,98},{8,10}... | collective-permute-start | bytes 98312 | tf_op jit(solution)/shard_map/ppermute | solution.py:411
  74.5 2.9 %collective-permute-start.8 = (bf16[1,128,128]{2,1,0:T(8,128)(2,1)}, bf16[1,128,128]{2,1,0:T(8,128)(2,1)}, u32[]{:S(2)}, u32[]{:S(2)}) collective-permute-start(bf16[1,128,128]{2,1,0:T(8,128)(2,1)} %get-tuple-element.31), channel_id=1, source_target_pairs={{0,128},{1,129},{33,161},{32,160},{64,192},{65,193},{97,225},{96,2... | collective-permute-start | bytes 98312 | tf_op jit(solution)/shard_map/ppermute | solution.py:411
  77.7 3.0 %collective-permute-done.8 = bf16[1,128,128]{2,1,0:T(8,128)(2,1)} collective-permute-done((bf16[1,128,128]{2,1,0:T(8,128)(2,1)}, bf16[1,128,128]{2,1,0:T(8,128)(2,1)}, u32[]{:S(2)}, u32[]{:S(2)}) %collective-permute-start.8) | collective-permute-done | bytes 32800 | tf_op jit(solution)/shard_map/ppermute | solution.py:411
  81.5 5.3 %collective-permute-start.10 = (bf16[1,4,128,128]{3,2,1,0:T(8,128)(2,1)S(1)}, bf16[1,4,128,128]{3,2,1,0:T(8,128)(2,1)S(1)}, u32[]{:S(2)}, u32[]{:S(2)}) collective-permute-start(bf16[1,4,128,128]{3,2,1,0:T(8,128)(2,1)S(1)} %maximum_bitcast_fusion.1.pull_mine), channel_id=1, source_target_pairs={{1,33},{33,1},{32,64},{64,32},{65,97},{97,65},{96,8},{8,96},{9,41}... | collective-permute-start | bytes 393224 | tf_op jit(solution)/shard_map/ppermute | solution.py:427
  86.8 2.1 %collective-permute-start.9 = (bf16[1,4,128,128]{3,2,1,0:T(8,128)(2,1)S(1)}, bf16[1,4,128,128]{3,2,1,0:T(8,128)(2,1)S(1)}, u32[]{:S(2)}, u32[]{:S(2)}) collective-permute-start(bf16[1,4,128,128]{3,2,1,0:T(8,128)(2,1)S(1)} %maximum_bitcast_fusion.1.pull_mine), channel_id=1, source_target_pairs={{0,1},{1,0},{33,32},{32,33},{64,65},{65,64},{97,96},{96,97},{8,9},... | collective-permute-start | bytes 393224 | tf_op jit(solution)/shard_map/ppermute | solution.py:427
  88.9 1.7 %shard_map.116.kern_two = bf16[1152,4096]{1,0:T(8,128)(2,1)S(1)} custom-call(f32[12,3,128,128]{3,2,1,0:T(8,128)S(1)} %get-tuple-element.18.send_ref, f32[2,3,128]{2,1,0:T(4,128)S(1)} %get-tuple-element.19.recv_ref), custom_call_target="tpu_custom_call" | custom-call | flops 900000000 | bytes 1048576 | tf_op jit(solution)/shard_map/pallas_call | solution.py:535
  90.6 1.7 %shard_map.115.kern_one = bf16[1152,4096]{1,0:T(8,128)(2,1)S(1)} custom-call(f32[12,3,128,128]{3,2,1,0:T(8,128)S(1)} %get-tuple-element.18.send_ref, f32[2,3,128]{2,1,0:T(4,128)S(1)} %get-tuple-element.19.recv_ref), custom_call_target="tpu_custom_call" | custom-call | flops 900000000 | bytes 1048576 | tf_op jit(solution)/shard_map/pallas_call | solution.py:535
  92.5 19.0 %shard_map.117 = f32[3,4,4,128]{3,2,1,0:T(4,128)S(1)} custom-call(s32[1]{0:T(128)} %bitcast.flag, f32[2,4,4,128]{3,2,1,0:T(4,128)S(1)} %bitcast.25, f32[2,4,4,128]{3,2,1,0:T(4,128)S(1)} %bitcast.27, f32[12,3,128,128]{3,2,1,0:T(8,128)S(1)} %get-tuple-element.18.send_ref, f32[2,3,128]{2,1,0:T(4,128)S(1)} %get-tuple-element.19.recv_ref, ...), custom_call_target="tpu_custom_call" | custom-call | flops 7200000000 | bytes 1048576 | tf_op jit(solution)/shard_map/pallas_call | solution.py:536
  111.5 2.0 %all_gather.19 = f32[2,4,4,128]{3,2,1,0:T(4,128)S(1)} all-gather(f32[1,4,4,128]{3,2,1,0:T(4,128)S(1)} %get-tuple-element.32), channel_id=1, replica_groups={{0,1},{33,32},{64,65},{97,96},{8,9},{41,40},{72,73},{105,104},{16,17},{..., dimensions={0}, use_global_device_ids=true | all-gather | bytes 24576 | tf_op jit(solution)/shard_map/all_gather | solution.py:419
  113.5 5.6 %all_gather.20 = f32[2,4,4,128]{3,2,1,0:T(4,128)S(1)} all-gather(f32[1,4,4,128]{3,2,1,0:T(4,128)S(1)} %get-tuple-element.33), channel_id=1, replica_groups={{1,33},{32,64},{65,97},{96,8},{9,41},{40,72},{73,105},{104,16},{17,49},..., dimensions={0}, use_global_device_ids=true | all-gather | bytes 24576 | tf_op jit(solution)/shard_map/all_gather | solution.py:419
  119.1 3.4 %collective-permute-start.11 = (f32[1,4,128]{2,1,0:T(4,128)S(1)}, f32[1,4,128]{2,1,0:T(4,128)S(1)}, u32[]{:S(2)}, u32[]{:S(2)}) collective-permute-start(f32[1,4,128]{2,1,0:T(4,128)S(1)} %get-tuple-element.34), channel_id=1, source_target_pairs={{0,2},{1,3},{33,35},{32,34},{64,66},{65,67},{97,99},{96,98},{8,10}... | collective-permute-start | bytes 6152 | tf_op jit(solution)/shard_map/ppermute | solution.py:411
  122.5 2.5 %collective-permute-start.12 = (f32[1,4,128]{2,1,0:T(4,128)S(1)}, f32[1,4,128]{2,1,0:T(4,128)S(1)}, u32[]{:S(2)}, u32[]{:S(2)}) collective-permute-start(f32[1,4,128]{2,1,0:T(4,128)S(1)} %get-tuple-element.35), channel_id=1, source_target_pairs={{0,128},{1,129},{33,161},{32,160},{64,192},{65,193},{97,225},{96,2... | collective-permute-start | bytes 6152 | tf_op jit(solution)/shard_map/ppermute | solution.py:411
  124.9 3.0 %collective-permute-done.12 = f32[1,4,128]{2,1,0:T(4,128)S(1)} collective-permute-done((f32[1,4,128]{2,1,0:T(4,128)S(1)}, f32[1,4,128]{2,1,0:T(4,128)S(1)}, u32[]{:S(2)}, u32[]{:S(2)}) %collective-permute-start.12) | collective-permute-done | bytes 2080 | tf_op jit(solution)/shard_map/ppermute | solution.py:411
  127.9 2.2 %collective-permute-start.13 = (f32[2,4,128]{2,1,0:T(4,128)S(1)}, f32[2,4,128]{2,1,0:T(4,128)S(1)}, u32[]{:S(2)}, u32[]{:S(2)}) collective-permute-start(f32[2,4,128]{2,1,0:T(4,128)S(1)} %fusion.1), channel_id=1, source_target_pairs={{0,0},{1,1},{33,2},{32,3},{64,4},{65,5},{97,6},{96,7},{8,8},{9,9},... | collective-permute-start | bytes 12296 | tf_op jit(solution)/shard_map/ppermute | solution.py:407
  130.1 6.7 %collective-permute-done.13 = f32[2,4,128]{2,1,0:T(4,128)S(1)} collective-permute-done((f32[2,4,128]{2,1,0:T(4,128)S(1)}, f32[2,4,128]{2,1,0:T(4,128)S(1)}, u32[]{:S(2)}, u32[]{:S(2)}) %collective-permute-start.13) | collective-permute-done | bytes 4128 | tf_op jit(solution)/shard_map/ppermute | solution.py:407
  (62 shorter events, 5.8 us)
Async XLA Ops:
  0.6 58.1 %copy-start.16 = (f32[2,8,128]{2,1,0:T(8,128)S(1)}, f32[2,8,128]{2,1,0:T(8,128)}, u32[]{:S(2)}) copy-start(f32[2,8,128]{2,1,0:T(8,128)} %param.15) | copy-start | bytes 24580
  2.0 9.4 %collective-permute-start = (f32[2,4,128]{2,1,0:T(4,128)S(1)}, f32[2,4,128]{2,1,0:T(4,128)S(1)}, u32[]{:S(2)}, u32[]{:S(2)}) collective-permute-start(f32[2,4,128]{2,1,0:T(4,128)S(1)} %maximum_bitcast_fusion.2), channel_id=1, source_target_pairs={{0,0},{1,1},{2,33},{3,32},{4,64},{5,65},{6,97},{7,96},{8,8},{9,9},... | collective-permute-start | bytes 12296 | tf_op jit(solution)/shard_map/ppermute | solution.py:401
  11.4 6.7 %collective-permute-start.1 = (f32[1,4,128]{2,1,0:T(4,128)S(1)}, f32[1,4,128]{2,1,0:T(4,128)S(1)}, u32[]{:S(2)}, u32[]{:S(2)}) collective-permute-start(f32[1,4,128]{2,1,0:T(4,128)S(1)} %get-tuple-element.37), channel_id=1, source_target_pairs={{0,2},{1,3},{33,35},{32,34},{64,66},{65,67},{97,99},{96,98},{8,10}... | collective-permute-start | bytes 6152 | tf_op jit(solution)/shard_map/ppermute | solution.py:411
  14.1 39.4 %copy-start.7 = (f32[2,8,128]{2,1,0:T(8,128)}, f32[2,8,128]{2,1,0:T(8,128)S(1)}, u32[]{:S(2)}) copy-start(f32[2,8,128]{2,1,0:T(8,128)S(1)} %broadcast_multiply_fusion.1.weights.weights_one) | copy-start | bytes 24580
  14.1 51.8 %copy-start.4 = (bf16[128,128]{1,0:T(8,128)(2,1)S(1)}, bf16[128,128]{1,0:T(8,128)(2,1)}, u32[]{:S(2)}) copy-start(bf16[128,128]{1,0:T(8,128)(2,1)} %out_weight.1) | copy-start | bytes 98308
  14.1 51.8 %copy-start.9 = (f32[128]{0:T(128)S(1)}, f32[128]{0:T(128)}, u32[]{:S(2)}) copy-start(f32[128]{0:T(128)} %param.19) | copy-start | bytes 1540
  14.1 5.6 %collective-permute-start.2 = (f32[1,4,128]{2,1,0:T(4,128)S(1)}, f32[1,4,128]{2,1,0:T(4,128)S(1)}, u32[]{:S(2)}, u32[]{:S(2)}) collective-permute-start(f32[1,4,128]{2,1,0:T(4,128)S(1)} %get-tuple-element.36), channel_id=1, source_target_pairs={{0,128},{1,129},{33,161},{32,160},{64,192},{65,193},{97,225},{96,2... | collective-permute-start | bytes 6152 | tf_op jit(solution)/shard_map/ppermute | solution.py:411
  21.5 48.9 %copy-start.2 = (f32[8,4,128]{2,1,0:T(4,128)}, f32[8,4,128]{2,1,0:T(4,128)S(1)}, u32[]{:S(2)}) copy-start(f32[8,4,128]{2,1,0:T(4,128)S(1)} %all-gather) | copy-start | bytes 49156
  32.1 38.3 %copy-start.5 = (f32[8,4,128]{2,1,0:T(4,128)}, f32[8,4,128]{2,1,0:T(4,128)S(1)}, u32[]{:S(2)}) copy-start(f32[8,4,128]{2,1,0:T(4,128)S(1)} %all-gather.1) | copy-start | bytes 49156
  41.9 6.9 %copy-start.12 = (f32[2,3,128,128]{3,2,1,0:T(8,128)}, f32[2,3,128,128]{3,2,1,0:T(8,128)S(1)}, u32[]{:S(2)}) copy-start(f32[2,3,128,128]{3,2,1,0:T(8,128)S(1)} %get-tuple-element.22.vectors) | copy-start | bytes 1179652
  42.0 6.9 %copy-start.14 = (f32[2,128,128]{2,1,0:T(8,128)}, f32[2,128,128]{2,1,0:T(8,128)S(1)}, u32[]{:S(2)}) copy-start(f32[2,128,128]{2,1,0:T(8,128)S(1)} %get-tuple-element.21.hidden) | copy-start | bytes 393220
  42.0 6.9 %collective-permute-start.3 = (bf16[1,512,128]{2,1,0:T(8,128)(2,1)S(1)}, bf16[1,512,128]{2,1,0:T(8,128)(2,1)S(1)}, u32[]{:S(2)}, u32[]{:S(2)}) collective-permute-start(bf16[1,512,128]{2,1,0:T(8,128)(2,1)S(1)} %get-tuple-element.28), channel_id=1, source_target_pairs={{0,2},{1,3},{33,35},{32,34},{64,66},{65,67},{97,99},{96,98},{8,10}... | collective-permute-start | bytes 393224 | tf_op jit(solution)/shard_map/ppermute | solution.py:411
  44.6 6.9 %collective-permute-start.4 = (bf16[1,512,128]{2,1,0:T(8,128)(2,1)S(1)}, bf16[1,512,128]{2,1,0:T(8,128)(2,1)S(1)}, u32[]{:S(2)}, u32[]{:S(2)}) collective-permute-start(bf16[1,512,128]{2,1,0:T(8,128)(2,1)S(1)} %get-tuple-element.29), channel_id=1, source_target_pairs={{0,128},{1,129},{33,161},{32,160},{64,192},{65,193},{97,225},{96,2... | collective-permute-start | bytes 393224 | tf_op jit(solution)/shard_map/ppermute | solution.py:411
  51.6 7.1 %collective-permute-start.5 = (bf16[1,4,512,128]{3,2,1,0:T(8,128)(2,1)S(1)}, bf16[1,4,512,128]{3,2,1,0:T(8,128)(2,1)S(1)}, u32[]{:S(2)}, u32[]{:S(2)}) collective-permute-start(bf16[1,4,512,128]{3,2,1,0:T(8,128)(2,1)S(1)} %maximum_bitcast_fusion.feat_mine), channel_id=1, source_target_pairs={{0,1},{1,0},{33,32},{32,33},{64,65},{65,64},{97,96},{96,97},{8,9},... | collective-permute-start | bytes 1572872 | tf_op jit(solution)/shard_map/ppermute | solution.py:427
  53.5 12.3 %collective-permute-start.6 = (bf16[1,4,512,128]{3,2,1,0:T(8,128)(2,1)S(1)}, bf16[1,4,512,128]{3,2,1,0:T(8,128)(2,1)S(1)}, u32[]{:S(2)}, u32[]{:S(2)}) collective-permute-start(bf16[1,4,512,128]{3,2,1,0:T(8,128)(2,1)S(1)} %maximum_bitcast_fusion.feat_mine), channel_id=1, source_target_pairs={{1,33},{33,1},{32,64},{64,32},{65,97},{97,65},{96,8},{8,96},{9,41}... | collective-permute-start | bytes 1572872 | tf_op jit(solution)/shard_map/ppermute | solution.py:427
  65.8 4.5 %copy-start = (bf16[1,4,512,128]{3,2,1,0:T(8,128)(2,1)}, bf16[1,4,512,128]{3,2,1,0:T(8,128)(2,1)S(1)}, u32[]{:S(2)}) copy-start(bf16[1,4,512,128]{3,2,1,0:T(8,128)(2,1)S(1)} %collective-permute-done.6.feat_odd) | copy-start | bytes 1572868
  70.4 0.6 copy-start.10
  71.6 6.1 %collective-permute-start.7 = (bf16[1,128,128]{2,1,0:T(8,128)(2,1)}, bf16[1,128,128]{2,1,0:T(8,128)(2,1)}, u32[]{:S(2)}, u32[]{:S(2)}) collective-permute-start(bf16[1,128,128]{2,1,0:T(8,128)(2,1)} %get-tuple-element.30), channel_id=1, source_target_pairs={{0,2},{1,3},{33,35},{32,34},{64,66},{65,67},{97,99},{96,98},{8,10}... | collective-permute-start | bytes 98312 | tf_op jit(solution)/shard_map/ppermute | solution.py:411
  74.5 6.1 %collective-permute-start.8 = (bf16[1,128,128]{2,1,0:T(8,128)(2,1)}, bf16[1,128,128]{2,1,0:T(8,128)(2,1)}, u32[]{:S(2)}, u32[]{:S(2)}) collective-permute-start(bf16[1,128,128]{2,1,0:T(8,128)(2,1)} %get-tuple-element.31), channel_id=1, source_target_pairs={{0,128},{1,129},{33,161},{32,160},{64,192},{65,193},{97,225},{96,2... | collective-permute-start | bytes 98312 | tf_op jit(solution)/shard_map/ppermute | solution.py:411
  81.4 11.0 %copy-start.1 = (bf16[1,4,512,128]{3,2,1,0:T(8,128)(2,1)S(1)}, bf16[1,4,512,128]{3,2,1,0:T(8,128)(2,1)}, u32[]{:S(2)}) copy-start(bf16[1,4,512,128]{3,2,1,0:T(8,128)(2,1)} %copy-done) | copy-start | bytes 1572868
  81.5 11.0 %copy-start.3 = (f32[8,4,128]{2,1,0:T(4,128)S(1)}, f32[8,4,128]{2,1,0:T(4,128)}, u32[]{:S(2)}) copy-start(f32[8,4,128]{2,1,0:T(4,128)} %copy-done.2) | copy-start | bytes 49156
  81.5 11.0 %copy-start.6 = (f32[8,4,128]{2,1,0:T(4,128)S(1)}, f32[8,4,128]{2,1,0:T(4,128)}, u32[]{:S(2)}) copy-start(f32[8,4,128]{2,1,0:T(4,128)} %copy-done.5) | copy-start | bytes 49156
  81.5 11.0 %copy-start.8 = (f32[2,8,128]{2,1,0:T(8,128)S(1)}, f32[2,8,128]{2,1,0:T(8,128)}, u32[]{:S(2)}) copy-start(f32[2,8,128]{2,1,0:T(8,128)} %copy-done.7) | copy-start | bytes 24580
  81.5 11.0 %copy-start.11 = (f32[2,1,128]{2,1,0:T(1,128)S(1)}, f32[2,1,128]{2,1,0:T(1,128)}, u32[]{:S(2)}) copy-start(f32[2,1,128]{2,1,0:T(1,128)} %copy-done.10) | copy-start | bytes 3076
  81.5 11.0 %copy-start.13 = (f32[2,3,128,128]{3,2,1,0:T(8,128)S(1)}, f32[2,3,128,128]{3,2,1,0:T(8,128)}, u32[]{:S(2)}) copy-start(f32[2,3,128,128]{3,2,1,0:T(8,128)} %copy-done.12) | copy-start | bytes 1179652
  81.5 11.0 %copy-start.15 = (f32[2,128,128]{2,1,0:T(8,128)S(1)}, f32[2,128,128]{2,1,0:T(8,128)}, u32[]{:S(2)}) copy-start(f32[2,128,128]{2,1,0:T(8,128)} %copy-done.14) | copy-start | bytes 393220
  81.5 10.9 %collective-permute-start.10 = (bf16[1,4,128,128]{3,2,1,0:T(8,128)(2,1)S(1)}, bf16[1,4,128,128]{3,2,1,0:T(8,128)(2,1)S(1)}, u32[]{:S(2)}, u32[]{:S(2)}) collective-permute-start(bf16[1,4,128,128]{3,2,1,0:T(8,128)(2,1)S(1)} %maximum_bitcast_fusion.1.pull_mine), channel_id=1, source_target_pairs={{1,33},{33,1},{32,64},{64,32},{65,97},{97,65},{96,8},{8,96},{9,41}... | collective-permute-start | bytes 393224 | tf_op jit(solution)/shard_map/ppermute | solution.py:427
  86.8 5.6 %collective-permute-start.9 = (bf16[1,4,128,128]{3,2,1,0:T(8,128)(2,1)S(1)}, bf16[1,4,128,128]{3,2,1,0:T(8,128)(2,1)S(1)}, u32[]{:S(2)}, u32[]{:S(2)}) collective-permute-start(bf16[1,4,128,128]{3,2,1,0:T(8,128)(2,1)S(1)} %maximum_bitcast_fusion.1.pull_mine), channel_id=1, source_target_pairs={{0,1},{1,0},{33,32},{32,33},{64,65},{65,64},{97,96},{96,97},{8,9},... | collective-permute-start | bytes 393224 | tf_op jit(solution)/shard_map/ppermute | solution.py:427
  119.1 5.9 %collective-permute-start.11 = (f32[1,4,128]{2,1,0:T(4,128)S(1)}, f32[1,4,128]{2,1,0:T(4,128)S(1)}, u32[]{:S(2)}, u32[]{:S(2)}) collective-permute-start(f32[1,4,128]{2,1,0:T(4,128)S(1)} %get-tuple-element.34), channel_id=1, source_target_pairs={{0,2},{1,3},{33,35},{32,34},{64,66},{65,67},{97,99},{96,98},{8,10}... | collective-permute-start | bytes 6152 | tf_op jit(solution)/shard_map/ppermute | solution.py:411
  122.5 5.5 %collective-permute-start.12 = (f32[1,4,128]{2,1,0:T(4,128)S(1)}, f32[1,4,128]{2,1,0:T(4,128)S(1)}, u32[]{:S(2)}, u32[]{:S(2)}) collective-permute-start(f32[1,4,128]{2,1,0:T(4,128)S(1)} %get-tuple-element.35), channel_id=1, source_target_pairs={{0,128},{1,129},{33,161},{32,160},{64,192},{65,193},{97,225},{96,2... | collective-permute-start | bytes 6152 | tf_op jit(solution)/shard_map/ppermute | solution.py:411
  127.9 8.8 %collective-permute-start.13 = (f32[2,4,128]{2,1,0:T(4,128)S(1)}, f32[2,4,128]{2,1,0:T(4,128)S(1)}, u32[]{:S(2)}, u32[]{:S(2)}) collective-permute-start(f32[2,4,128]{2,1,0:T(4,128)S(1)} %fusion.1), channel_id=1, source_target_pairs={{0,0},{1,1},{33,2},{32,3},{64,4},{65,5},{97,6},{96,7},{8,8},{9,9},... | collective-permute-start | bytes 12296 | tf_op jit(solution)/shard_map/ppermute | solution.py:407
